TPU v7x, 128 devices: a whole 4x4x4 slice. The times are simulated.
128 devices in a mesh: dp: 16 (over x_lo, y, core), tensor: 8 (over x_hi, z).
Axes of the slice: x: 4 (x_hi: 2, x_lo: 2; x = x_hi * 2 + x_lo), y: 4, z: 4, core: 2. Of those that a mesh axis runs over, the one named last changes fastest.
Arguments:
- tokens: bfloat16 [16384, 1024], P(('dp', 'tensor')), may hold values from -6 to 6
- cotangent: bfloat16 [16384, 1024], P(('dp', 'tensor')), may hold values from -6 to 6
- w_qkv: bfloat16 [1, 1024, 3, 1024], P(None, None, None, 'tensor'), may hold values from -0.25 to 0.25
- qv_bias: float32 [1, 2, 1024], P(None, None, 'tensor'), may hold values from -1.8 to 1.8
- w_out: bfloat16 [1, 1024, 1024], P(None, 'tensor'), may hold values from -0.5 to 0.5
- w_fc1: bfloat16 [1, 1024, 4096], P(None, None, 'tensor'), may hold values from -0.1875 to 0.1875
- b_fc1: float32 [1, 4096], P(None, 'tensor'), may hold values from -1.8 to 1.8
- w_fc2: bfloat16 [1, 4096, 1024], P(None, 'tensor'), may hold values from -0.09375 to 0.09375
- norm_gain: float32 [1, 2, 1024], replicated, may hold values from 0.1 to 1.9
- norm_shift: float32 [1, 2, 1024], replicated, may hold values from -1.8 to 1.8
- out_bias: float32 [1, 2, 1024], replicated, may hold values from -1.8 to 1.8
- layer_scale: float32 [1, 2, 1024], replicated, may hold values from 0.3 to 1.5
Outputs:
- activations: float32 [16384, 1024], P(('dp', 'tensor'))
- input_grad: float32 [16384, 1024], P(('dp', 'tensor'))
- grad_w_qkv: float32 [1, 1024, 3, 1024], P(None, None, None, 'tensor')
- grad_qv_bias: float32 [1, 2, 1024], P(None, None, 'tensor')
- grad_w_out: float32 [1, 1024, 1024], P(None, 'tensor')
- grad_w_fc1: float32 [1, 1024, 4096], P(None, None, 'tensor')
- grad_b_fc1: float32 [1, 4096], P(None, 'tensor')
- grad_w_fc2: float32 [1, 4096, 1024], P(None, 'tensor')
- grad_norm_gain: float32 [1, 2, 1024], replicated
- grad_norm_shift: float32 [1, 2, 1024], replicated
- grad_out_bias: float32 [1, 2, 1024], replicated
- grad_layer_scale: float32 [1, 2, 1024], replicated
All inputs are finite; a program needn't handle non-finite values.
Results may differ from a plain program's by a relative error of at most 0.012.
The roundings to bfloat16 on the way count: a program that leaves them out, or rounds other values in their place, can miss the bound.
Values may be sent and summed in bfloat16 or wider, within the bound.
No kernel may reach another device: no remote copies, remote signals or barrier semaphores. Data moves between devices by JAX's collectives and lax.ppermute only.
A program may use at most 128 MiB of HBM per device.

v0:
```python
import jax
import jax.numpy as jnp
from jax import lax
from jax.experimental import pallas as pl
from jax.experimental.pallas import tpu as pltpu
from jax.sharding import PartitionSpec as P

HD = 64
BLOCK = 256
inv_root_two = 0.7071067811865476
inv_root_two_pi = 0.3989422804014327
f32 = jnp.float32
bf16 = jnp.bfloat16


def dot_nn(a, b):
    return lax.dot_general(a, b, (((1,), (0,)), ((), ())), preferred_element_type=f32)


def dot_nt(a, b):
    return lax.dot_general(a, b, (((1,), (1,)), ((), ())), preferred_element_type=f32)


def params():
    return pltpu.CompilerParams(vmem_limit_bytes=48 * 1024 * 1024)


def whole(shape):
    return pl.BlockSpec(shape, lambda i, *_: (0,) * len(shape))


def rows_of(width, block=BLOCK):
    return pl.BlockSpec((block, width), lambda i, *_: (i, 0))


def rows_in_order(width, blocks):
    return pl.BlockSpec((BLOCK, width), lambda i, core: ((i + core[0] * (blocks // 2)) % blocks, 0))


def norm_pieces(values):
    centred = values - jnp.mean(values, -1, keepdims=True)
    inv_dev = lax.rsqrt(jnp.mean(centred * centred, -1, keepdims=True) + 1e-06)
    return centred * inv_dev, inv_dev


def project_kernel(x_ref, gain_ref, shift_ref, w_ref, bias_ref, h_ref, q_ref, k_ref, v_ref):
    normed, _ = norm_pieces(x_ref[...].astype(f32))
    h = (normed * gain_ref[...] + shift_ref[...]).astype(bf16)
    h_ref[...] = h
    q_ref[...] = (dot_nn(h, w_ref[0]) + bias_ref[0:1, :]).astype(bf16)
    k_ref[...] = dot_nn(h, w_ref[1]).astype(bf16)
    v_ref[...] = (dot_nn(h, w_ref[2]) + bias_ref[1:2, :]).astype(bf16)


def project(x, gain, shift, w, bias):
    rows, model = x.shape
    width = w.shape[2]
    out = jax.ShapeDtypeStruct((rows, width), bf16)
    return pl.pallas_call(
        project_kernel,
        grid=(rows // BLOCK,),
        in_specs=[rows_of(model), whole((1, model)), whole((1, model)), whole(w.shape), whole(bias.shape)],
        out_specs=[rows_of(model)] + [rows_of(width)] * 3,
        out_shape=[jax.ShapeDtypeStruct((rows, model), bf16), out, out, out],
        compiler_params=params(),
        name="norm_project",
    )(x, gain, shift, w, bias)


def lane_mask(shape, head, dim):
    return (lax.broadcasted_iota(jnp.int32, shape, dim) // HD) == head


def only_head(values, head, dim=1):
    return jnp.where(lane_mask(values.shape, head, dim), values, jnp.zeros_like(values))


def attend_kernel(core_ref, q_ref, k_ref, v_ref, o_ref, lse_ref):
    q = q_ref[...] * jnp.asarray(HD**-0.5, bf16)
    v_t = v_ref[...].T
    total = None
    for head in range(q.shape[1] // HD):
        scores = dot_nt(k_ref[...], only_head(q, head))
        top = jnp.max(scores, 0, keepdims=True)
        shifted = jnp.exp(scores - top)
        row_sum = jnp.sum(shifted, 0, keepdims=True)
        prob = (shifted * (1.0 / row_sum)).astype(bf16)
        lse_ref[head : head + 1, :] = top + jnp.log(row_sum)
        piece = dot_nn(only_head(v_t, head, 0), prob)
        total = piece if total is None else total + piece
    o_ref[...] = total.astype(bf16).T


def attend(core, q, k, v):
    rows, width = q.shape
    heads = width // HD
    return pl.pallas_call(
        attend_kernel,
        grid_spec=pltpu.PrefetchScalarGridSpec(
            num_scalar_prefetch=1,
            grid=(rows // BLOCK,),
            in_specs=[rows_of(width), whole(k.shape), whole(v.shape)],
            out_specs=[
                rows_in_order(width, rows // BLOCK),
                pl.BlockSpec((heads, BLOCK), lambda i, *_: (0, i)),
            ],
        ),
        out_shape=[jax.ShapeDtypeStruct((rows, width), bf16), jax.ShapeDtypeStruct((heads, rows), f32)],
        compiler_params=params(),
        name="attend",
    )(core, q, k, v)


def attend_back_kernel(
    core_ref,
    q_ref,
    do_ref,
    lse_ref,
    k_ref,
    v_ref,
    dq_ref,
    dk_ref,
    dv_ref,
    sum_ref,
    dk_acc,
    dv_acc,
):
    step = pl.program_id(0)
    last = pl.num_programs(0) - 1
    scale = HD**-0.5

    @pl.when(step == 0)
    def _():
        dk_acc[...] = jnp.zeros_like(dk_acc)
        dv_acc[...] = jnp.zeros_like(dv_acc)
        sum_ref[...] = jnp.zeros_like(sum_ref)

    q = q_ref[...] * jnp.asarray(scale, bf16)
    do = do_ref[...]
    k_t = k_ref[...].T
    dq_t = None
    for head in range(q.shape[1] // HD):
        q_h = only_head(q, head)
        do_h = only_head(do, head)
        prob = jnp.exp(dot_nt(k_ref[...], q_h) - lse_ref[head : head + 1, :])
        d_prob = dot_nt(v_ref[...], do_h)
        row = jnp.sum(d_prob * prob, 0, keepdims=True)
        d_score = (prob * (d_prob - row)).astype(bf16)
        dv_acc[...] += dot_nn(prob.astype(bf16), do_h)
        dk_acc[...] += dot_nn(d_score, q_h)
        piece = dot_nn(only_head(k_t, head, 0), d_score)
        dq_t = piece if dq_t is None else dq_t + piece
    dq = (dq_t * scale).astype(bf16).T
    dq_ref[...] = dq
    sum_ref[0:1, :] += jnp.sum(dq.astype(f32), 0, keepdims=True)

    @pl.when(step == last)
    def _():
        dk_ref[...] = dk_acc[...].astype(bf16)
        dv = dv_acc[...].astype(bf16)
        dv_ref[...] = dv
        sum_ref[1:2, :] = jnp.sum(dv.astype(f32), 0, keepdims=True)


def attend_back(core, q, k, v, do, lse):
    rows, width = q.shape
    heads = width // HD
    out = jax.ShapeDtypeStruct((rows, width), bf16)
    return pl.pallas_call(
        attend_back_kernel,
        grid_spec=pltpu.PrefetchScalarGridSpec(
            num_scalar_prefetch=1,
            grid=(rows // BLOCK,),
            in_specs=[
                rows_of(width),
                rows_in_order(width, rows // BLOCK),
                pl.BlockSpec((heads, BLOCK), lambda i, *_: (0, i)),
                whole(k.shape),
                whole(v.shape),
            ],
            out_specs=[rows_of(width), whole(k.shape), whole(v.shape), whole((8, width))],
            scratch_shapes=[pltpu.VMEM((rows, width), f32), pltpu.VMEM((rows, width), f32)],
        ),
        out_shape=[out, out, out, jax.ShapeDtypeStruct((8, width), f32)],
        compiler_params=params(),
        name="attend_back",
    )(core, q, do, lse, k, v)


def hidden_kernel(core_ref, h_ref, g_ref, w1_ref, b1_ref, w2_ref, m_ref, du_ref, dh_ref, f_ref, sum_ref):
    step = pl.program_id(0)
    u = dot_nn(h_ref[...], w1_ref[...]) + b1_ref[...]
    phi = 0.5 * (1.0 + lax.erf(u * inv_root_two))
    m = (u * phi).astype(bf16)
    m_ref[...] = m
    dm = dot_nt(g_ref[...], w2_ref[...])
    du = (dm * (phi + u * jnp.exp(-0.5 * u * u) * inv_root_two_pi)).astype(bf16)
    du_ref[...] = du
    dh_ref[...] = dot_nt(du, w1_ref[...]).astype(bf16)
    f_ref[...] = dot_nn(m, w2_ref[...]).astype(bf16)

    @pl.when(step == 0)
    def _():
        sum_ref[...] = jnp.zeros_like(sum_ref)

    sum_ref[0:1, :] += jnp.sum(du.astype(f32), 0, keepdims=True)


def hidden_block(core, h, g, w1, b1, w2):
    rows, model = h.shape
    width = w1.shape[1]
    return pl.pallas_call(
        hidden_kernel,
        grid_spec=pltpu.PrefetchScalarGridSpec(
            num_scalar_prefetch=1,
            grid=(rows // BLOCK,),
            in_specs=[
                rows_of(model),
                rows_in_order(model, rows // BLOCK),
                whole(w1.shape),
                whole((1, width)),
                whole(w2.shape),
            ],
            out_specs=[
                rows_in_order(width, rows // BLOCK),
                rows_of(width),
                rows_of(model),
                rows_of(model),
                whole((8, width)),
            ],
        ),
        out_shape=[
            jax.ShapeDtypeStruct((rows, width), bf16),
            jax.ShapeDtypeStruct((rows, width), bf16),
            jax.ShapeDtypeStruct((rows, model), bf16),
            jax.ShapeDtypeStruct((rows, model), bf16),
            jax.ShapeDtypeStruct((8, width), f32),
        ],
        compiler_params=params(),
        name="hidden_block",
    )(core, h, g, w1, b1, w2)


def project_back_kernel(dq_ref, dk_ref, dv_ref, w_ref, x_ref, early_ref, lo_ref, hi_ref, sum_ref):
    step = pl.program_id(0)
    half = pl.num_programs(0) // 2
    dh = dot_nt(dq_ref[...], w_ref[0]) + dot_nt(dk_ref[...], w_ref[1]) + dot_nt(dv_ref[...], w_ref[2])
    normed, _ = norm_pieces(x_ref[...].astype(f32))

    @pl.when(step == 0)
    def _():
        sum_ref[...] = early_ref[...]

    @pl.when(step < half)
    def _():
        lo_ref[pl.ds(pl.multiple_of(step * BLOCK, BLOCK), BLOCK), :] = dh.astype(bf16)

    @pl.when(step >= half)
    def _():
        hi_ref[pl.ds(pl.multiple_of((step - half) * BLOCK, BLOCK), BLOCK), :] = dh.astype(bf16)

    sum_ref[0:1, :] += jnp.sum(dh * normed, 0, keepdims=True)
    sum_ref[1:2, :] += jnp.sum(dh, 0, keepdims=True)

    @pl.when(step == 2 * half - 1)
    def _():
        hi_ref[half * BLOCK :, :] = sum_ref[...].astype(bf16)


def project_back(dq, dk, dv, w, x, early):
    rows, model = x.shape
    width = dq.shape[1]
    lo = (rows // 2, model)
    hi = (rows // 2 + 16, model)
    return pl.pallas_call(
        project_back_kernel,
        grid=(rows // BLOCK,),
        in_specs=[rows_of(width)] * 3 + [whole(w.shape), rows_of(model), whole((16, model))],
        out_specs=[whole(lo), whole(hi)],
        out_shape=[jax.ShapeDtypeStruct(lo, bf16), jax.ShapeDtypeStruct(hi, bf16)],
        scratch_shapes=[pltpu.VMEM((16, model), f32)],
        compiler_params=params(),
        name="project_back",
    )(dq, dk, dv, w, x, early)


def norm_back(upstream, normed, inv_dev, gain):
    scaled = upstream * gain
    return inv_dev * (
        scaled
        - jnp.mean(scaled, -1, keepdims=True)
        - normed * jnp.mean(scaled * normed, -1, keepdims=True)
    )


AXES = ("dp", "tensor")


def members(key):
    found = {}
    for core in range(2):
        for z in range(4):
            for y in range(4):
                for xh in range(2):
                    for xl in range(2):
                        found.setdefault(key(xh, xl, y, z, core), []).append(
                            ((xl * 4 + y) * 2 + core) * 8 + xh * 4 + z
                        )
    return list(found.values())


def links(move):
    pairs = []
    for xh in range(2):
        for xl in range(2):
            for y in range(4):
                for z in range(4):
                    for core in range(2):
                        there = move(xh, xl, y, z, core)
                        if there is None:
                            continue
                        ph, pl_, py, pz, pc = there
                        pairs.append(
                            (
                                ((xl * 4 + y) * 2 + core) * 8 + xh * 4 + z,
                                ((pl_ * 4 + py % 4) * 2 + pc) * 8 + ph * 4 + pz % 4,
                            )
                        )
    return pairs


z_up = links(lambda xh, xl, y, z, c: (xh, xl, y, z + 1, c))
z_down = links(lambda xh, xl, y, z, c: (xh, xl, y, z - 1, c))
z_far = links(lambda xh, xl, y, z, c: (xh, xl, y, z + 2, c))
y_up = links(lambda xh, xl, y, z, c: (xh, xl, y + 1, z, c))
y_down = links(lambda xh, xl, y, z, c: (xh, xl, y - 1, z, c))
y_far = links(lambda xh, xl, y, z, c: (xh, xl, y + 2, z, c))
x_far = links(lambda xh, xl, y, z, c: (1 - xh, xl, y, z, c))
x_near = links(lambda xh, xl, y, z, c: (xh, 1 - xl, y, z, c))
cores = links(lambda xh, xl, y, z, c: (xh, xl, y, z, 1 - c))
regroup = links(lambda xh, xl, y, z, c: (c, xl, y, z, xh))
home = links(lambda xh, xl, y, z, c: (c, xl, y, z, c) if xh != c else None)
ring_z = members(lambda xh, xl, y, z, c: (xh, xl, y, c))
ring_y = members(lambda xh, xl, y, z, c: (xh, xl, z, c))
image = members(lambda xh, xl, y, z, c: (xh, xl, y))


def move(values, pairs):
    return lax.ppermute(values, AXES, pairs)


def exchange(values, groups):
    return lax.all_to_all(values, AXES, 0, 0, axis_index_groups=groups, tiled=True)


def gather(values, groups):
    return lax.all_gather(values, AXES, axis=0, axis_index_groups=groups, tiled=True)


def ring_from(values, up, down, far):
    return [values, move(values, down), move(values, up), move(values, far)]


def spread(rows):
    half = exchange(jnp.concatenate([rows] * 4, 0), ring_z)
    return jnp.concatenate([half, move(half, cores)], 0)


def wide(values):
    return values.astype(f32)


def low(values):
    return values.astype(bf16)


def turn(values, axis, start):
    return lax.dynamic_slice_in_dim(jnp.concatenate([values, values], axis), start % 4, 4, axis)


def collect(lo, hi):
    mine = low(wide(lo) + wide(move(hi, cores)))
    got = exchange(mine, ring_z).reshape(4, -1, mine.shape[1])
    return jnp.sum(wide(got), 0)


def at_home(here, there, home_here):
    return jnp.where(home_here, here, there), jnp.where(home_here, there, here)


def shards(
    tokens,
    cotangent,
    w_qkv,
    qv_bias,
    w_out,
    w_fc1,
    b_fc1,
    w_fc2,
    norm_gain,
    norm_shift,
    out_bias,
    layer_scale,
):
    layer = 0
    place = lax.axis_index("dp")
    core = place % 2
    y = (place // 2) % 4
    x_hi = lax.axis_index("tensor") // 4
    z = lax.axis_index("tensor") % 4
    home_here = x_hi == core
    core_arg = core.astype(jnp.int32).reshape(1)
    width = w_qkv.shape[3]
    hidden_here = w_fc1.shape[2]
    own, model = tokens.shape

    rows_in = move(tokens, regroup)
    qkv_in = move(jnp.moveaxis(w_qkv[layer], 1, 0), regroup)
    biases = move(jnp.concatenate([qv_bias[layer].reshape(1, -1), b_fc1], 1), regroup)
    out_in = move(w_out[layer], regroup)
    grad_in = move(cotangent, regroup)
    fc1_in = move(w_fc1[layer], regroup)
    fc2_in = move(w_fc2[layer], regroup)
    qv_in = biases[:, : 2 * width].reshape(2, width)
    hidden_bias = biases[:, 2 * width :]

    tokens_full = spread(rows_in)
    out_full = gather(out_in, image)
    normed_full, query_rows, key_rows, value_rows = project(
        tokens_full, norm_gain[layer, 0:1], norm_shift[layer, 0:1], qkv_in, qv_in
    )
    mixed, log_total = attend(core_arg, query_rows, key_rows, value_rows)
    state = wide(rows_in)
    normed, inv_dev = norm_pieces(state)

    gradient = wide(grad_in)
    down_grad = low(layer_scale[layer, 1] * gradient)
    bias_two = jnp.sum(wide(down_grad), 0)
    down_full = gather(down_grad, image)

    pieces = exchange(mixed, image).reshape(8, own, width)
    mixed_own = jnp.moveaxis(pieces, 0, 1).reshape(own, model)
    branch = jnp.dot(mixed_own, out_full, preferred_element_type=f32) + out_bias[layer, 0]
    middle = state + layer_scale[layer, 0] * branch
    normed_two, inv_two = norm_pieces(middle)
    shifted_two = normed_two * norm_gain[layer, 1] + norm_shift[layer, 1]
    normed_two_full = spread(low(shifted_two))

    hidden, act_grad, partial_two, partial_f, hidden_sums = hidden_block(
        core_arg, normed_two_full, down_full, fc1_in, hidden_bias, fc2_in
    )
    half = normed_two_full.shape[0] // 2
    rows_two = collect(partial_two[:half], partial_two[half:])
    grad_b1 = hidden_sums[0]

    grad_fc2 = jnp.einsum("gf,gd->fd", hidden, down_full, preferred_element_type=f32)
    grad_fc1 = jnp.einsum("gd,gf->df", normed_two_full, act_grad, preferred_element_type=f32)
    joined = jnp.concatenate(
        [low(grad_fc1), low(grad_fc2[:, : model // 2]), low(grad_fc2[:, model // 2 :])], 0
    )
    fc_quarter = lax.psum_scatter(
        joined, AXES, scatter_dimension=0, axis_index_groups=ring_y, tiled=True
    )
    fc_quarter = low(wide(fc_quarter) + wide(move(fc_quarter, home)))
    fc_quarter = low(wide(fc_quarter) + wide(move(fc_quarter, x_near)))
    fc_half = fc_quarter.shape[0] // 2
    fc_part = jnp.where(home_here, fc_quarter[:fc_half], move(fc_quarter[fc_half:], cores))
    fc_got = gather(fc_part, ring_y).reshape(4, fc_half, -1)
    fc_first, fc_second = at_home(fc_got, move(fc_got, cores), home_here)
    fc_total = wide(jnp.stack([fc_first, fc_second], 1).reshape(joined.shape))
    total_fc1 = fc_total[:model]
    total_fc2 = jnp.concatenate(
        [fc_total[model : model + hidden_here], fc_total[model + hidden_here :]], 1
    )

    gain_two = jnp.sum(rows_two * normed_two, 0)
    shift_two = jnp.sum(rows_two, 0)
    gradient_two = gradient + norm_back(rows_two, normed_two, inv_two, norm_gain[layer, 1])
    scale_one = jnp.sum(gradient_two * branch, 0)
    attn_grad = low(layer_scale[layer, 0] * gradient_two)
    bias_one = jnp.sum(wide(attn_grad), 0)
    mixed_grad = low(
        jnp.einsum("gd,cd->gc", attn_grad, out_full, preferred_element_type=f32)
    )
    mixed_grad = jnp.moveaxis(mixed_grad.reshape(own, 8, width), 1, 0).reshape(8 * own, width)
    mixed_grad = exchange(mixed_grad, image)

    f_mine = low(wide(partial_f[:half]) + wide(move(partial_f[half:], cores)))
    f_turned = turn(f_mine.reshape(4, own, model), 0, z)
    sent = [jnp.concatenate([f_turned[n], attn_grad], 0) for n in range(4)]
    got = [sent[0], move(sent[3], z_down), move(sent[1], z_up), move(sent[2], z_far)]
    branch_two = (
        wide(got[0][:own]) + wide(got[1][:own]) + wide(got[2][:own]) + wide(got[3][:own])
    ) + out_bias[layer, 1]
    attn_half = jnp.concatenate([piece[own:] for piece in got], 0)
    attn_full = jnp.concatenate([attn_half, move(attn_half, cores)], 0)
    mixed_turned = turn(mixed.reshape(2, 4, own, width), 1, z)
    mixed_first, mixed_second = at_home(mixed_turned[0], mixed_turned[1], core == 0)
    mixed_turned = jnp.stack([mixed_first, mixed_second])
    mixed_turned = jnp.stack([mixed_turned[:, n] for n in (0, 1, 3, 2)], 1)
    grad_out = jnp.einsum(
        "gc,gd->cd",
        mixed_turned.reshape(8 * own, width),
        attn_full,
        preferred_element_type=f32,
    )
    state_out = move(middle + layer_scale[layer, 1] * branch_two, regroup)
    scale_two = jnp.sum(gradient * branch_two, 0)

    query_grad, key_grad, value_grad, qv_sums = attend_back(
        core_arg, query_rows, key_rows, value_rows, mixed_grad, log_total
    )
    stacked = jnp.stack([query_grad, key_grad, value_grad])
    grad_qkv = low(jnp.einsum("gd,tgc->tdc", normed_full, stacked, preferred_element_type=f32))
    early = jnp.stack(
        [
            jnp.zeros_like(gain_two),
            jnp.zeros_like(gain_two),
            gain_two,
            shift_two,
            bias_one,
            bias_two,
            scale_one,
            scale_two,
        ]
    )
    early = jnp.concatenate([early, jnp.zeros_like(early)], 0)
    lo, hi = project_back(query_grad, key_grad, value_grad, qkv_in, tokens_full, early)

    payload = jnp.concatenate(
        [grad_qkv.reshape(3 * model, width), low(grad_out).reshape(model, width)], 0
    )
    quarter = payload.shape[0] // 4
    payload = turn(payload.reshape(4, quarter, width), 0, y)
    rows_q = (
        wide(payload[0])
        + wide(move(payload[1], y_up))
        + wide(move(payload[3], y_down))
        + wide(move(payload[2], y_far))
    )

    hi_got = move(hi, cores)
    mine = low(wide(lo) + wide(hi_got[:half])).reshape(4, own, model)
    small = low(wide(hi[half:]) + wide(hi_got[half:]))
    mine = jnp.concatenate([mine, jnp.broadcast_to(small[None], (4, 16, model))], 1)
    got = exchange(mine.reshape(-1, model), ring_z).reshape(4, own + 16, model)
    rows_one = jnp.sum(wide(got[:, :own]), 0)
    small = low(jnp.sum(wide(got[:, own : own + 8]), 0)).reshape(8 * model // width, width)
    gradient_one = gradient_two + norm_back(rows_one, normed, inv_dev, norm_gain[layer, 0])
    gradient_out = move(gradient_one, regroup)

    wide_bias = jnp.concatenate(
        [qv_sums[:2].reshape(-1), grad_b1, jnp.zeros((model - 2 * width - hidden_here,), f32)]
    )
    wide_bias = jnp.concatenate([wide_bias, jnp.zeros_like(wide_bias)]).reshape(-1, width)
    flow = jnp.concatenate([low(rows_q), small, low(wide_bias)], 0)
    flow = low(wide(flow) + wide(move(flow, x_far)))
    flow = low(wide(flow) + wide(move(flow, x_near)))
    fine = quarter // 2
    kept = jnp.where(home_here, flow[:fine], move(flow[fine:quarter], cores))
    here, above, below, across = ring_from(
        jnp.concatenate([kept, flow[quarter:]], 0), y_up, y_down, y_far
    )
    tail = (wide(here[fine:]) + wide(across[fine:])) + (wide(above[fine:]) + wide(below[fine:]))
    small_total = tail[: 8 * model // width].reshape(8, model)
    bias_mine = low(tail[8 * model // width :])
    block = jnp.concatenate([here[:fine], above[:fine], across[:fine], below[:fine], bias_mine], 0)
    other = move(block, cores)
    first, second = at_home(block, other, home_here)
    ordered = jnp.stack(
        [first[: 4 * fine].reshape(4, fine, width), second[: 4 * fine].reshape(4, fine, width)], 1
    )
    total = wide(turn(ordered, 0, 4 - y).reshape(4 * quarter, width))
    total_qkv = jnp.moveaxis(total[: 3 * model].reshape(3, model, width), 0, 1)
    total_out = total[3 * model :].reshape(width, model)
    bias_total = wide(first[4 * fine :]).reshape(2, model)[:1]
    return (
        state_out,
        gradient_out,
        total_qkv[None],
        bias_total[:, : 2 * width].reshape(1, 2, width),
        total_out[None],
        total_fc1[None],
        bias_total[:, 2 * width : 2 * width + hidden_here],
        total_fc2[None],
        jnp.stack([small_total[0], small_total[2]])[None],
        jnp.stack([small_total[1], small_total[3]])[None],
        small_total[4:6][None],
        small_total[6:8][None],
    )


def solution(mesh):
    return jax.shard_map(
        shards,
        mesh=mesh,
        in_specs=(
            P(("dp", "tensor"), None),
            P(("dp", "tensor"), None),
            P(None, None, None, "tensor"),
            P(None, None, "tensor"),
            P(None, "tensor", None),
            P(None, None, "tensor"),
            P(None, "tensor"),
            P(None, "tensor", None),
            P(),
            P(),
            P(),
            P(),
        ),
        out_specs=(
            P(("dp", "tensor"), None),
            P(("dp", "tensor"), None),
            P(None, None, None, "tensor"),
            P(None, None, "tensor"),
            P(None, "tensor", None),
            P(None, None, "tensor"),
            P(None, "tensor"),
            P(None, "tensor", None),
            P(),
            P(),
            P(),
            P(),
        ),
        check_vma=False,
    )
```

profile of v0, /device:TPU:1, one launch (start us, length us, event | category | flops | bytes accessed | tf_op | source)
XLA Modules:
  0.0 375.2 jit_solution(10238525551067740284)
XLA Ops:
  7.3 6.2 %collective-permute-start.4 = (bf16[128,1024]{1,0:T(8,128)(2,1)}, bf16[128,1024]{1,0:T(8,128)(2,1)S(1)}, u32[]{:S(2)}, u32[]{:S(2)}) collective-permute-start(bf16[128,1024]{1,0:T(8,128)(2,1)} %bitcast.186), channel_id=1, source_target_pairs={{0,0},{8,4},{1,1},{9,5},{2,2},{10,6},{3,3},{11,7},{16,16},{24,20},... | collective-permute-start | bytes 786440 | tf_op jit(solution)/shard_map/ppermute | solution.py:349
  13.5 4.3 %collective-permute-done.4 = bf16[128,1024]{1,0:T(8,128)(2,1)S(1)} collective-permute-done((bf16[128,1024]{1,0:T(8,128)(2,1)}, bf16[128,1024]{1,0:T(8,128)(2,1)S(1)}, u32[]{:S(2)}, u32[]{:S(2)}) %collective-permute-start.4) | collective-permute-done | bytes 262176 | tf_op jit(solution)/shard_map/ppermute | solution.py:349
  18.5 5.1 %collective-permute-start = (bf16[128,1024]{1,0:T(8,128)(2,1)}, bf16[128,1024]{1,0:T(8,128)(2,1)S(1)}, u32[]{:S(2)}, u32[]{:S(2)}) collective-permute-start(bf16[128,1024]{1,0:T(8,128)(2,1)} %param.12), channel_id=1, source_target_pairs={{0,0},{8,4},{1,1},{9,5},{2,2},{10,6},{3,3},{11,7},{16,16},{24,20},... | collective-permute-start | bytes 786440 | tf_op jit(solution)/shard_map/ppermute | solution.py:349
  23.7 4.3 %collective-permute-done = bf16[128,1024]{1,0:T(8,128)(2,1)S(1)} collective-permute-done((bf16[128,1024]{1,0:T(8,128)(2,1)}, bf16[128,1024]{1,0:T(8,128)(2,1)S(1)}, u32[]{:S(2)}, u32[]{:S(2)}) %collective-permute-start) | collective-permute-done | bytes 262176 | tf_op jit(solution)/shard_map/ppermute | solution.py:349
  28.1 20.7 %all_to_all.56 = bf16[4,128,1024]{2,1,0:T(8,128)(2,1)S(1)} all-to-all(bf16[4,128,1024]{2,1,0:T(8,128)(2,1)S(1)} %bitcast.146), channel_id=1, replica_groups={{0,1,2,3},{64,65,66,67},{4,5,6,7},{68,69,70,71},{16,17,18,19},{80,81,82..., dimensions={0} | all-to-all | bytes 2097152 | tf_op jit(solution)/shard_map/all_to_all | solution.py:353
  48.8 5.2 %collective-permute-start.6 = (bf16[128,1024]{1,0:T(8,128)(2,1)S(1)}, bf16[128,1024]{1,0:T(8,128)(2,1)S(1)}, u32[]{:S(2)}, u32[]{:S(2)}) collective-permute-start(bf16[128,1024]{1,0:T(8,128)(2,1)S(1)} %copy-done.49), channel_id=1, source_target_pairs={{0,0},{8,4},{1,1},{9,5},{2,2},{10,6},{3,3},{11,7},{16,16},{24,20},... | collective-permute-start | bytes 786440 | tf_op jit(solution)/shard_map/ppermute | solution.py:349
  55.9 5.1 %collective-permute-start.3 = (f32[1,768]{1,0:T(1,128)S(1)}, f32[1,768]{1,0:T(1,128)S(1)}, u32[]{:S(2)}, u32[]{:S(2)}) collective-permute-start(f32[1,768]{1,0:T(1,128)S(1)} %pad_maximum_fusion.13), channel_id=1, source_target_pairs={{0,0},{8,4},{1,1},{9,5},{2,2},{10,6},{3,3},{11,7},{16,16},{24,20},... | collective-permute-start | bytes 9224 | tf_op jit(solution)/shard_map/ppermute | solution.py:349
  61.2 7.8 %collective-permute-done.3 = f32[1,768]{1,0:T(1,128)S(1)} collective-permute-done((f32[1,768]{1,0:T(1,128)S(1)}, f32[1,768]{1,0:T(1,128)S(1)}, u32[]{:S(2)}, u32[]{:S(2)}) %collective-permute-start.3) | collective-permute-done | bytes 3104 | tf_op jit(solution)/shard_map/ppermute | solution.py:349
  76.4 5.4 %attend.1 = (bf16[1024,128]{1,0:T(8,128)(2,1)S(1)}, f32[2,1024]{1,0:T(2,128)S(1)}) custom-call(s32[1]{0:T(128)} %bitcast.1.core_ref, bf16[1024,128]{1,0:T(8,128)(2,1)S(1)} %get-tuple-element.29.q_ref, bf16[1024,128]{1,0:T(8,128)(2,1)S(1)} %get-tuple-element.30.k_ref, bf16[1024,128]{1,0:T(8,128)(2,1)S(1)} %get-tuple-element.31.v_ref), custom_call_target="tpu_custom_call" | custom-call | tf_op jit(solution)/shard_map/attend/pallas_call | solution.py:97
  83.3 4.0 %all-to-all-start.1 = ((bf16[8,128,128]{1,2,0:T(8,128)(2,1)}), bf16[8,128,128]{1,2,0:T(8,128)(2,1)}, u32[]{:S(2)}, u32[]{:S(2)}) async-start(bf16[8,128,128]{1,2,0:T(8,128)(2,1)} %copy.29), calls=%async_computation.1 | async-start | bytes 524288 | tf_op jit(solution)/shard_map/all_to_all | solution.py:353
  88.4 5.6 %all-to-all-done.1 = bf16[8,128,128]{1,2,0:T(8,128)(2,1)} async-done(((bf16[8,128,128]{1,2,0:T(8,128)(2,1)}), bf16[8,128,128]{1,2,0:T(8,128)(2,1)}, u32[]{:S(2)}, u32[]{:S(2)}) %all-to-all-start.1) | async-done | bytes 262176 | tf_op jit(solution)/shard_map/all_to_all | solution.py:353
  98.0 17.7 %all_to_all.57 = bf16[4,128,1024]{2,1,0:T(8,128)(2,1)} all-to-all(bf16[4,128,1024]{2,1,0:T(8,128)(2,1)S(1)} %bitcast.145), channel_id=1, replica_groups={{0,1,2,3},{64,65,66,67},{4,5,6,7},{68,69,70,71},{16,17,18,19},{80,81,82..., dimensions={0} | all-to-all | bytes 2097152 | tf_op jit(solution)/shard_map/all_to_all | solution.py:353
  117.2 3.9 %collective-permute-start.7 = (bf16[1024,512]{1,0:T(8,128)(2,1)}, bf16[1024,512]{1,0:T(8,128)(2,1)}, u32[]{:S(2)}, u32[]{:S(2)}) collective-permute-start(bf16[1024,512]{1,0:T(8,128)(2,1)} %bitcast.20), channel_id=1, source_target_pairs={{0,0},{8,4},{1,1},{9,5},{2,2},{10,6},{3,3},{11,7},{16,16},{24,20},... | collective-permute-start | bytes 3145736 | tf_op jit(solution)/shard_map/ppermute | solution.py:349
  128.2 6.9 %collective-permute-done.7.w1_ref = bf16[1024,512]{1,0:T(8,128)(2,1)} collective-permute-done((bf16[1024,512]{1,0:T(8,128)(2,1)}, bf16[1024,512]{1,0:T(8,128)(2,1)}, u32[]{:S(2)}, u32[]{:S(2)}) %collective-permute-start.7) | collective-permute-done | bytes 1048608 | tf_op jit(solution)/shard_map/ppermute | solution.py:349
  135.1 11.2 %collective-permute-done.8.w2_ref = bf16[512,1024]{1,0:T(8,128)(2,1)} collective-permute-done((bf16[512,1024]{1,0:T(8,128)(2,1)}, bf16[512,1024]{1,0:T(8,128)(2,1)}, u32[]{:S(2)}, u32[]{:S(2)}) %collective-permute-start.8) | collective-permute-done | bytes 1048608 | tf_op jit(solution)/shard_map/ppermute | solution.py:349
  146.3 8.9 %hidden_block.1 = (bf16[1024,512]{1,0:T(8,128)(2,1)S(1)}, bf16[1024,512]{1,0:T(8,128)(2,1)S(1)}, bf16[1024,1024]{1,0:T(8,128)(2,1)}, bf16[1024,1024]{1,0:T(8,128)(2,1)}, f32[8,512]{1,0:T(8,128)S(1)}) custom-call(s32[1]{0:T(128)} %bitcast.1.core_ref, bf16[1024,1024]{1,0:T(8,128)(2,1)} %pad_maximum_fusion.1.h_ref, ...), custom_call_target="tpu_custom_call" | custom-call | tf_op jit(solution)/shard_map/hidden_block/pallas_call | solution.py:212
  163.0 4.2 %all-to-all-start.3 = ((bf16[4,128,1024]{2,1,0:T(8,128)(2,1)}), bf16[4,128,1024]{2,1,0:T(8,128)(2,1)}, u32[]{:S(2)}, u32[]{:S(2)}) async-start(bf16[4,128,1024]{2,1,0:T(8,128)(2,1)} %bitcast.142), calls=%async_computation.3 | async-start | bytes 2097152 | tf_op jit(solution)/shard_map/all_to_all | solution.py:353
  167.5 4.3 %convolution_convert_fusion.1 = bf16[1024,512]{1,0:T(8,128)(2,1)} fusion(bf16[1024,512]{1,0:T(8,128)(2,1)} %copy-done.14, bf16[512,1024]{1,0:T(8,128)(2,1)} %collective-permute-done.5, bf16[512,1024]{1,0:T(8,128)(2,1)} %bitcast.19), kind=kOutput, calls=%fused_computation.22 | convolution fusion | flops 1078460416 | bytes 4194304 | tf_op jit(solution)/shard_map/gd,gf->df/dot_general | solution.py:457
  175.7 6.9 %all-to-all-done.3 = bf16[4,128,1024]{2,1,0:T(8,128)(2,1)} async-done(((bf16[4,128,1024]{2,1,0:T(8,128)(2,1)}), bf16[4,128,1024]{2,1,0:T(8,128)(2,1)}, u32[]{:S(2)}, u32[]{:S(2)}) %all-to-all-start.3) | async-done | bytes 1048608 | tf_op jit(solution)/shard_map/all_to_all | solution.py:353
  193.0 9.2 %collective-permute-done.11 = bf16[256,1024]{1,0:T(8,128)(2,1)} collective-permute-done((bf16[256,1024]{1,0:T(8,128)(2,1)}, bf16[256,1024]{1,0:T(8,128)(2,1)}, u32[]{:S(2)}, u32[]{:S(2)}) %collective-permute-start.11) | collective-permute-done | bytes 524320 | tf_op jit(solution)/shard_map/ppermute | solution.py:349
  207.0 7.3 %collective-permute-done.13 = bf16[256,1024]{1,0:T(8,128)(2,1)} collective-permute-done((bf16[256,1024]{1,0:T(8,128)(2,1)}, bf16[256,1024]{1,0:T(8,128)(2,1)}, u32[]{:S(2)}, u32[]{:S(2)}) %collective-permute-start.13) | collective-permute-done | bytes 524320 | tf_op jit(solution)/shard_map/ppermute | solution.py:349
  217.0 4.8 %collective-permute-start.17 = (bf16[512,1024]{1,0:T(8,128)(2,1)}, bf16[512,1024]{1,0:T(8,128)(2,1)}, u32[]{:S(2)}, u32[]{:S(2)}) collective-permute-start(bf16[512,1024]{1,0:T(8,128)(2,1)} %pad_maximum_fusion.6), channel_id=1, source_target_pairs={{0,8},{8,0},{1,9},{9,1},{2,10},{10,2},{3,11},{11,3},{16,24},{24,16... | collective-permute-start | bytes 3145736 | tf_op jit(solution)/shard_map/ppermute | solution.py:349
  229.1 4.3 %all-to-all-done.4 = bf16[8,128,128]{2,1,0:T(8,128)(2,1)S(1)} async-done(((bf16[8,128,128]{2,1,0:T(8,128)(2,1)}), bf16[8,128,128]{2,1,0:T(8,128)(2,1)S(1)}, u32[]{:S(2)}, u32[]{:S(2)}) %all-to-all-start.4) | async-done | bytes 262176 | tf_op jit(solution)/shard_map/all_to_all | solution.py:353
  235.3 8.3 %attend_back.1 = (bf16[1024,128]{1,0:T(8,128)(2,1)S(1)}, bf16[1024,128]{1,0:T(8,128)(2,1)S(1)}, bf16[1024,128]{1,0:T(8,128)(2,1)S(1)}, f32[8,128]{1,0:T(8,128)S(1)}) custom-call(s32[1]{0:T(128)} %bitcast.1.core_ref, bf16[1024,128]{1,0:T(8,128)(2,1)S(1)} %get-tuple-element.29.q_ref, bf16[1024,128]{1,0:T(8,128)(2,1)S(1)} %bitcast.136, ...), custom_call_target="tpu_custom_call" | custom-call | tf_op jit(solution)/shard_map/attend_back/pallas_call | solution.py:169
  249.8 4.5 %project_back.1 = (bf16[512,1024]{1,0:T(8,128)(2,1)S(1)}, bf16[528,1024]{1,0:T(8,128)(2,1)}) custom-call(bf16[1024,128]{1,0:T(8,128)(2,1)S(1)} %copy-done.7, bf16[1024,128]{1,0:T(8,128)(2,1)S(1)} %copy-done.9, bf16[1024,128]{1,0:T(8,128)(2,1)S(1)} %copy-done.11, bf16[3,1024,128]{2,1,0:T(8,128)(2,1)S(1)} %collective-permute-done.2.w_ref, ...), custom_call_target="tpu_custom_call" | custom-call | tf_op jit(solution)/shard_map/project_back/pallas_call | solution.py:275
  276.7 4.3 %collective-permute-start.14 = (f32[128,1024]{1,0:T(8,128)}, f32[128,1024]{1,0:T(8,128)S(1)}, u32[]{:S(2)}, u32[]{:S(2)}) collective-permute-start(f32[128,1024]{1,0:T(8,128)} %get-tuple-element.63), channel_id=1, source_target_pairs={{0,0},{8,4},{1,1},{9,5},{2,2},{10,6},{3,3},{11,7},{16,16},{24,20},... | collective-permute-start | bytes 1572872 | tf_op jit(solution)/shard_map/ppermute | solution.py:349
  281.3 5.4 %collective-permute-done.19 = bf16[1024,128]{1,0:T(8,128)(2,1)S(1)} collective-permute-done((bf16[1024,128]{1,0:T(8,128)(2,1)S(1)}, bf16[1024,128]{1,0:T(8,128)(2,1)S(1)}, u32[]{:S(2)}, u32[]{:S(2)}) %collective-permute-start.19) | collective-permute-done | bytes 262176 | tf_op jit(solution)/shard_map/ppermute | solution.py:349
  291.4 11.7 %collective-permute-done.21 = bf16[1104,128]{1,0:T(8,128)(2,1)S(1)} collective-permute-done((bf16[1104,128]{1,0:T(8,128)(2,1)S(1)}, bf16[1104,128]{1,0:T(8,128)(2,1)S(1)}, u32[]{:S(2)}, u32[]{:S(2)}) %collective-permute-start.21) | collective-permute-done | bytes 282656 | tf_op jit(solution)/shard_map/ppermute | solution.py:349
  305.0 3.7 collective-permute-done.22
  308.8 8.2 %collective-permute-start.23 = (bf16[512,128]{1,0:T(8,128)(2,1)S(1)}, bf16[512,128]{1,0:T(8,128)(2,1)S(1)}, u32[]{:S(2)}, u32[]{:S(2)}) collective-permute-start(bf16[512,128]{1,0:T(8,128)(2,1)S(1)} %slice.366), channel_id=1, source_target_pairs={{0,8},{8,0},{1,9},{9,1},{2,10},{10,2},{3,11},{11,3},{16,24},{24,16... | collective-permute-start | bytes 393224 | tf_op jit(solution)/shard_map/ppermute | solution.py:349
  326.0 6.0 %collective-permute-done.16 = f32[128,1024]{1,0:T(8,128)S(1)} collective-permute-done((f32[128,1024]{1,0:T(8,128)S(1)}, f32[128,1024]{1,0:T(8,128)S(1)}, u32[]{:S(2)}, u32[]{:S(2)}) %collective-permute-start.16) | collective-permute-done | bytes 524320 | tf_op jit(solution)/shard_map/ppermute | solution.py:349
  343.4 14.3 %all-gather.8.cloned.1.call-done = bf16[1024,512]{1,0:T(8,128)(2,1)} async-done(((bf16[256,512]{1,0:T(8,128)(2,1)}), bf16[1024,512]{1,0:T(8,128)(2,1)}) %all-gather.8.cloned.1.call-update) | async-done | bytes 1048592 | tf_op jit(solution)/shard_map/all_gather | solution.py:357
  (278 shorter events, 130.6 us)
Async XLA Ops:
  7.3 86.7 %all-gather.4.cloned.1.call-start = ((), (), s32[]{:S(2)}) async-start(), calls=%async_computation.7 | async-start | bytes 2359296 | tf_op jit(solution)/shard_map/all_gather | solution.py:357
  7.3 10.4 %collective-permute-start.4 = (bf16[128,1024]{1,0:T(8,128)(2,1)}, bf16[128,1024]{1,0:T(8,128)(2,1)S(1)}, u32[]{:S(2)}, u32[]{:S(2)}) collective-permute-start(bf16[128,1024]{1,0:T(8,128)(2,1)} %bitcast.186), channel_id=1, source_target_pairs={{0,0},{8,4},{1,1},{9,5},{2,2},{10,6},{3,3},{11,7},{16,16},{24,20},... | collective-permute-start | bytes 786440 | tf_op jit(solution)/shard_map/ppermute | solution.py:349
  18.5 127.9 %all-gather.6.cloned.1.call-start = ((), (), s32[]{:S(2)}) async-start(), calls=%async_computation.8 | async-start | bytes 2359296 | tf_op jit(solution)/shard_map/all_gather | solution.py:357
  18.5 9.5 %collective-permute-start = (bf16[128,1024]{1,0:T(8,128)(2,1)}, bf16[128,1024]{1,0:T(8,128)(2,1)S(1)}, u32[]{:S(2)}, u32[]{:S(2)}) collective-permute-start(bf16[128,1024]{1,0:T(8,128)(2,1)} %param.12), channel_id=1, source_target_pairs={{0,0},{8,4},{1,1},{9,5},{2,2},{10,6},{3,3},{11,7},{16,16},{24,20},... | collective-permute-start | bytes 786440 | tf_op jit(solution)/shard_map/ppermute | solution.py:349
  48.8 21.1 %collective-permute-start.1 = (bf16[512,1024]{1,0:T(8,128)(2,1)S(1)}, bf16[512,1024]{1,0:T(8,128)(2,1)}, u32[]{:S(2)}, u32[]{:S(2)}) collective-permute-start(bf16[512,1024]{1,0:T(8,128)(2,1)S(1)} %bitcast.147), channel_id=1, source_target_pairs={{0,8},{8,0},{1,9},{9,1},{2,10},{10,2},{3,11},{11,3},{16,24},{24,16... | collective-permute-start | bytes 3145736 | tf_op jit(solution)/shard_map/ppermute | solution.py:349
  48.8 20.3 %collective-permute-start.6 = (bf16[128,1024]{1,0:T(8,128)(2,1)S(1)}, bf16[128,1024]{1,0:T(8,128)(2,1)S(1)}, u32[]{:S(2)}, u32[]{:S(2)}) collective-permute-start(bf16[128,1024]{1,0:T(8,128)(2,1)S(1)} %copy-done.49), channel_id=1, source_target_pairs={{0,0},{8,4},{1,1},{9,5},{2,2},{10,6},{3,3},{11,7},{16,16},{24,20},... | collective-permute-start | bytes 786440 | tf_op jit(solution)/shard_map/ppermute | solution.py:349
  54.0 17.6 %collective-permute-start.2 = (bf16[3,1024,128]{2,1,0:T(8,128)(2,1)}, bf16[3,1024,128]{2,1,0:T(8,128)(2,1)S(1)}, u32[]{:S(2)}, u32[]{:S(2)}) collective-permute-start(bf16[3,1024,128]{2,1,0:T(8,128)(2,1)} %bitcast.7), channel_id=1, source_target_pairs={{0,0},{8,4},{1,1},{9,5},{2,2},{10,6},{3,3},{11,7},{16,16},{24,20},... | collective-permute-start | bytes 2359304 | tf_op jit(solution)/shard_map/ppermute | solution.py:349
  55.9 13.1 %collective-permute-start.3 = (f32[1,768]{1,0:T(1,128)S(1)}, f32[1,768]{1,0:T(1,128)S(1)}, u32[]{:S(2)}, u32[]{:S(2)}) collective-permute-start(f32[1,768]{1,0:T(1,128)S(1)} %pad_maximum_fusion.13), channel_id=1, source_target_pairs={{0,0},{8,4},{1,1},{9,5},{2,2},{10,6},{3,3},{11,7},{16,16},{24,20},... | collective-permute-start | bytes 9224 | tf_op jit(solution)/shard_map/ppermute | solution.py:349
  83.3 10.6 %all-to-all-start.1 = ((bf16[8,128,128]{1,2,0:T(8,128)(2,1)}), bf16[8,128,128]{1,2,0:T(8,128)(2,1)}, u32[]{:S(2)}, u32[]{:S(2)}) async-start(bf16[8,128,128]{1,2,0:T(8,128)(2,1)} %copy.29), calls=%async_computation.1 | async-start | bytes 524288 | tf_op jit(solution)/shard_map/all_to_all | solution.py:353
  117.2 17.9 %collective-permute-start.7 = (bf16[1024,512]{1,0:T(8,128)(2,1)}, bf16[1024,512]{1,0:T(8,128)(2,1)}, u32[]{:S(2)}, u32[]{:S(2)}) collective-permute-start(bf16[1024,512]{1,0:T(8,128)(2,1)} %bitcast.20), channel_id=1, source_target_pairs={{0,0},{8,4},{1,1},{9,5},{2,2},{10,6},{3,3},{11,7},{16,16},{24,20},... | collective-permute-start | bytes 3145736 | tf_op jit(solution)/shard_map/ppermute | solution.py:349
  121.1 25.3 %collective-permute-start.8 = (bf16[512,1024]{1,0:T(8,128)(2,1)}, bf16[512,1024]{1,0:T(8,128)(2,1)}, u32[]{:S(2)}, u32[]{:S(2)}) collective-permute-start(bf16[512,1024]{1,0:T(8,128)(2,1)} %bitcast.21), channel_id=1, source_target_pairs={{0,0},{8,4},{1,1},{9,5},{2,2},{10,6},{3,3},{11,7},{16,16},{24,20},... | collective-permute-start | bytes 3145736 | tf_op jit(solution)/shard_map/ppermute | solution.py:349
  158.9 12.9 %collective-permute-start.9 = (bf16[512,1024]{1,0:T(8,128)(2,1)}, bf16[512,1024]{1,0:T(8,128)(2,1)}, u32[]{:S(2)}, u32[]{:S(2)}) collective-permute-start(bf16[512,1024]{1,0:T(8,128)(2,1)} %slice.269), channel_id=1, source_target_pairs={{0,8},{8,0},{1,9},{9,1},{2,10},{10,2},{3,11},{11,3},{16,24},{24,16... | collective-permute-start | bytes 3145736 | tf_op jit(solution)/shard_map/ppermute | solution.py:349
  163.0 19.5 %all-to-all-start.3 = ((bf16[4,128,1024]{2,1,0:T(8,128)(2,1)}), bf16[4,128,1024]{2,1,0:T(8,128)(2,1)}, u32[]{:S(2)}, u32[]{:S(2)}) async-start(bf16[4,128,1024]{2,1,0:T(8,128)(2,1)} %bitcast.142), calls=%async_computation.3 | async-start | bytes 2097152 | tf_op jit(solution)/shard_map/all_to_all | solution.py:353
  167.3 120.2 %reduce-scatter.2.cloned.1.call-start = ((), (), s32[]{:S(2)}) async-start(), calls=%async_computation.9 | async-start | bytes 2621440 | tf_op jit(solution)/shard_map/reduce_scatter | solution.py:461
  189.3 13.0 %collective-permute-start.11 = (bf16[256,1024]{1,0:T(8,128)(2,1)}, bf16[256,1024]{1,0:T(8,128)(2,1)}, u32[]{:S(2)}, u32[]{:S(2)}) collective-permute-start(bf16[256,1024]{1,0:T(8,128)(2,1)} %get-tuple-element.85), channel_id=1, source_target_pairs={{0,3},{8,11},{1,0},{9,8},{2,1},{10,9},{3,2},{11,10},{16,19},{24,27... | collective-permute-start | bytes 1572872 | tf_op jit(solution)/shard_map/ppermute | solution.py:349
  190.3 15.1 %collective-permute-start.12 = (bf16[256,1024]{1,0:T(8,128)(2,1)}, bf16[256,1024]{1,0:T(8,128)(2,1)}, u32[]{:S(2)}, u32[]{:S(2)}) collective-permute-start(bf16[256,1024]{1,0:T(8,128)(2,1)} %get-tuple-element.87), channel_id=1, source_target_pairs={{0,1},{8,9},{1,2},{9,10},{2,3},{10,11},{3,0},{11,8},{16,17},{24,25... | collective-permute-start | bytes 1572872 | tf_op jit(solution)/shard_map/ppermute | solution.py:349
  192.4 21.9 %collective-permute-start.13 = (bf16[256,1024]{1,0:T(8,128)(2,1)}, bf16[256,1024]{1,0:T(8,128)(2,1)}, u32[]{:S(2)}, u32[]{:S(2)}) collective-permute-start(bf16[256,1024]{1,0:T(8,128)(2,1)} %get-tuple-element.86), channel_id=1, source_target_pairs={{0,2},{8,10},{1,3},{9,11},{2,0},{10,8},{3,1},{11,9},{16,18},{24,26... | collective-permute-start | bytes 1572872 | tf_op jit(solution)/shard_map/ppermute | solution.py:349
  217.0 42.1 %collective-permute-start.17 = (bf16[512,1024]{1,0:T(8,128)(2,1)}, bf16[512,1024]{1,0:T(8,128)(2,1)}, u32[]{:S(2)}, u32[]{:S(2)}) collective-permute-start(bf16[512,1024]{1,0:T(8,128)(2,1)} %pad_maximum_fusion.6), channel_id=1, source_target_pairs={{0,8},{8,0},{1,9},{9,1},{2,10},{10,2},{3,11},{11,3},{16,24},{24,16... | collective-permute-start | bytes 3145736 | tf_op jit(solution)/shard_map/ppermute | solution.py:349
  223.5 9.9 %all-to-all-start.4 = ((bf16[8,128,128]{2,1,0:T(8,128)(2,1)}), bf16[8,128,128]{2,1,0:T(8,128)(2,1)S(1)}, u32[]{:S(2)}, u32[]{:S(2)}) async-start(bf16[8,128,128]{2,1,0:T(8,128)(2,1)} %bitcast.159), calls=%async_computation.4 | async-start | bytes 524288 | tf_op jit(solution)/shard_map/all_to_all | solution.py:353
  267.7 23.1 %all-to-all-start.5 = ((bf16[4,144,1024]{2,1,0:T(8,128)(2,1)}), bf16[4,144,1024]{2,1,0:T(8,128)(2,1)S(1)}, u32[]{:S(2)}, u32[]{:S(2)}) async-start(bf16[4,144,1024]{2,1,0:T(8,128)(2,1)} %pad_maximum_fusion.3), calls=%async_computation.5 | async-start | bytes 2359296 | tf_op jit(solution)/shard_map/all_to_all | solution.py:353
  271.2 86.5 %all-gather.8.cloned.1.call-start = ((), (), s32[]{:S(2)}) async-start(), calls=%async_computation.10 | async-start | bytes 1310720 | tf_op jit(solution)/shard_map/all_gather | solution.py:357
  274.5 12.2 %collective-permute-start.19 = (bf16[1024,128]{1,0:T(8,128)(2,1)S(1)}, bf16[1024,128]{1,0:T(8,128)(2,1)S(1)}, u32[]{:S(2)}, u32[]{:S(2)}) collective-permute-start(bf16[1024,128]{1,0:T(8,128)(2,1)S(1)} %get-tuple-element.71), channel_id=1, source_target_pairs={{0,48},{8,56},{1,49},{9,57},{2,50},{10,58},{3,51},{11,59},{16,0},{... | collective-permute-start | bytes 786440 | tf_op jit(solution)/shard_map/ppermute | solution.py:349
  275.6 11.8 %collective-permute-start.18 = (bf16[1024,128]{1,0:T(8,128)(2,1)S(1)}, bf16[1024,128]{1,0:T(8,128)(2,1)S(1)}, u32[]{:S(2)}, u32[]{:S(2)}) collective-permute-start(bf16[1024,128]{1,0:T(8,128)(2,1)S(1)} %get-tuple-element.70), channel_id=1, source_target_pairs={{0,16},{8,24},{1,17},{9,25},{2,18},{10,26},{3,19},{11,27},{16,32},... | collective-permute-start | bytes 786440 | tf_op jit(solution)/shard_map/ppermute | solution.py:349
  276.7 49.3 %collective-permute-start.14 = (f32[128,1024]{1,0:T(8,128)}, f32[128,1024]{1,0:T(8,128)S(1)}, u32[]{:S(2)}, u32[]{:S(2)}) collective-permute-start(f32[128,1024]{1,0:T(8,128)} %get-tuple-element.63), channel_id=1, source_target_pairs={{0,0},{8,4},{1,1},{9,5},{2,2},{10,6},{3,3},{11,7},{16,16},{24,20},... | collective-permute-start | bytes 1572872 | tf_op jit(solution)/shard_map/ppermute | solution.py:349
  287.6 16.2 %collective-permute-start.28 = (bf16[512,512]{1,0:T(8,128)(2,1)}, bf16[512,512]{1,0:T(8,128)(2,1)S(1)}, u32[]{:S(2)}, u32[]{:S(2)}) collective-permute-start(bf16[512,512]{1,0:T(8,128)(2,1)} %reduce-scatter.2.cloned.1.call-done), channel_id=1, source_target_pairs={{8,12},{9,13},{10,14},{11,15},{24,28},{25,29},{26,30},{27,31},{40,... | collective-permute-start | bytes 1572872 | tf_op jit(solution)/shard_map/ppermute | solution.py:349
  290.8 12.3 %collective-permute-start.21 = (bf16[1104,128]{1,0:T(8,128)(2,1)S(1)}, bf16[1104,128]{1,0:T(8,128)(2,1)S(1)}, u32[]{:S(2)}, u32[]{:S(2)}) collective-permute-start(bf16[1104,128]{1,0:T(8,128)(2,1)S(1)} %pad_maximum_fusion.11), channel_id=1, source_target_pairs={{0,4},{8,12},{1,5},{9,13},{2,6},{10,14},{3,7},{11,15},{16,20},{24,... | collective-permute-start | bytes 847880 | tf_op jit(solution)/shard_map/ppermute | solution.py:349
  303.9 18.2 %collective-permute-start.29 = (bf16[512,512]{1,0:T(8,128)(2,1)S(1)}, bf16[512,512]{1,0:T(8,128)(2,1)S(1)}, u32[]{:S(2)}, u32[]{:S(2)}) collective-permute-start(bf16[512,512]{1,0:T(8,128)(2,1)S(1)} %add_convert_fusion.4), channel_id=1, source_target_pairs={{0,64},{8,72},{1,65},{9,73},{2,66},{10,74},{3,67},{11,75},{16,80},... | collective-permute-start | bytes 1572872 | tf_op jit(solution)/shard_map/ppermute | solution.py:349
  308.8 10.4 %collective-permute-start.23 = (bf16[512,128]{1,0:T(8,128)(2,1)S(1)}, bf16[512,128]{1,0:T(8,128)(2,1)S(1)}, u32[]{:S(2)}, u32[]{:S(2)}) collective-permute-start(bf16[512,128]{1,0:T(8,128)(2,1)S(1)} %slice.366), channel_id=1, source_target_pairs={{0,8},{8,0},{1,9},{9,1},{2,10},{10,2},{3,11},{11,3},{16,24},{24,16... | collective-permute-start | bytes 393224 | tf_op jit(solution)/shard_map/ppermute | solution.py:349
  317.3 14.6 %collective-permute-start.16 = (f32[128,1024]{1,0:T(8,128)S(1)}, f32[128,1024]{1,0:T(8,128)S(1)}, u32[]{:S(2)}, u32[]{:S(2)}) collective-permute-start(f32[128,1024]{1,0:T(8,128)S(1)} %fusion.27), channel_id=1, source_target_pairs={{0,0},{8,4},{1,1},{9,5},{2,2},{10,6},{3,3},{11,7},{16,16},{24,20},... | collective-permute-start | bytes 1572872 | tf_op jit(solution)/shard_map/ppermute | solution.py:349
  320.0 15.2 %collective-permute-start.24 = (bf16[592,128]{1,0:T(8,128)(2,1)}, bf16[592,128]{1,0:T(8,128)(2,1)}, u32[]{:S(2)}, u32[]{:S(2)}) collective-permute-start(bf16[592,128]{1,0:T(8,128)(2,1)} %pad_maximum_fusion.12), channel_id=1, source_target_pairs={{0,48},{8,56},{1,49},{9,57},{2,50},{10,58},{3,51},{11,59},{16,0},{... | collective-permute-start | bytes 454664 | tf_op jit(solution)/shard_map/ppermute | solution.py:349
  322.3 13.8 %collective-permute-start.30 = (bf16[256,512]{1,0:T(8,128)(2,1)S(1)}, bf16[256,512]{1,0:T(8,128)(2,1)S(1)}, u32[]{:S(2)}, u32[]{:S(2)}) collective-permute-start(bf16[256,512]{1,0:T(8,128)(2,1)S(1)} %slice.385), channel_id=1, source_target_pairs={{0,8},{8,0},{1,9},{9,1},{2,10},{10,2},{3,11},{11,3},{16,24},{24,16... | collective-permute-start | bytes 786440 | tf_op jit(solution)/shard_map/ppermute | solution.py:349
  340.8 18.4 %collective-permute-start.27 = (bf16[2064,128]{1,0:T(8,128)(2,1)S(1)}, bf16[2064,128]{1,0:T(8,128)(2,1)S(1)}, u32[]{:S(2)}, u32[]{:S(2)}) collective-permute-start(bf16[2064,128]{1,0:T(8,128)(2,1)S(1)} %constant_dynamic-update-slice_fusion.5), channel_id=1, source_target_pairs={{0,8},{8,0},{1,9},{9,1},{2,10},{10,2},{3,11},{11,3},{16,24},{24,16... | collective-permute-start | bytes 1585160 | tf_op jit(solution)/shard_map/ppermute | solution.py:349
  (58 other events, 693.0 us)
Sparse Core Ops, SparseCore 0:
  18.6 32.0 all-gather.3
  70.0 25.4 all-gather.5
  193.2 30.5 reduce-scatter.1
  337.0 20.6 all-gather.7
where the time goes:
time: 378 us; the launch traced here: 375 us
  waiting for transfers between devices  114 us (30%)
  starting transfers between devices  89.8 us (24%)
  blocking collectives  38.4 us (10%)
  other arithmetic  38.1 us (10%)
  local copies, waits for them, and re-layouts  34.9 us (9%)
  Pallas kernels  30.5 us (8%)
  between operations  14.9 us (4%)
  matrix products  14.4 us (4%)
    ppermute x32, waiting for transfers between devices, move(): return lax.ppermute(values, AXES, pairs)  83.2 us
    ppermute x32, starting transfers between devices, move(): return lax.ppermute(values, AXES, pairs)  74.1 us
    all_to_all x2, blocking collectives, exchange(): lax.all_to_all(values, AXES, 0, 0, axis_index_groups=groups, tiled=True)  38.4 us
    all_to_all x4, waiting for transfers between devices, exchange(): lax.all_to_all(values, AXES, 0, 0, axis_index_groups=groups, tiled=True)  16.7 us
    all_to_all x4, starting transfers between devices, exchange(): lax.all_to_all(values, AXES, 0, 0, axis_index_groups=groups, tiled=True)  15.1 us
    all_gather x3, waiting for transfers between devices, gather(): lax.all_gather(values, AXES, axis=0, axis_index_groups=groups, tiled=True)  14.3 us
    unnamed x105, local copies, waits for them, and re-layouts  14.2 us
    pallas_call x1, Pallas kernels, hidden_block(): pl.pallas_call(hidden_kernel, grid_spec=pltpu.PrefetchScalarGridSpec(num_...  8.88 us
  transfers between devices with their start and end apart: 40, of which 20 were waited for; matrix products, arithmetic and copies ran while one was open for 17% of the time, Pallas kernels for 6%

commit v1 on v0

v1 whole, which is shorter than its diff:
```python
import functools

import jax
import jax.numpy as jnp
from jax import lax
from jax.experimental import pallas as pl
from jax.experimental.pallas import tpu as pltpu
from jax.sharding import PartitionSpec as P

HD = 64
BLOCK = 256
inv_root_two = 0.7071067811865476
inv_root_two_pi = 0.3989422804014327
f32 = jnp.float32
bf16 = jnp.bfloat16


def dot_nn(a, b):
    return lax.dot_general(a, b, (((1,), (0,)), ((), ())), preferred_element_type=f32)


def dot_nt(a, b):
    return lax.dot_general(a, b, (((1,), (1,)), ((), ())), preferred_element_type=f32)


def params(mebibytes=24):
    return pltpu.CompilerParams(vmem_limit_bytes=mebibytes * 1024 * 1024)


def whole(shape):
    return pl.BlockSpec(shape, lambda i, *_: (0,) * len(shape))


def rows_of(width, block=BLOCK):
    return pl.BlockSpec((block, width), lambda i, *_: (i, 0))


def rows_in_order(width, blocks):
    return pl.BlockSpec((BLOCK, width), lambda i, core: ((i + core[0] * (blocks // 2)) % blocks, 0))


def half_specs(width, blocks):
    half = blocks // 2
    return [
        pl.BlockSpec((BLOCK, width), lambda i, *_: (jnp.minimum(i, half - 1), 0)),
        pl.BlockSpec((BLOCK, width), lambda i, *_: (jnp.maximum(i - half, 0), 0)),
    ]


def from_halves(lo_ref, hi_ref):
    return jnp.where(pl.program_id(0) < pl.num_programs(0) // 2, lo_ref[...], hi_ref[...])


def to_halves(values, lo_ref, hi_ref):
    step = pl.program_id(0)
    half = pl.num_programs(0) // 2

    @pl.when(step < half)
    def _():
        lo_ref[pl.ds(pl.multiple_of(step * BLOCK, BLOCK), BLOCK), :] = values

    @pl.when(step >= half)
    def _():
        hi_ref[pl.ds(pl.multiple_of((step - half) * BLOCK, BLOCK), BLOCK), :] = values


def norm_pieces(values):
    centred = values - jnp.mean(values, -1, keepdims=True)
    inv_dev = lax.rsqrt(jnp.mean(centred * centred, -1, keepdims=True) + 1e-06)
    return centred * inv_dev, inv_dev


def project_kernel(lo_ref, hi_ref, gain_ref, shift_ref, w_ref, bias_ref, h_ref, q_ref, k_ref, v_ref):
    normed, _ = norm_pieces(from_halves(lo_ref, hi_ref).astype(f32))
    h = (normed * gain_ref[...] + shift_ref[...]).astype(bf16)
    h_ref[...] = h
    q_ref[...] = (dot_nn(h, w_ref[0]) + bias_ref[0:1, :]).astype(bf16)
    k_ref[...] = dot_nn(h, w_ref[1]).astype(bf16)
    v_ref[...] = (dot_nn(h, w_ref[2]) + bias_ref[1:2, :]).astype(bf16)


def project(lo, hi, gain, shift, w, bias):
    rows, model = 2 * lo.shape[0], lo.shape[1]
    width = w.shape[2]
    out = jax.ShapeDtypeStruct((rows, width), bf16)
    return pl.pallas_call(
        project_kernel,
        grid=(rows // BLOCK,),
        in_specs=half_specs(model, rows // BLOCK)
        + [whole((1, model)), whole((1, model)), whole(w.shape), whole(bias.shape)],
        out_specs=[rows_of(model)] + [rows_of(width)] * 3,
        out_shape=[jax.ShapeDtypeStruct((rows, model), bf16), out, out, out],
        compiler_params=params(),
        name="norm_project",
    )(lo, hi, gain, shift, w, bias)


def lane_mask(shape, head, dim):
    return (lax.broadcasted_iota(jnp.int32, shape, dim) // HD) == head


def only_head(values, head, dim=1):
    return jnp.where(lane_mask(values.shape, head, dim), values, jnp.zeros_like(values))


def attend_kernel(core_ref, q_ref, k_ref, v_ref, o_ref, own_ref, lse_ref):
    q = q_ref[...] * jnp.asarray(HD**-0.5, bf16)
    v_t = v_ref[...].T
    total = None
    for head in range(q.shape[1] // HD):
        scores = dot_nt(k_ref[...], only_head(q, head))
        top = jnp.max(scores, 0, keepdims=True)
        shifted = jnp.exp(scores - top)
        row_sum = jnp.sum(shifted, 0, keepdims=True)
        prob = (shifted * (1.0 / row_sum)).astype(bf16)
        lse_ref[head : head + 1, :] = top + jnp.log(row_sum)
        piece = dot_nn(only_head(v_t, head, 0), prob)
        total = piece if total is None else total + piece
    o = total.astype(bf16).T
    o_ref[...] = o
    own_ref[...] = o


def attend(core, q, k, v):
    rows, width = q.shape
    heads = width // HD
    return pl.pallas_call(
        attend_kernel,
        grid_spec=pltpu.PrefetchScalarGridSpec(
            num_scalar_prefetch=1,
            grid=(rows // BLOCK,),
            in_specs=[rows_of(width), whole(k.shape), whole(v.shape)],
            out_specs=[
                rows_in_order(width, rows // BLOCK),
                rows_of(width),
                pl.BlockSpec((heads, BLOCK), lambda i, *_: (0, i)),
            ],
        ),
        out_shape=[jax.ShapeDtypeStruct((rows, width), bf16)] * 2 + [jax.ShapeDtypeStruct((heads, rows), f32)],
        compiler_params=params(),
        name="attend",
    )(core, q, k, v)


def attend_back_kernel(
    q_ref,
    do_lo_ref,
    do_hi_ref,
    lse_ref,
    k_ref,
    v_ref,
    dq_ref,
    dk_ref,
    dv_ref,
    sum_ref,
    dk_acc,
    dv_acc,
):
    step = pl.program_id(0)
    last = pl.num_programs(0) - 1
    scale = HD**-0.5

    @pl.when(step == 0)
    def _():
        dk_acc[...] = jnp.zeros_like(dk_acc)
        dv_acc[...] = jnp.zeros_like(dv_acc)
        sum_ref[...] = jnp.zeros_like(sum_ref)

    q = q_ref[...] * jnp.asarray(scale, bf16)
    do = from_halves(do_lo_ref, do_hi_ref)
    k_t = k_ref[...].T
    dq_t = None
    for head in range(q.shape[1] // HD):
        q_h = only_head(q, head)
        do_h = only_head(do, head)
        prob = jnp.exp(dot_nt(k_ref[...], q_h) - lse_ref[head : head + 1, :])
        d_prob = dot_nt(v_ref[...], do_h)
        row = jnp.sum(d_prob * prob, 0, keepdims=True)
        d_score = (prob * (d_prob - row)).astype(bf16)
        dv_acc[...] += dot_nn(prob.astype(bf16), do_h)
        dk_acc[...] += dot_nn(d_score, q_h)
        piece = dot_nn(only_head(k_t, head, 0), d_score)
        dq_t = piece if dq_t is None else dq_t + piece
    dq = (dq_t * scale).astype(bf16).T
    dq_ref[...] = dq
    sum_ref[0:1, :] += jnp.sum(dq.astype(f32), 0, keepdims=True)

    @pl.when(step == last)
    def _():
        dk_ref[...] = dk_acc[...].astype(bf16)
        dv = dv_acc[...].astype(bf16)
        dv_ref[...] = dv
        sum_ref[1:2, :] = jnp.sum(dv.astype(f32), 0, keepdims=True)


def attend_back(q, k, v, do_lo, lo_block, do_hi, hi_block, lse):
    rows, width = q.shape
    heads = width // HD
    half = rows // BLOCK // 2
    out = jax.ShapeDtypeStruct((rows, width), bf16)
    return pl.pallas_call(
        attend_back_kernel,
        grid=(rows // BLOCK,),
        in_specs=[
            rows_of(width),
            pl.BlockSpec((BLOCK, width), lambda i: (jnp.minimum(i, half - 1), lo_block)),
            pl.BlockSpec((BLOCK, width), lambda i: (jnp.maximum(i - half, 0), hi_block)),
            pl.BlockSpec((heads, BLOCK), lambda i: (0, i)),
            whole(k.shape),
            whole(v.shape),
        ],
        out_specs=[rows_of(width), whole(k.shape), whole(v.shape), whole((8, width))],
        out_shape=[out, out, out, jax.ShapeDtypeStruct((8, width), f32)],
        scratch_shapes=[pltpu.VMEM((rows, width), f32), pltpu.VMEM((rows, width), f32)],
        compiler_params=params(),
        name="attend_back",
    )(q, do_lo, do_hi, lse, k, v)


def pack_kernel(qkv_ref, out_ref, grad_ref, bias_ref, pack_ref):
    parts, rows, width = qkv_ref.shape
    for n in range(parts):
        pack_ref[n * rows : (n + 1) * rows, :] = qkv_ref[n]
    start = parts * rows
    for ref in (out_ref, grad_ref):
        for n in range(ref.shape[1] // width):
            pack_ref[start : start + width, :] = ref[:, n * width : (n + 1) * width]
            start += width
    pack_ref[start:, :] = bias_ref[...]


def pack(qkv, out, grad, bias):
    width = qkv.shape[2]
    rows = qkv.shape[0] * qkv.shape[1] + 2 * out.shape[1] + bias.shape[0]
    return pl.pallas_call(
        pack_kernel,
        out_shape=jax.ShapeDtypeStruct((rows, width), bf16),
        compiler_params=params(),
        name="pack",
    )(qkv, out, grad, bias)


def unpack_kernel(home_ref, mine_ref, got_ref, qkv_ref, both_ref, bias_ref):
    parts, rows, width = qkv_ref.shape
    first = home_ref[0] == 1
    pick = lambda start, size: jnp.where(
        first, mine_ref[start : start + size, :], got_ref[start : start + size, :]
    )
    for n in range(parts):
        qkv_ref[n] = pick(n * rows, rows)
    start = parts * rows
    for half in range(2):
        for n in range(both_ref.shape[2] // width):
            both_ref[half, :, n * width : (n + 1) * width] = pick(start, width)
            start += width
    bias_ref[...] = pick(start, bias_ref.shape[0])


def unpack(home, mine, got, parts, model, bias_rows):
    width = mine.shape[1]
    like = jax.ShapeDtypeStruct
    vmem = pl.BlockSpec(memory_space=pltpu.VMEM)
    return pl.pallas_call(
        unpack_kernel,
        in_specs=[pl.BlockSpec(memory_space=pltpu.SMEM), vmem, vmem],
        out_shape=[
            like((parts, model, width), bf16),
            like((2, width, model), bf16),
            like((bias_rows, width), bf16),
        ],
        compiler_params=params(),
        name="unpack",
    )(home, mine, got)


def middle_kernel(pieces_ref, w_ref, x_ref, bias_ref, scale_ref, gain_ref, shift_ref, sent_ref, a_ref, x1_ref):
    o = jnp.concatenate([pieces_ref[n] for n in range(pieces_ref.shape[0])], 1)
    w = jnp.concatenate([w_ref[n, 0] for n in range(w_ref.shape[0])], 0)
    a = dot_nn(o, w) + bias_ref[...]
    a_ref[...] = a
    x1 = x_ref[...].astype(f32) + scale_ref[...] * a
    x1_ref[...] = x1
    normed, _ = norm_pieces(x1)
    h = (normed * gain_ref[...] + shift_ref[...]).astype(bf16)
    for n in range(4):
        sent_ref[n] = h


def first_of_pairs(pairs):
    return pl.BlockSpec((pairs.shape[0], 1) + pairs.shape[2:], lambda i, *_: (0, 0, 0, 0))


def middle_rows(pieces, w, x, bias, scale, gain, shift):
    rows, model = x.shape
    like = jax.ShapeDtypeStruct
    return pl.pallas_call(
        middle_kernel,
        grid=(1,),
        in_specs=[whole(pieces.shape), first_of_pairs(w)]
        + [whole(v.shape) for v in (x, bias, scale, gain, shift)],
        out_specs=[whole((4, rows, model)), whole((rows, model)), whole((rows, model))],
        out_shape=[like((4, rows, model), bf16), like((rows, model), f32), like((rows, model), f32)],
        compiler_params=params(48),
        name="middle_rows",
    )(pieces, w, x, bias, scale, gain, shift)


def norm_back(upstream, normed, inv_dev, gain):
    scaled = upstream * gain
    return inv_dev * (
        scaled
        - jnp.mean(scaled, -1, keepdims=True)
        - normed * jnp.mean(scaled * normed, -1, keepdims=True)
    )


def norm_back_rows(upstream, values, gain):
    normed, inv_dev = norm_pieces(values)
    return normed, norm_back(upstream, normed, inv_dev, gain)


def middle_back_kernel(
    core_ref,
    got_ref,
    x1_ref,
    a_ref,
    gy_ref,
    gain_ref,
    scale_ref,
    bias_ref,
    w_ref,
    f_sum_ref,
    g1_ref,
    sent_ref,
    early_ref,
):
    total = lambda v: jnp.sum(v, 0, keepdims=True)
    dh2 = got_ref[0].astype(f32)
    for n in range(1, 4):
        dh2 = dh2 + got_ref[n].astype(f32)
    gy = gy_ref[0].astype(f32)
    normed, back = norm_back_rows(dh2, x1_ref[...], gain_ref[...])
    g1 = gy + back
    g1_ref[...] = g1
    da = (scale_ref[0:1, :] * g1).astype(bf16)
    w = jnp.concatenate([w_ref[n, 0] for n in range(w_ref.shape[0])], 0)
    do = dot_nt(da, w).astype(bf16)
    width = sent_ref.shape[2] - da.shape[1]
    first = core_ref[0] == 0
    half = da.shape[1] // 2
    piece = width // 2
    for n in range(4):
        low_part = do[:, n * piece : (n + 1) * piece]
        high_part = do[:, half + n * piece : half + (n + 1) * piece]
        sent_ref[n, :, : 2 * half] = da
        sent_ref[n, :, 2 * half : 2 * half + piece] = jnp.where(first, high_part, low_part)
        sent_ref[n, :, 2 * half + piece :] = jnp.where(first, low_part, high_part)
    early_ref[...] = jnp.zeros_like(early_ref)
    early_ref[2:3, :] = total(dh2 * normed)
    early_ref[3:4, :] = total(dh2)
    early_ref[4:5, :] = total(da.astype(f32))
    early_ref[5:6, :] = total((scale_ref[1:2, :] * gy).astype(bf16).astype(f32))
    early_ref[6:7, :] = total(g1 * a_ref[...])
    early_ref[7:8, :] = f_sum_ref[0:1, :] + bias_ref[...] * total(gy)


def middle_back(core, got, x1, a, gy, gain, scale, bias, w, f_sums, width):
    rows, model = x1.shape
    like = jax.ShapeDtypeStruct
    return pl.pallas_call(
        middle_back_kernel,
        grid_spec=pltpu.PrefetchScalarGridSpec(
            num_scalar_prefetch=1,
            grid=(1,),
            in_specs=[whole(v.shape) for v in (got, x1, a)]
            + [pl.BlockSpec((1,) + gy.shape[1:], lambda i, *_: (1, 0, 0))]
            + [whole(v.shape) for v in (gain, scale, bias)]
            + [first_of_pairs(w), whole(f_sums.shape)],
            out_specs=[
                whole((rows, model)),
                whole((4, rows, model + 2 * width)),
                whole((16, model)),
            ],
        ),
        out_shape=[
            like((rows, model), f32),
            like((4, rows, model + 2 * width), bf16),
            like((16, model), f32),
        ],
        compiler_params=params(48),
        name="middle_back",
    )(core, got, x1, a, gy, gain, scale, bias, w, f_sums)


def weight_kernel(h_ref, dq_ref, dk_ref, dv_ref, o_ref, da_lo_ref, da_hi_ref, out_ref, turned):
    @pl.when(pl.program_id(0) == 0)
    def _():
        for n, ref in enumerate((dq_ref, dk_ref, dv_ref, o_ref)):
            turned[n] = ref[...].T

    part = out_ref.shape[0] // 4
    for n in range(3):
        out_ref[n * part : (n + 1) * part, :] = dot_nn(turned[n], h_ref[...]).astype(bf16).T
    rows = da_lo_ref.shape[0]
    grad = dot_nn(turned[3, :, :rows], da_lo_ref[...]) + dot_nn(turned[3, :, rows:], da_hi_ref[...])
    width = out_ref.shape[1]
    for n in range(part // width):
        start = 3 * part + n * width
        out_ref[start : start + width, :] = grad[:, n * width : (n + 1) * width].astype(bf16)


def weight_grads(h, dq, dk, dv, o, da_lo, da_hi):
    rows, model = h.shape
    width = dq.shape[1]
    part = model // 4
    columns = lambda n: (0, n)
    return pl.pallas_call(
        weight_kernel,
        grid=(4,),
        in_specs=[pl.BlockSpec((rows, part), columns)]
        + [whole((rows, width))] * 4
        + [pl.BlockSpec((rows // 2, part), columns)] * 2,
        out_specs=pl.BlockSpec((4 * part, width), lambda n: (n, 0)),
        scratch_shapes=[pltpu.VMEM((4, width, rows), bf16)],
        out_shape=jax.ShapeDtypeStruct((16 * part, width), bf16),
        compiler_params=params(),
        name="weight_grads",
    )(h, dq, dk, dv, o, da_lo, da_hi)


def block_kernel(extra, here_ref, above_ref, below_ref, across_ref, out_ref):
    fine = here_ref.shape[0] - extra
    for n, ref in enumerate((here_ref, above_ref, across_ref, below_ref)):
        out_ref[n * fine : (n + 1) * fine, :] = ref[:fine, :]
    pair = lambda a, b: a[fine:, :].astype(f32) + b[fine:, :].astype(f32)
    total = pair(here_ref, across_ref) + pair(above_ref, below_ref)
    out_ref[4 * fine :, :] = total.astype(bf16)


def block_rows(extra, here, above, below, across):
    rows, width = here.shape
    return pl.pallas_call(
        functools.partial(block_kernel, extra),
        out_shape=jax.ShapeDtypeStruct((4 * (rows - extra) + extra, width), bf16),
        compiler_params=params(),
        name="block_rows",
    )(here, above, below, across)


def finish_kernel(place_ref, block_ref, other_ref, qkv_ref, out_ref):
    home = place_ref[0] == 1
    y = place_ref[1]
    parts, model, width = qkv_ref.shape
    part = model // 4
    fine = 2 * part
    for n in range(4):
        rows = slice(n * fine, (n + 1) * fine)
        mine, theirs = block_ref[rows, :].astype(f32), other_ref[rows, :].astype(f32)
        first, second = jnp.where(home, mine, theirs), jnp.where(home, theirs, mine)
        quarter = lax.rem(y + n, 4)
        at = pl.ds(pl.multiple_of(quarter * part, part), part)
        qkv_ref[0, at, :] = first[:part]
        qkv_ref[1, at, :] = first[part:]
        qkv_ref[2, at, :] = second[:part]
        for k in range(part // width):
            out_ref[quarter, :, k * width : (k + 1) * width] = second[
                part + k * width : part + (k + 1) * width
            ]


def finish(place, block, other, model):
    width = block.shape[1]
    like = jax.ShapeDtypeStruct
    vmem = pl.BlockSpec(memory_space=pltpu.VMEM)
    return pl.pallas_call(
        finish_kernel,
        in_specs=[pl.BlockSpec(memory_space=pltpu.SMEM), vmem, vmem],
        out_shape=[like((3, model, width), f32), like((4, width, model // 4), f32)],
        compiler_params=params(),
        name="finish",
    )(place, block, other)


def finish_hidden_kernel(home_ref, mine_ref, theirs_ref, one_ref, two_ref):
    home = home_ref[0] == 1
    half, width = mine_ref.shape[1:]
    model = one_ref.shape[0]
    for n in range(4):
        mine, theirs = mine_ref[n].astype(f32), theirs_ref[n].astype(f32)
        for k, rows in enumerate((jnp.where(home, mine, theirs), jnp.where(home, theirs, mine))):
            start = (2 * n + k) * half
            if start < model:
                one_ref[start : start + half, :] = rows
            else:
                column, row = divmod(start - model, width)
                two_ref[row : row + half, column * width : (column + 1) * width] = rows


def finish_hidden(home, mine, theirs, model):
    width = mine.shape[2]
    like = jax.ShapeDtypeStruct
    vmem = pl.BlockSpec(memory_space=pltpu.VMEM)
    return pl.pallas_call(
        finish_hidden_kernel,
        in_specs=[pl.BlockSpec(memory_space=pltpu.SMEM), vmem, vmem],
        out_shape=[like((model, width), f32), like((width, model), f32)],
        compiler_params=params(),
        name="finish_hidden",
    )(home, mine, theirs)


def join_kernel(lo_ref, f_lo_ref, got_ref, f_got_ref, out_ref):
    rows = out_ref.shape[1] // 2
    for n in range(4):
        block = slice(n * rows, (n + 1) * rows)
        for half, (one, two) in enumerate(((lo_ref, got_ref), (f_lo_ref, f_got_ref))):
            total = one[block, :].astype(f32) + two[block, :].astype(f32)
            out_ref[n, half * rows : (half + 1) * rows, :] = total.astype(bf16)


def join_rows(lo, f_lo, got, f_got):
    rows, model = lo.shape
    return pl.pallas_call(
        join_kernel,
        out_shape=jax.ShapeDtypeStruct((4, rows // 2, model), bf16),
        compiler_params=params(),
        name="join_rows",
    )(lo, f_lo, got, f_got)


def last_kernel(
    got_ref, x_ref, g1_ref, gain_ref, x1_ref, bias_ref, scale_ref, grad_ref, state_ref, sent_ref
):
    rows = x_ref.shape[0]
    total = got_ref[0].astype(f32)
    for n in range(1, 4):
        total = total + got_ref[n].astype(f32)
    _, back = norm_back_rows(total[:rows], x_ref[...].astype(f32), gain_ref[...])
    grad = g1_ref[...] + back
    state = x1_ref[...] + scale_ref[...] * (total[rows:] + bias_ref[...])
    grad_ref[...] = grad
    state_ref[...] = state
    sent_ref[:rows, :] = grad.astype(bf16)
    sent_ref[rows:, :] = state.astype(bf16)


def last_rows(got, x, g1, gain, x1, bias, scale):
    rows, model = x.shape
    like = jax.ShapeDtypeStruct
    return pl.pallas_call(
        last_kernel,
        out_shape=[
            like((rows, model), f32),
            like((rows, model), f32),
            like((2 * rows, model), bf16),
        ],
        compiler_params=params(),
        name="last_rows",
    )(got, x, g1, gain, x1, bias, scale)


def hidden_kernel(
    core_ref,
    h_lo_ref,
    h_hi_ref,
    g_ref,
    scale_ref,
    mine_ref,
    theirs_ref,
    b1_ref,
    h_ref,
    df_ref,
    m_ref,
    du_ref,
    lo_ref,
    hi_ref,
    f_lo_ref,
    f_hi_ref,
    du_sum_ref,
    f_sum_ref,
    w_ref,
):
    step = pl.program_id(0)
    model = h_lo_ref.shape[1]
    width = w_ref.shape[1]
    w1 = w_ref.at[:model]
    w2 = [w_ref.at[model + n : model + n + width] for n in range(0, model, width)]

    @pl.when(step == 0)
    def _():
        w_ref[...] = jnp.where(core_ref[1] == 1, mine_ref[...], theirs_ref[...])

    h = from_halves(h_lo_ref, h_hi_ref)
    h_ref[...] = h
    gy = jnp.concatenate([g_ref[n, 0] for n in range(g_ref.shape[0])], 0).astype(f32)
    df = (gy * scale_ref[...]).astype(bf16)
    df_ref[...] = df
    u = dot_nn(h, w1[...]) + b1_ref[...]
    phi = 0.5 * (1.0 + lax.erf(u * inv_root_two))
    m = (u * phi).astype(bf16)
    m_ref[...] = m
    dm = None
    for n, part in enumerate(w2):
        piece = dot_nt(df[:, n * width : (n + 1) * width], part[...])
        dm = piece if dm is None else dm + piece
    du = (dm * (phi + u * jnp.exp(-0.5 * u * u) * inv_root_two_pi)).astype(bf16)
    du_ref[...] = du
    to_halves(dot_nt(du, w1[...]).astype(bf16), lo_ref, hi_ref)
    f = jnp.concatenate([dot_nn(m, part[...]) for part in w2], 1)
    to_halves(f.astype(bf16), f_lo_ref, f_hi_ref)

    @pl.when(step == 0)
    def _():
        du_sum_ref[...] = jnp.zeros_like(du_sum_ref)
        f_sum_ref[...] = jnp.zeros_like(f_sum_ref)

    du_sum_ref[0:1, :] += jnp.sum(du.astype(f32), 0, keepdims=True)
    f_sum_ref[0:1, :] += jnp.sum(gy * f, 0, keepdims=True)


def hidden_block(core, h_lo, h_hi, g, scale, mine, theirs, b1):
    rows, model = 2 * h_lo.shape[0], h_lo.shape[1]
    width = mine.shape[1]
    blocks = rows // BLOCK
    each = BLOCK // g.shape[2]
    like = jax.ShapeDtypeStruct
    return pl.pallas_call(
        hidden_kernel,
        grid_spec=pltpu.PrefetchScalarGridSpec(
            num_scalar_prefetch=1,
            grid=(blocks,),
            in_specs=half_specs(model, blocks)
            + [
                pl.BlockSpec(
                    (each, 1) + g.shape[2:],
                    lambda i, core: ((i + core[0] * (blocks // 2)) % blocks, 1, 0, 0),
                ),
                whole((1, model)),
                whole(mine.shape),
                whole(mine.shape),
                whole((1, width)),
            ],
            out_specs=[
                rows_of(model),
                rows_in_order(model, blocks),
                rows_in_order(width, blocks),
                rows_of(width),
                whole((rows // 2, model)),
                whole((rows // 2, model)),
                whole((rows // 2, model)),
                whole((rows // 2, model)),
                whole((8, width)),
                whole((8, model)),
            ],
            scratch_shapes=[pltpu.VMEM(mine.shape, bf16)],
        ),
        out_shape=[
            like((rows, model), bf16),
            like((rows, model), bf16),
            like((rows, width), bf16),
            like((rows, width), bf16),
            like((rows // 2, model), bf16),
            like((rows // 2, model), bf16),
            like((rows // 2, model), bf16),
            like((rows // 2, model), bf16),
            like((8, width), f32),
            like((8, model), f32),
        ],
        compiler_params=params(40),
        name="hidden_block",
    )(core, h_lo, h_hi, g, scale, mine, theirs, b1)


def project_back_kernel(
    dq_ref, dk_ref, dv_ref, w_ref, x_lo_ref, x_hi_ref, early_ref, lo_ref, hi_ref, fold_ref, sum_ref
):
    step = pl.program_id(0)
    last = pl.num_programs(0) - 1
    dh = dot_nt(dq_ref[...], w_ref[0]) + dot_nt(dk_ref[...], w_ref[1]) + dot_nt(dv_ref[...], w_ref[2])
    normed, _ = norm_pieces(from_halves(x_lo_ref, x_hi_ref).astype(f32))

    @pl.when(step == 0)
    def _():
        sum_ref[...] = early_ref[...]

    to_halves(dh.astype(bf16), lo_ref, hi_ref)
    sum_ref[0:1, :] += jnp.sum(dh * normed, 0, keepdims=True)
    sum_ref[1:2, :] += jnp.sum(dh, 0, keepdims=True)

    @pl.when(step == last)
    def _():
        width = fold_ref.shape[1]
        for n in range(sum_ref.shape[1] // width):
            fold_ref[8 * n : 8 * n + 8, :] = sum_ref[0:8, n * width : (n + 1) * width]


def project_back(dq, dk, dv, w, x_lo, x_hi, early):
    rows, model = 2 * x_lo.shape[0], x_lo.shape[1]
    width = dq.shape[1]
    half = (rows // 2, model)
    folded = (8 * model // width, width)
    return pl.pallas_call(
        project_back_kernel,
        grid=(rows // BLOCK,),
        in_specs=[rows_of(width)] * 3
        + [whole(w.shape)]
        + half_specs(model, rows // BLOCK)
        + [whole((16, model))],
        out_specs=[whole(half), whole(half), whole(folded)],
        out_shape=[
            jax.ShapeDtypeStruct(half, bf16),
            jax.ShapeDtypeStruct(half, bf16),
            jax.ShapeDtypeStruct(folded, f32),
        ],
        scratch_shapes=[pltpu.VMEM((16, model), f32)],
        compiler_params=params(),
        name="project_back",
    )(dq, dk, dv, w, x_lo, x_hi, early)


AXES = ("dp", "tensor")


def members(key):
    found = {}
    for core in range(2):
        for z in range(4):
            for y in range(4):
                for xh in range(2):
                    for xl in range(2):
                        found.setdefault(key(xh, xl, y, z, core), []).append(
                            ((xl * 4 + y) * 2 + core) * 8 + xh * 4 + z
                        )
    return list(found.values())


def links(move):
    pairs = []
    for xh in range(2):
        for xl in range(2):
            for y in range(4):
                for z in range(4):
                    for core in range(2):
                        there = move(xh, xl, y, z, core)
                        if there is None:
                            continue
                        ph, pl_, py, pz, pc = there
                        pairs.append(
                            (
                                ((xl * 4 + y) * 2 + core) * 8 + xh * 4 + z,
                                ((pl_ * 4 + py % 4) * 2 + pc) * 8 + ph * 4 + pz % 4,
                            )
                        )
    return pairs


z_up = links(lambda xh, xl, y, z, c: (xh, xl, y, z + 1, c))
z_down = links(lambda xh, xl, y, z, c: (xh, xl, y, z - 1, c))
z_far = links(lambda xh, xl, y, z, c: (xh, xl, y, z + 2, c))
y_up = links(lambda xh, xl, y, z, c: (xh, xl, y + 1, z, c))
y_down = links(lambda xh, xl, y, z, c: (xh, xl, y - 1, z, c))
y_far = links(lambda xh, xl, y, z, c: (xh, xl, y + 2, z, c))
x_far = links(lambda xh, xl, y, z, c: (1 - xh, xl, y, z, c))
x_near = links(lambda xh, xl, y, z, c: (xh, 1 - xl, y, z, c))
cores = links(lambda xh, xl, y, z, c: (xh, xl, y, z, 1 - c))
regroup = links(lambda xh, xl, y, z, c: (c, xl, y, z, xh) if xh != c else None)
home = links(lambda xh, xl, y, z, c: (c, xl, y, z, c) if xh != c else None)
ring_z = members(lambda xh, xl, y, z, c: (xh, xl, y, c))
ring_y = members(lambda xh, xl, y, z, c: (xh, xl, z, c))
image = members(lambda xh, xl, y, z, c: (xh, xl, y))


def move(values, pairs):
    return lax.ppermute(values, AXES, pairs)


def exchange(values, groups):
    return lax.all_to_all(values, AXES, 0, 0, axis_index_groups=groups, tiled=True)


def gather(values, groups):
    return lax.all_gather(values, AXES, axis=0, axis_index_groups=groups, tiled=True)


def ring_from(values, up, down, far):
    return [values, move(values, down), move(values, up), move(values, far)]


def spread(rows):
    half = exchange(jnp.concatenate([rows] * 4, 0), ring_z)
    return half, move(half, cores)


def terms(values):
    first = lax.reduce_precision(values, 8, 7)
    rest = values - first
    second = lax.reduce_precision(rest, 8, 7)
    return low(jnp.concatenate([first, second, rest - second], 0))


def after(values, *others):
    return lax.optimization_barrier((values, *others))[0]


def wide(values):
    return values.astype(f32)


def low(values):
    return values.astype(bf16)


def turn(values, axis, start):
    return lax.dynamic_slice_in_dim(jnp.concatenate([values, values], axis), start % 4, 4, axis)


def unfold(values, rows):
    return jnp.concatenate([values[n : n + rows] for n in range(0, values.shape[0], rows)], 1)


def at_home(here, there, home_here):
    return jnp.where(home_here, here, there), jnp.where(home_here, there, here)


def shards(
    tokens,
    cotangent,
    w_qkv,
    qv_bias,
    w_out,
    w_fc1,
    b_fc1,
    w_fc2,
    norm_gain,
    norm_shift,
    out_bias,
    layer_scale,
):
    layer = 0
    place = lax.axis_index("dp")
    core = place % 2
    y = (place // 2) % 4
    x_hi = lax.axis_index("tensor") // 4
    z = lax.axis_index("tensor") % 4
    home_here = x_hi == core
    core_arg = core.astype(jnp.int32).reshape(1)
    home_arg = home_here.astype(jnp.int32).reshape(1)
    width = w_qkv.shape[3]
    hidden_here = w_fc1.shape[2]
    own, model = tokens.shape

    def regrouped(values):
        return jnp.where(home_here, values, move(values, regroup))

    rows_in = regrouped(tokens)
    bias_terms = terms(jnp.concatenate([qv_bias[layer].reshape(-1, width), b_fc1.reshape(-1, width)], 0))
    bias_rows = bias_terms.shape[0]
    bias_terms = jnp.pad(bias_terms, ((0, -bias_rows % 16), (0, 0)))
    first = pack(jnp.moveaxis(w_qkv[layer], 1, 0), w_out[layer], cotangent, bias_terms)
    first_got = move(after(first, rows_in), regroup)
    tokens_lo = exchange(jnp.concatenate([rows_in] * 4, 0), ring_z)
    fc_mine = jnp.concatenate(
        [w_fc1[layer], w_fc2[layer][:, :hidden_here], w_fc2[layer][:, hidden_here:]], 0
    )
    first_got, tokens_lo, fc_mine = lax.optimization_barrier((first_got, tokens_lo, fc_mine))
    tokens_hi = move(tokens_lo, cores)
    qkv_in, out_grad, biases = unpack(
        home_arg, first, first_got, 3, model, bias_terms.shape[0]
    )
    biases = jnp.sum(wide(biases[:bias_rows]).reshape(3, -1, width), 0)
    qv_in = biases[:2]
    hidden_bias = biases[2:].reshape(1, hidden_here)
    out_grad_full = gather(out_grad.reshape(2 * own, model), image).reshape(8, 2, own, model)

    normed_full, query_rows, key_rows, value_rows = project(
        tokens_lo, tokens_hi, norm_gain[layer, 0:1], norm_shift[layer, 0:1], qkv_in, qv_in
    )
    mixed, mixed_own, log_total = attend(core_arg, query_rows, key_rows, value_rows)
    pieces = exchange(mixed, image).reshape(8, own, width)
    fc_got = move(after(fc_mine, pieces), regroup)
    sent_two, branch, middle = middle_rows(
        pieces,
        out_grad_full,
        rows_in,
        out_bias[layer, 0:1],
        layer_scale[layer, 0:1],
        norm_gain[layer, 1:2],
        norm_shift[layer, 1:2],
    )
    two_lo = exchange(sent_two, ring_z).reshape(4 * own, model)
    two_hi = move(two_lo, cores)
    half = two_lo.shape[0]

    normed_two_full, down_full, hidden, act_grad, lo_two, hi_two, f_lo, f_hi, du_sums, f_sums = (
        hidden_block(
            jnp.concatenate([core_arg, home_arg]),
            two_lo,
            two_hi,
            out_grad_full,
            layer_scale[layer, 1:2],
            fc_mine,
            fc_got,
            hidden_bias,
        )
    )
    mine_two = low(wide(lo_two) + wide(move(hi_two, cores)))
    got_two = exchange(mine_two.reshape(4, own, model), ring_z)
    grad_b1 = du_sums[0]

    grad_fc2 = jnp.einsum("gf,gd->fd", hidden, down_full, preferred_element_type=f32)
    grad_fc1 = jnp.einsum("gd,gf->df", normed_two_full, act_grad, preferred_element_type=f32)
    joined = jnp.concatenate(
        [low(grad_fc1), low(grad_fc2[:, : model // 2]), low(grad_fc2[:, model // 2 :])], 0
    )
    joined, got_two = lax.optimization_barrier((joined, got_two))
    fc_quarter_y = lax.psum_scatter(
        joined, AXES, scatter_dimension=0, axis_index_groups=ring_y, tiled=True
    )
    gradient_two, sent, early = middle_back(
        core_arg,
        got_two,
        middle,
        branch,
        out_grad,
        norm_gain[layer, 1:2],
        layer_scale[layer],
        out_bias[layer, 1:2],
        out_grad_full,
        f_sums,
        width,
    )
    back_lo = exchange(sent, ring_z).reshape(4 * own, model + 2 * width)
    back_hi = move(back_lo[:, : model + width], cores)
    query_grad, key_grad, value_grad, qv_sums = attend_back(
        query_rows,
        key_rows,
        value_rows,
        back_lo,
        (model + width) // width,
        back_hi,
        model // width,
        log_total,
    )
    fc_quarter = low(wide(fc_quarter_y) + wide(move(fc_quarter_y, x_near)))
    query_grad, fc_quarter = lax.optimization_barrier((query_grad, fc_quarter))
    payload = weight_grads(
        normed_full, query_grad, key_grad, value_grad, mixed_own, back_lo, back_hi
    )
    query_grad = after(query_grad, payload)
    fc_quarter = low(wide(fc_quarter) + wide(move(fc_quarter, x_far)))
    lo, hi, small = project_back(
        query_grad, key_grad, value_grad, qkv_in, tokens_lo, tokens_hi, early
    )
    got = exchange(join_rows(lo, f_lo, move(hi, cores), move(f_hi, cores)), ring_z)

    quarter = payload.shape[0] // 4
    got_q = exchange(payload, ring_y)
    got_q, fc_quarter = lax.optimization_barrier((got_q, fc_quarter))
    rows_q = jnp.sum(wide(got_q).reshape(4, quarter, width), 0)
    wide_bias = jnp.concatenate(
        [qv_sums[:2].reshape(-1), grad_b1, jnp.zeros((model - 2 * width - hidden_here,), f32)]
    )
    wide_bias = jnp.concatenate([wide_bias, jnp.zeros_like(wide_bias)]).reshape(-1, width)
    flow = jnp.concatenate([low(rows_q), low(small), low(wide_bias)], 0)
    flow = low(wide(flow) + wide(move(flow, x_far)))
    fc_half = fc_quarter.shape[0] // 2
    fc_part = jnp.where(home_here, fc_quarter[:fc_half], move(fc_quarter[fc_half:], cores))
    flow = low(wide(flow) + wide(move(flow, x_near)))
    flow, fc_part = lax.optimization_barrier((flow, fc_part))
    fc_all = gather(fc_part, ring_y).reshape(4, fc_half, -1)
    fine = quarter // 2
    kept = jnp.where(home_here, flow[:fine], move(flow[fine:quarter], cores))
    sent_y = jnp.concatenate([kept, flow[quarter:]], 0)
    got_y = ring_from(sent_y, y_up, y_down, y_far)
    (here, above, below, across), got = lax.optimization_barrier((tuple(got_y), got))
    gradient_one, state_one, rows_sent = last_rows(
        got,
        rows_in,
        gradient_two,
        norm_gain[layer, 0:1],
        middle,
        out_bias[layer, 1:2],
        layer_scale[layer, 1:2],
    )
    rows_back = wide(move(rows_sent, regroup))
    gradient_out = jnp.where(home_here, gradient_one, rows_back[:own])
    state_out = jnp.where(home_here, state_one, rows_back[own:])
    extra = flow.shape[0] - quarter
    block = block_rows(extra, here, above, below, across)
    tail = block[4 * fine :]
    other = move(block, cores)
    small_rows = small.shape[0]
    small = low(wide(tail[:small_rows]) + wide(other[4 * fine : 4 * fine + small_rows]))
    small = jnp.sum(wide(exchange(jnp.concatenate([small] * 4, 0), ring_z)).reshape(4, -1, width), 0)
    small_total = unfold(small, 8)
    total_qkv, total_out = finish(
        jnp.concatenate([home_arg, y.astype(jnp.int32).reshape(1)]), block, other, model
    )
    total_qkv = jnp.moveaxis(total_qkv, 0, 1)
    total_out = jnp.moveaxis(total_out, 0, 1).reshape(width, model)
    total_fc1, total_fc2 = finish_hidden(home_arg, fc_all, move(fc_all, cores), model)
    bias_rows_mine = jnp.where(home_here, tail[small_rows:], other[4 * fine + small_rows :])
    bias_total = wide(bias_rows_mine).reshape(2, model)[:1]
    return (
        state_out,
        gradient_out,
        total_qkv[None],
        bias_total[:, : 2 * width].reshape(1, 2, width),
        total_out[None],
        total_fc1[None],
        bias_total[:, 2 * width : 2 * width + hidden_here],
        total_fc2[None],
        jnp.stack([small_total[0], small_total[2]])[None],
        jnp.stack([small_total[1], small_total[3]])[None],
        small_total[4:6][None],
        small_total[6:8][None],
    )


def solution(mesh):
    return jax.shard_map(
        shards,
        mesh=mesh,
        in_specs=(
            P(("dp", "tensor"), None),
            P(("dp", "tensor"), None),
            P(None, None, None, "tensor"),
            P(None, None, "tensor"),
            P(None, "tensor", None),
            P(None, None, "tensor"),
            P(None, "tensor"),
            P(None, "tensor", None),
            P(),
            P(),
            P(),
            P(),
        ),
        out_specs=(
            P(("dp", "tensor"), None),
            P(("dp", "tensor"), None),
            P(None, None, None, "tensor"),
            P(None, None, "tensor"),
            P(None, "tensor", None),
            P(None, None, "tensor"),
            P(None, "tensor"),
            P(None, "tensor", None),
            P(),
            P(),
            P(),
            P(),
        ),
        check_vma=False,
    )
```

time: 378 us -> 290 us (0.77)
  waiting for transfers between devices: 114 us -> 50.8 us
  starting transfers between devices: 89.8 us -> 65.8 us
  Pallas kernels: 30.5 us -> 53.9 us
  other arithmetic: 38.1 us -> 19.6 us
  blocking collectives: 38.4 us -> 50.1 us
  matrix products: 14.4 us -> 4.77 us
  local copies, waits for them, and re-layouts: 34.9 us -> 27.3 us
    ppermute x32 -> x21, waiting for transfers between devices: 83.2 us -> 21.4 us  [move(): return lax.ppermute(values, AXES, pairs)]
    ppermute x32 -> x21, starting transfers between devices: 74.1 us -> 45.2 us  [move(): return lax.ppermute(values, AXES, pairs)]
    pallas_call x2 -> x12, Pallas kernels: 11.7 us -> 33 us  [the longest x1 8.34 us: attend_back(): pl.pallas_call(attend_back_kernel, grid=(rows // BLOCK,), in_specs=[rows_...]
    all_to_all x2 -> x3, blocking collectives: 38.4 us -> 50.1 us  [exchange(): lax.all_to_all(values, AXES, 0, 0, axis_index_groups=groups, tiled=True)]
    slice x18 -> x8, local copies, waits for them, and re-layouts: 11.1 us -> 1.93 us  [the longest x1 1.1 us: shards(): back_hi = move(back_lo[:, :model + width], cores)]
    reduce_sum x11 -> x3, other arithmetic: 10.3 us -> 1.49 us  [the longest x1 1.47 us: shards(): rows_q = jnp.sum(wide(got_q).reshape(4, quarter, width), 0)]
    all_gather x3 -> x2, waiting for transfers between devices: 14.3 us -> 6.22 us  [gather(): lax.all_gather(values, AXES, axis=0, axis_index_groups=groups, tiled=True)]
    dot_general x4 -> x0, matrix products: 7.85 us -> none  [the longest x1 2.95 us: shards(): jnp.dot(mixed_own, out_full, preferred_element_type=f32)]
  transfers between devices with their start and end apart: 40 -> 29, of which waited for: 20 -> 15; matrix products, arithmetic and copies ran while one was open for 17% -> 11% of each run, Pallas kernels for 6% -> 13%
where the time goes in v1:
time: 290 us; the launch traced here: 287 us
  starting transfers between devices  65.8 us (23%)
  Pallas kernels  53.9 us (19%)
  waiting for transfers between devices  50.8 us (18%)
  blocking collectives  50.1 us (17%)
  local copies, waits for them, and re-layouts  27.3 us (9%)
  other arithmetic  19.6 us (7%)
  between operations  14.6 us (5%)
  matrix products  4.77 us (2%)
    all_to_all x3, blocking collectives, exchange(): lax.all_to_all(values, AXES, 0, 0, axis_index_groups=groups, tiled=True)  50.1 us
    ppermute x21, starting transfers between devices, move(): return lax.ppermute(values, AXES, pairs)  45.2 us
    ppermute x21, waiting for transfers between devices, move(): return lax.ppermute(values, AXES, pairs)  21.4 us
    all_to_all x5, starting transfers between devices, exchange(): lax.all_to_all(values, AXES, 0, 0, axis_index_groups=groups, tiled=True)  20.5 us
    all_to_all x5, waiting for transfers between devices, exchange(): lax.all_to_all(values, AXES, 0, 0, axis_index_groups=groups, tiled=True)  19.5 us
    unnamed x126, local copies, waits for them, and re-layouts  19.2 us
    pallas_call x1, Pallas kernels, hidden_block(): pl.pallas_call(hidden_kernel, grid_spec=pltpu.PrefetchScalarGridSpec(num_...  11 us
    pallas_call x1, Pallas kernels, attend_back(): pl.pallas_call(attend_back_kernel, grid=(rows // BLOCK,), in_specs=[rows_...  8.34 us
  transfers between devices with their start and end apart: 29, of which 15 were waited for; matrix products, arithmetic and copies ran while one was open for 11% of the time, Pallas kernels for 13%

profile of v1, /device:TPU:1, one launch (start us, length us, event | category | flops | bytes accessed | tf_op | source)
XLA Modules:
  0.0 286.9 jit_solution(4159424998095624683)
XLA Ops:
  7.2 6.0 %collective-permute-start = (bf16[128,1024]{1,0:T(8,128)(2,1)}, bf16[128,1024]{1,0:T(8,128)(2,1)S(1)}, u32[]{:S(2)}, u32[]{:S(2)}) collective-permute-start(bf16[128,1024]{1,0:T(8,128)(2,1)} %param.12), channel_id=1, source_target_pairs={{8,4},{9,5},{10,6},{11,7},{24,20},{25,21},{26,22},{27,23},{40,36},... | collective-permute-start | bytes 786440 | tf_op jit(solution)/shard_map/ppermute | solution.py:774
  18.3 4.4 %collective-permute-start.1 = (bf16[5152,128]{1,0:T(8,128)(2,1)}, bf16[5152,128]{1,0:T(8,128)(2,1)}, u32[]{:S(2)}, u32[]{:S(2)}) collective-permute-start(bf16[5152,128]{1,0:T(8,128)(2,1)} %pack.1.mine_ref), channel_id=1, source_target_pairs={{8,4},{9,5},{10,6},{11,7},{24,20},{25,21},{26,22},{27,23},{40,36},... | collective-permute-start | bytes 3956744 | tf_op jit(solution)/shard_map/ppermute | solution.py:774
  23.8 5.0 %all-to-all-start = ((bf16[4,128,1024]{2,1,0:T(8,128)(2,1)}), bf16[4,128,1024]{2,1,0:T(8,128)(2,1)S(1)}, u32[]{:S(2)}, u32[]{:S(2)}) async-start(bf16[4,128,1024]{2,1,0:T(8,128)(2,1)} %bitcast.5), calls=%async_computation | async-start | bytes 2097152 | tf_op jit(solution)/shard_map/all_to_all | solution.py:778
  28.9 2.7 pad_maximum_fusion.mine_ref
  31.6 7.0 %all-to-all-done = bf16[4,128,1024]{2,1,0:T(8,128)(2,1)S(1)} async-done(((bf16[4,128,1024]{2,1,0:T(8,128)(2,1)}), bf16[4,128,1024]{2,1,0:T(8,128)(2,1)S(1)}, u32[]{:S(2)}, u32[]{:S(2)}) %all-to-all-start) | async-done | bytes 1048608 | tf_op jit(solution)/shard_map/all_to_all | solution.py:778
  39.2 2.8 unpack.1
  44.9 3.5 %norm_project.1 = (bf16[1024,1024]{1,0:T(8,128)(2,1)S(1)}, bf16[1024,128]{1,0:T(8,128)(2,1)S(1)}, bf16[1024,128]{1,0:T(8,128)(2,1)S(1)}, bf16[1024,128]{1,0:T(8,128)(2,1)S(1)}) custom-call(bf16[512,1024]{1,0:T(8,128)(2,1)S(1)} %bitcast.71, bf16[512,1024]{1,0:T(8,128)(2,1)S(1)} %collective-permute-done.2.hi_ref.x_hi_ref, ...), custom_call_target="tpu_custom_call" | custom-call | tf_op jit(solution)/shard_map/norm_project/pallas_call | solution.py:86
  49.7 5.4 %attend.1 = (bf16[1024,128]{1,0:T(8,128)(2,1)S(1)}, bf16[1024,128]{1,0:T(8,128)(2,1)S(1)}, f32[2,1024]{1,0:T(2,128)S(1)}) custom-call(s32[1]{0:T(128)} %bitcast.12.core_ref, bf16[1024,128]{1,0:T(8,128)(2,1)S(1)} %get-tuple-element.77.q_ref, bf16[1024,128]{1,0:T(8,128)(2,1)S(1)} %get-tuple-element.78.k_ref, bf16[1024,128]{1,0:T(8,128)(2,1)S(1)} %get-tuple-element.79.v_ref), custom_call_target="tpu_custom_call" | custom-call | tf_op jit(solution)/shard_map/attend/pallas_call | solution.py:127
  55.1 13.9 %all_to_all.62.pieces_ref = bf16[8,128,128]{2,1,0:T(8,128)(2,1)S(1)} all-to-all(bf16[8,128,128]{2,1,0:T(8,128)(2,1)S(1)} %bitcast.81), channel_id=1, replica_groups={{0,1,2,3,8,9,10,11},{64,65,66,67,72,73,74,75},{4,5,6,7,12,13,14,15},{68..., dimensions={0} | all-to-all | bytes 524288 | tf_op jit(solution)/shard_map/all_to_all | solution.py:778
  69.0 4.0 %collective-permute-start.4 = (bf16[2048,512]{1,0:T(8,128)(2,1)}, bf16[2048,512]{1,0:T(8,128)(2,1)}, u32[]{:S(2)}, u32[]{:S(2)}) collective-permute-start(bf16[2048,512]{1,0:T(8,128)(2,1)} %pad_maximum_fusion.mine_ref), channel_id=1, source_target_pairs={{8,4},{9,5},{10,6},{11,7},{24,20},{25,21},{26,22},{27,23},{40,36},... | collective-permute-start | bytes 6291464 | tf_op jit(solution)/shard_map/ppermute | solution.py:774
  73.0 6.2 %all-gather.3.cloned.1.call-done = bf16[2048,1024]{1,0:T(8,128)(2,1)} async-done(((bf16[256,1024]{1,0:T(8,128)(2,1)}), bf16[2048,1024]{1,0:T(8,128)(2,1)}) %all-gather.3.cloned.1.call-update) | async-done | bytes 4194320 | tf_op jit(solution)/shard_map/all_gather | solution.py:782
  81.6 17.1 %all_to_all.63 = bf16[4,128,1024]{2,1,0:T(8,128)(2,1)S(1)} all-to-all(bf16[4,128,1024]{2,1,0:T(8,128)(2,1)S(1)} %get-tuple-element.82), channel_id=1, replica_groups={{0,1,2,3},{64,65,66,67},{4,5,6,7},{68,69,70,71},{16,17,18,19},{80,81,82..., dimensions={0} | all-to-all | bytes 2097152 | tf_op jit(solution)/shard_map/all_to_all | solution.py:778
  102.4 11.0 %hidden_block.1 = (bf16[1024,1024]{1,0:T(8,128)(2,1)S(1)}, bf16[1024,1024]{1,0:T(8,128)(2,1)S(1)}, bf16[1024,512]{1,0:T(8,128)(2,1)S(1)}, bf16[1024,512]{1,0:T(8...) custom-call(s32[2]{0:T(128)S(1)} %pad_add_fusion.core_ref, ...), custom_call_target="tpu_custom_call" | custom-call | tf_op jit(solution)/shard_map/hidden_block/pallas_call | solution.py:627
  118.5 3.5 %all-to-all-start.3 = ((bf16[4,128,1024]{2,1,0:T(8,128)(2,1)}), bf16[4,128,1024]{2,1,0:T(8,128)(2,1)S(1)}, u32[]{:S(2)}, u32[]{:S(2)}) async-start(bf16[4,128,1024]{2,1,0:T(8,128)(2,1)} %bitcast.87), calls=%async_computation.3 | async-start | bytes 2097152 | tf_op jit(solution)/shard_map/all_to_all | solution.py:778
  127.9 8.9 %all-to-all-done.3.got_ref = bf16[4,128,1024]{2,1,0:T(8,128)(2,1)S(1)} async-done(((bf16[4,128,1024]{2,1,0:T(8,128)(2,1)}), bf16[4,128,1024]{2,1,0:T(8,128)(2,1)S(1)}, u32[]{:S(2)}, u32[]{:S(2)}) %all-to-all-start.3) | async-done | bytes 1048608 | tf_op jit(solution)/shard_map/all_to_all | solution.py:778
  136.9 3.1 %middle_back.1 = (f32[128,1024]{1,0:T(8,128)S(1)}, bf16[4,128,1280]{2,1,0:T(8,128)(2,1)S(1)}, f32[16,1024]{1,0:T(8,128)S(1)}) custom-call(s32[1]{0:T(128)} %bitcast.12.core_ref, bf16[4,128,1024]{2,1,0:T(8,128)(2,1)S(1)} %all-to-all-done.3.got_ref, f32[128,1024]{1,0:T(8,128)S(1)} %get-tuple-element.92.x1_ref, f32[128,1024]{1,0:T(8,128)S(1)} %copy-done.37, ...), custom_call_target="tpu_custom_call" | custom-call | tf_op jit(solution)/shard_map/middle_back/pallas_call | solution.py:370
  140.6 19.2 %all_to_all.64 = bf16[4,128,1280]{2,1,0:T(8,128)(2,1)S(1)} all-to-all(bf16[4,128,1280]{2,1,0:T(8,128)(2,1)S(1)} %get-tuple-element.95), channel_id=1, replica_groups={{0,1,2,3},{64,65,66,67},{4,5,6,7},{68,69,70,71},{16,17,18,19},{80,81,82..., dimensions={0} | all-to-all | bytes 2621440 | tf_op jit(solution)/shard_map/all_to_all | solution.py:778
  162.9 3.6 %reduce-scatter.2.cloned.1.call-done = bf16[512,512]{1,0:T(8,128)(2,1)} async-done(((bf16[2048,512]{1,0:T(8,128)(2,1)}), bf16[512,512]{1,0:T(8,128)(2,1)}) %reduce-scatter.2.cloned.1.call-update) | async-done | bytes 524304 | tf_op jit(solution)/shard_map/reduce_scatter | solution.py:916
  171.3 8.3 %attend_back.1 = (bf16[1024,128]{1,0:T(8,128)(2,1)S(1)}, bf16[1024,128]{1,0:T(8,128)(2,1)S(1)}, bf16[1024,128]{1,0:T(8,128)(2,1)S(1)}, f32[8,128]{1,0:T(8,128)S(1)}) custom-call(bf16[1024,128]{1,0:T(8,128)(2,1)S(1)} %copy-done.19, bf16[512,1280]{1,0:T(8,128)(2,1)S(1)} %bitcast.68, bf16[512,1152]{1,0:T(8,128)(2,1)S(1)} %collective-permute-done.6.do_hi_ref.da_hi_ref, ...), custom_call_target="tpu_custom_call" | custom-call | tf_op jit(solution)/shard_map/attend_back/pallas_call | solution.py:201
  183.3 2.9 %weight_grads.1 = bf16[4096,128]{1,0:T(8,128)(2,1)S(1)} custom-call(bf16[1024,1024]{1,0:T(8,128)(2,1)S(1)} %copy-done.8, bf16[1024,128]{1,0:T(8,128)(2,1)S(1)} %get-tuple-element.105.dq_ref, bf16[1024,128]{1,0:T(8,128)(2,1)S(1)} %get-tuple-element.100.dk_ref, bf16[1024,128]{1,0:T(8,128)(2,1)S(1)} %get-tuple-element.101.dv_ref, ...), custom_call_target="tpu_custom_call" | custom-call | tf_op jit(solution)/shard_map/weight_grads/pallas_call | solution.py:417
  187.2 4.4 %all-to-all-start.5 = ((bf16[4,1024,128]{2,1,0:T(8,128)(2,1)}), bf16[4,1024,128]{2,1,0:T(8,128)(2,1)}, u32[]{:S(2)}, u32[]{:S(2)}) async-start(bf16[4,1024,128]{2,1,0:T(8,128)(2,1)} %bitcast.73), calls=%async_computation.6 | async-start | bytes 2097152 | tf_op jit(solution)/shard_map/all_to_all | solution.py:778
  197.0 4.6 %project_back.1 = (bf16[512,1024]{1,0:T(8,128)(2,1)S(1)}, bf16[512,1024]{1,0:T(8,128)(2,1)}, f32[64,128]{1,0:T(8,128)S(1)}) custom-call(bf16[1024,128]{1,0:T(8,128)(2,1)S(1)} %copy-done.12, bf16[1024,128]{1,0:T(8,128)(2,1)S(1)} %copy-done.14, bf16[1024,128]{1,0:T(8,128)(2,1)S(1)} %copy-done.16, bf16[3,1024,128]{2,1,0:T(8,128)(2,1)S(1)} %copy-done.6, ...), custom_call_target="tpu_custom_call" | custom-call | tf_op jit(solution)/shard_map/project_back/pallas_call | solution.py:702
  208.9 2.8 collective-permute-start.11
  214.7 3.0 %join_rows.1 = bf16[4,256,1024]{2,1,0:T(8,128)(2,1)} custom-call(bf16[512,1024]{1,0:T(8,128)(2,1)S(1)} %copy-done.27, bf16[512,1024]{1,0:T(8,128)(2,1)S(1)} %copy-done.25, bf16[512,1024]{1,0:T(8,128)(2,1)S(1)} %collective-permute-done.16.got_ref, bf16[512,1024]{1,0:T(8,128)(2,1)} %collective-permute-done.17.f_got_ref), custom_call_target="tpu_custom_call" | custom-call | tf_op jit(solution)/shard_map/join_rows/pallas_call | solution.py:523
  217.7 4.3 %all-to-all-start.6 = ((bf16[4,256,1024]{2,1,0:T(8,128)(2,1)}), bf16[4,256,1024]{2,1,0:T(8,128)(2,1)S(1)}, u32[]{:S(2)}, u32[]{:S(2)}) async-start(bf16[4,256,1024]{2,1,0:T(8,128)(2,1)} %join_rows.1), calls=%async_computation.7 | async-start | bytes 4194304 | tf_op jit(solution)/shard_map/all_to_all | solution.py:778
  225.0 3.5 %collective-permute-start.12 = (bf16[512,128]{1,0:T(8,128)(2,1)S(1)}, bf16[512,128]{1,0:T(8,128)(2,1)S(1)}, u32[]{:S(2)}, u32[]{:S(2)}) collective-permute-start(bf16[512,128]{1,0:T(8,128)(2,1)S(1)} %slice.176), channel_id=1, source_target_pairs={{0,8},{8,0},{1,9},{9,1},{2,10},{10,2},{3,11},{11,3},{16,24},{24,16... | collective-permute-start | bytes 393224 | tf_op jit(solution)/shard_map/ppermute | solution.py:774
  229.5 2.6 collective-permute-start.13
  235.0 4.0 %collective-permute-done.14.below_ref = bf16[592,128]{1,0:T(8,128)(2,1)S(1)} collective-permute-done((bf16[592,128]{1,0:T(8,128)(2,1)S(1)}, bf16[592,128]{1,0:T(8,128)(2,1)S(1)}, u32[]{:S(2)}, u32[]{:S(2)}) %collective-permute-start.14) | collective-permute-done | bytes 151584 | tf_op jit(solution)/shard_map/ppermute | solution.py:774
  240.5 3.5 %all-to-all-done.6.got_ref = bf16[4,256,1024]{2,1,0:T(8,128)(2,1)S(1)} async-done(((bf16[4,256,1024]{2,1,0:T(8,128)(2,1)}), bf16[4,256,1024]{2,1,0:T(8,128)(2,1)S(1)}, u32[]{:S(2)}, u32[]{:S(2)}) %all-to-all-start.6) | async-done | bytes 2097184 | tf_op jit(solution)/shard_map/all_to_all | solution.py:778
  248.3 8.9 %collective-permute-start.18 = (bf16[256,1024]{1,0:T(8,128)(2,1)}, bf16[256,1024]{1,0:T(8,128)(2,1)}, u32[]{:S(2)}, u32[]{:S(2)}) collective-permute-start(bf16[256,1024]{1,0:T(8,128)(2,1)} %get-tuple-element.119), channel_id=1, source_target_pairs={{8,4},{9,5},{10,6},{11,7},{24,20},{25,21},{26,22},{27,23},{40,36},... | collective-permute-start | bytes 1572872 | tf_op jit(solution)/shard_map/ppermute | solution.py:774
  258.0 6.4 %collective-permute-done.18 = bf16[256,1024]{1,0:T(8,128)(2,1)} collective-permute-done((bf16[256,1024]{1,0:T(8,128)(2,1)}, bf16[256,1024]{1,0:T(8,128)(2,1)}, u32[]{:S(2)}, u32[]{:S(2)}) %collective-permute-start.18) | collective-permute-done | bytes 524320 | tf_op jit(solution)/shard_map/ppermute | solution.py:774
  267.3 3.3 %all-to-all-start.7 = ((bf16[4,64,128]{2,1,0:T(8,128)(2,1)}), bf16[4,64,128]{2,1,0:T(8,128)(2,1)S(1)}, u32[]{:S(2)}, u32[]{:S(2)}) async-start(bf16[4,64,128]{2,1,0:T(8,128)(2,1)} %bitcast.42), calls=%async_computation.8 | async-start | bytes 131072 | tf_op jit(solution)/shard_map/all_to_all | solution.py:778
  (230 shorter events, 82.6 us)
Async XLA Ops:
  7.2 11.1 %collective-permute-start = (bf16[128,1024]{1,0:T(8,128)(2,1)}, bf16[128,1024]{1,0:T(8,128)(2,1)S(1)}, u32[]{:S(2)}, u32[]{:S(2)}) collective-permute-start(bf16[128,1024]{1,0:T(8,128)(2,1)} %param.12), channel_id=1, source_target_pairs={{8,4},{9,5},{10,6},{11,7},{24,20},{25,21},{26,22},{27,23},{40,36},... | collective-permute-start | bytes 786440 | tf_op jit(solution)/shard_map/ppermute | solution.py:774
  18.3 61.0 %copy-start.3 = (bf16[128,1024]{1,0:T(8,128)(2,1)}, bf16[128,1024]{1,0:T(8,128)(2,1)S(1)}, u32[]{:S(2)}) copy-start(bf16[128,1024]{1,0:T(8,128)(2,1)S(1)} %broadcast_select_fusion.x_ref) | copy-start | bytes 786436
  18.3 21.0 %collective-permute-start.1 = (bf16[5152,128]{1,0:T(8,128)(2,1)}, bf16[5152,128]{1,0:T(8,128)(2,1)}, u32[]{:S(2)}, u32[]{:S(2)}) collective-permute-start(bf16[5152,128]{1,0:T(8,128)(2,1)} %pack.1.mine_ref), channel_id=1, source_target_pairs={{8,4},{9,5},{10,6},{11,7},{24,20},{25,21},{26,22},{27,23},{40,36},... | collective-permute-start | bytes 3956744 | tf_op jit(solution)/shard_map/ppermute | solution.py:774
  23.8 14.8 %all-to-all-start = ((bf16[4,128,1024]{2,1,0:T(8,128)(2,1)}), bf16[4,128,1024]{2,1,0:T(8,128)(2,1)S(1)}, u32[]{:S(2)}, u32[]{:S(2)}) async-start(bf16[4,128,1024]{2,1,0:T(8,128)(2,1)} %bitcast.5), calls=%async_computation | async-start | bytes 2097152 | tf_op jit(solution)/shard_map/all_to_all | solution.py:778
  28.8 50.5 %all-gather.3.cloned.1.call-start = ((), (), s32[]{:S(2)}) async-start(), calls=%async_computation.9 | async-start | bytes 4718592 | tf_op jit(solution)/shard_map/all_gather | solution.py:782
  42.1 2.7 collective-permute-start.2
  69.0 31.2 %collective-permute-start.4 = (bf16[2048,512]{1,0:T(8,128)(2,1)}, bf16[2048,512]{1,0:T(8,128)(2,1)}, u32[]{:S(2)}, u32[]{:S(2)}) collective-permute-start(bf16[2048,512]{1,0:T(8,128)(2,1)} %pad_maximum_fusion.mine_ref), channel_id=1, source_target_pairs={{8,4},{9,5},{10,6},{11,7},{24,20},{25,21},{26,22},{27,23},{40,36},... | collective-permute-start | bytes 6291464 | tf_op jit(solution)/shard_map/ppermute | solution.py:774
  81.6 31.8 %copy-start.36 = (f32[128,1024]{1,0:T(8,128)}, f32[128,1024]{1,0:T(8,128)S(1)}, u32[]{:S(2)}) copy-start(f32[128,1024]{1,0:T(8,128)S(1)} %get-tuple-element.93.a_ref) | copy-start | bytes 1572868
  81.6 55.3 %copy-start.9 = (f32[128,1024]{1,0:T(8,128)}, f32[128,1024]{1,0:T(8,128)S(1)}, u32[]{:S(2)}) copy-start(f32[128,1024]{1,0:T(8,128)S(1)} %get-tuple-element.92.x1_ref) | copy-start | bytes 1572868
  98.7 3.7 %collective-permute-start.3 = (bf16[512,1024]{1,0:T(8,128)(2,1)S(1)}, bf16[512,1024]{1,0:T(8,128)(2,1)S(1)}, u32[]{:S(2)}, u32[]{:S(2)}) collective-permute-start(bf16[512,1024]{1,0:T(8,128)(2,1)S(1)} %bitcast.74), channel_id=1, source_target_pairs={{0,8},{8,0},{1,9},{9,1},{2,10},{10,2},{3,11},{11,3},{16,24},{24,16... | collective-permute-start | bytes 3145736 | tf_op jit(solution)/shard_map/ppermute | solution.py:774
  114.3 2.7 collective-permute-start.5
  118.5 18.3 %all-to-all-start.3 = ((bf16[4,128,1024]{2,1,0:T(8,128)(2,1)}), bf16[4,128,1024]{2,1,0:T(8,128)(2,1)S(1)}, u32[]{:S(2)}, u32[]{:S(2)}) async-start(bf16[4,128,1024]{2,1,0:T(8,128)(2,1)} %bitcast.87), calls=%async_computation.3 | async-start | bytes 2097152 | tf_op jit(solution)/shard_map/all_to_all | solution.py:778
  122.0 44.6 %reduce-scatter.2.cloned.1.call-start = ((), (), s32[]{:S(2)}) async-start(), calls=%async_computation.10 | async-start | bytes 2621440 | tf_op jit(solution)/shard_map/reduce_scatter | solution.py:916
  160.8 7.0 %collective-permute-start.6 = (bf16[512,1152]{1,0:T(8,128)(2,1)}, bf16[512,1152]{1,0:T(8,128)(2,1)S(1)}, u32[]{:S(2)}, u32[]{:S(2)}) collective-permute-start(bf16[512,1152]{1,0:T(8,128)(2,1)} %slice.208), channel_id=1, source_target_pairs={{0,8},{8,0},{1,9},{9,1},{2,10},{10,2},{3,11},{11,3},{16,24},{24,16... | collective-permute-start | bytes 3538952 | tf_op jit(solution)/shard_map/ppermute | solution.py:774
  166.6 13.1 %collective-permute-start.7 = (bf16[512,512]{1,0:T(8,128)(2,1)}, bf16[512,512]{1,0:T(8,128)(2,1)S(1)}, u32[]{:S(2)}, u32[]{:S(2)}) collective-permute-start(bf16[512,512]{1,0:T(8,128)(2,1)} %reduce-scatter.2.cloned.1.call-done), channel_id=1, source_target_pairs={{0,64},{8,72},{1,65},{9,73},{2,66},{10,74},{3,67},{11,75},{16,80},... | collective-permute-start | bytes 1572872 | tf_op jit(solution)/shard_map/ppermute | solution.py:774
  180.7 21.9 %collective-permute-start.8 = (bf16[512,512]{1,0:T(8,128)(2,1)}, bf16[512,512]{1,0:T(8,128)(2,1)}, u32[]{:S(2)}, u32[]{:S(2)}) collective-permute-start(bf16[512,512]{1,0:T(8,128)(2,1)} %add_convert_fusion.2), channel_id=1, source_target_pairs={{0,4},{8,12},{1,5},{9,13},{2,6},{10,14},{3,7},{11,15},{16,20},{24,... | collective-permute-start | bytes 1572872 | tf_op jit(solution)/shard_map/ppermute | solution.py:774
  187.2 17.8 %all-to-all-start.5 = ((bf16[4,1024,128]{2,1,0:T(8,128)(2,1)}), bf16[4,1024,128]{2,1,0:T(8,128)(2,1)}, u32[]{:S(2)}, u32[]{:S(2)}) async-start(bf16[4,1024,128]{2,1,0:T(8,128)(2,1)} %bitcast.73), calls=%async_computation.6 | async-start | bytes 2097152 | tf_op jit(solution)/shard_map/all_to_all | solution.py:778
  191.6 23.1 %collective-permute-start.17 = (bf16[512,1024]{1,0:T(8,128)(2,1)}, bf16[512,1024]{1,0:T(8,128)(2,1)}, u32[]{:S(2)}, u32[]{:S(2)}) collective-permute-start(bf16[512,1024]{1,0:T(8,128)(2,1)} %copy-done.50), channel_id=1, source_target_pairs={{0,8},{8,0},{1,9},{9,1},{2,10},{10,2},{3,11},{11,3},{16,24},{24,16... | collective-permute-start | bytes 3145736 | tf_op jit(solution)/shard_map/ppermute | solution.py:774
  202.6 12.1 %collective-permute-start.16 = (bf16[512,1024]{1,0:T(8,128)(2,1)}, bf16[512,1024]{1,0:T(8,128)(2,1)S(1)}, u32[]{:S(2)}, u32[]{:S(2)}) collective-permute-start(bf16[512,1024]{1,0:T(8,128)(2,1)} %get-tuple-element.114), channel_id=1, source_target_pairs={{0,8},{8,0},{1,9},{9,1},{2,10},{10,2},{3,11},{11,3},{16,24},{24,16... | collective-permute-start | bytes 3145736 | tf_op jit(solution)/shard_map/ppermute | solution.py:774
  206.5 7.0 %collective-permute-start.9 = (bf16[1104,128]{1,0:T(8,128)(2,1)S(1)}, bf16[1104,128]{1,0:T(8,128)(2,1)S(1)}, u32[]{:S(2)}, u32[]{:S(2)}) collective-permute-start(bf16[1104,128]{1,0:T(8,128)(2,1)S(1)} %pad_maximum_fusion.3), channel_id=1, source_target_pairs={{0,4},{8,12},{1,5},{9,13},{2,6},{10,14},{3,7},{11,15},{16,20},{24,... | collective-permute-start | bytes 847880 | tf_op jit(solution)/shard_map/ppermute | solution.py:774
  208.9 13.2 %collective-permute-start.11 = (bf16[256,512]{1,0:T(8,128)(2,1)}, bf16[256,512]{1,0:T(8,128)(2,1)}, u32[]{:S(2)}, u32[]{:S(2)}) collective-permute-start(bf16[256,512]{1,0:T(8,128)(2,1)} %slice.174), channel_id=1, source_target_pairs={{0,8},{8,0},{1,9},{9,1},{2,10},{10,2},{3,11},{11,3},{16,24},{24,16... | collective-permute-start | bytes 786440 | tf_op jit(solution)/shard_map/ppermute | solution.py:774
  214.3 9.5 %collective-permute-start.10 = (bf16[1104,128]{1,0:T(8,128)(2,1)}, bf16[1104,128]{1,0:T(8,128)(2,1)}, u32[]{:S(2)}, u32[]{:S(2)}) collective-permute-start(bf16[1104,128]{1,0:T(8,128)(2,1)} %add_convert_fusion.4), channel_id=1, source_target_pairs={{0,64},{8,72},{1,65},{9,73},{2,66},{10,74},{3,67},{11,75},{16,80},... | collective-permute-start | bytes 847880 | tf_op jit(solution)/shard_map/ppermute | solution.py:774
  217.7 26.3 %all-to-all-start.6 = ((bf16[4,256,1024]{2,1,0:T(8,128)(2,1)}), bf16[4,256,1024]{2,1,0:T(8,128)(2,1)S(1)}, u32[]{:S(2)}, u32[]{:S(2)}) async-start(bf16[4,256,1024]{2,1,0:T(8,128)(2,1)} %join_rows.1), calls=%async_computation.7 | async-start | bytes 4194304 | tf_op jit(solution)/shard_map/all_to_all | solution.py:778
  222.0 35.4 %all-gather.5.cloned.1.call-start = ((), (), s32[]{:S(2)}) async-start(), calls=%async_computation.11 | async-start | bytes 1310720 | tf_op jit(solution)/shard_map/all_gather | solution.py:782
  225.0 4.4 %collective-permute-start.12 = (bf16[512,128]{1,0:T(8,128)(2,1)S(1)}, bf16[512,128]{1,0:T(8,128)(2,1)S(1)}, u32[]{:S(2)}, u32[]{:S(2)}) collective-permute-start(bf16[512,128]{1,0:T(8,128)(2,1)S(1)} %slice.176), channel_id=1, source_target_pairs={{0,8},{8,0},{1,9},{9,1},{2,10},{10,2},{3,11},{11,3},{16,24},{24,16... | collective-permute-start | bytes 393224 | tf_op jit(solution)/shard_map/ppermute | solution.py:774
  229.5 5.6 %collective-permute-start.13 = (bf16[592,128]{1,0:T(8,128)(2,1)S(1)}, bf16[592,128]{1,0:T(8,128)(2,1)S(1)}, u32[]{:S(2)}, u32[]{:S(2)}) collective-permute-start(bf16[592,128]{1,0:T(8,128)(2,1)S(1)} %pad_maximum_fusion.4.here_ref), channel_id=1, source_target_pairs={{0,48},{8,56},{1,49},{9,57},{2,50},{10,58},{3,51},{11,59},{16,0},{... | collective-permute-start | bytes 454664 | tf_op jit(solution)/shard_map/ppermute | solution.py:774
  232.1 7.0 %collective-permute-start.14 = (bf16[592,128]{1,0:T(8,128)(2,1)S(1)}, bf16[592,128]{1,0:T(8,128)(2,1)S(1)}, u32[]{:S(2)}, u32[]{:S(2)}) collective-permute-start(bf16[592,128]{1,0:T(8,128)(2,1)S(1)} %pad_maximum_fusion.4.here_ref), channel_id=1, source_target_pairs={{0,16},{8,24},{1,17},{9,25},{2,18},{10,26},{3,19},{11,27},{16,32},... | collective-permute-start | bytes 454664 | tf_op jit(solution)/shard_map/ppermute | solution.py:774
  232.1 8.4 %collective-permute-start.15 = (bf16[592,128]{1,0:T(8,128)(2,1)S(1)}, bf16[592,128]{1,0:T(8,128)(2,1)S(1)}, u32[]{:S(2)}, u32[]{:S(2)}) collective-permute-start(bf16[592,128]{1,0:T(8,128)(2,1)S(1)} %pad_maximum_fusion.4.here_ref), channel_id=1, source_target_pairs={{0,32},{8,40},{1,33},{9,41},{2,34},{10,42},{3,35},{11,43},{16,48},... | collective-permute-start | bytes 454664 | tf_op jit(solution)/shard_map/ppermute | solution.py:774
  248.3 16.1 %collective-permute-start.18 = (bf16[256,1024]{1,0:T(8,128)(2,1)}, bf16[256,1024]{1,0:T(8,128)(2,1)}, u32[]{:S(2)}, u32[]{:S(2)}) collective-permute-start(bf16[256,1024]{1,0:T(8,128)(2,1)} %get-tuple-element.119), channel_id=1, source_target_pairs={{8,4},{9,5},{10,6},{11,7},{24,20},{25,21},{26,22},{27,23},{40,36},... | collective-permute-start | bytes 1572872 | tf_op jit(solution)/shard_map/ppermute | solution.py:774
  257.2 9.4 %collective-permute-start.19 = (bf16[2128,128]{1,0:T(8,128)(2,1)S(1)}, bf16[2128,128]{1,0:T(8,128)(2,1)S(1)}, u32[]{:S(2)}, u32[]{:S(2)}) collective-permute-start(bf16[2128,128]{1,0:T(8,128)(2,1)S(1)} %block_rows.1.block_ref), channel_id=1, source_target_pairs={{0,8},{8,0},{1,9},{9,1},{2,10},{10,2},{3,11},{11,3},{16,24},{24,16... | collective-permute-start | bytes 1634312 | tf_op jit(solution)/shard_map/ppermute | solution.py:774
  257.5 20.6 %collective-permute-start.20 = (bf16[4,256,512]{2,1,0:T(8,128)(2,1)}, bf16[4,256,512]{2,1,0:T(8,128)(2,1)S(1)}, u32[]{:S(2)}, u32[]{:S(2)}) collective-permute-start(bf16[4,256,512]{2,1,0:T(8,128)(2,1)} %bitcast.76), channel_id=1, source_target_pairs={{0,8},{8,0},{1,9},{9,1},{2,10},{10,2},{3,11},{11,3},{16,24},{24,16... | collective-permute-start | bytes 3145736 | tf_op jit(solution)/shard_map/ppermute | solution.py:774
  267.3 9.4 %all-to-all-start.7 = ((bf16[4,64,128]{2,1,0:T(8,128)(2,1)}), bf16[4,64,128]{2,1,0:T(8,128)(2,1)S(1)}, u32[]{:S(2)}, u32[]{:S(2)}) async-start(bf16[4,64,128]{2,1,0:T(8,128)(2,1)} %bitcast.42), calls=%async_computation.8 | async-start | bytes 131072 | tf_op jit(solution)/shard_map/all_to_all | solution.py:778
  (56 other events, 484.7 us)
Sparse Core Ops, SparseCore 0:
  42.2 36.9 all-gather.2
  137.0 29.5 reduce-scatter.1
  225.2 27.5 all-gather.4

commit v2 on v1

--- a/solution.py
+++ b/solution.py
@@ -463,9 +463,8 @@
         qkv_ref[1, at, :] = first[part:]
         qkv_ref[2, at, :] = second[:part]
         for k in range(part // width):
-            out_ref[quarter, :, k * width : (k + 1) * width] = second[
-                part + k * width : part + (k + 1) * width
-            ]
+            column = pl.multiple_of(quarter * part + k * width, width)
+            out_ref[:, pl.ds(column, width)] = second[part + k * width : part + (k + 1) * width]
 
 
 def finish(place, block, other, model):
@@ -475,7 +474,7 @@
     return pl.pallas_call(
         finish_kernel,
         in_specs=[pl.BlockSpec(memory_space=pltpu.SMEM), vmem, vmem],
-        out_shape=[like((3, model, width), f32), like((4, width, model // 4), f32)],
+        out_shape=[like((3, model, width), f32), like((width, model), f32)],
         compiler_params=params(),
         name="finish",
     )(place, block, other)
@@ -557,6 +556,24 @@
         compiler_params=params(),
         name="last_rows",
     )(got, x, g1, gain, x1, bias, scale)
+
+
+def settle_kernel(home_ref, grad_ref, state_ref, back_ref, grad_out_ref, state_out_ref):
+    home = home_ref[0] == 1
+    rows = grad_ref.shape[0]
+    grad_out_ref[...] = jnp.where(home, grad_ref[...], back_ref[:rows, :].astype(f32))
+    state_out_ref[...] = jnp.where(home, state_ref[...], back_ref[rows:, :].astype(f32))
+
+
+def settle(home, grad, state, back):
+    vmem = pl.BlockSpec(memory_space=pltpu.VMEM)
+    return pl.pallas_call(
+        settle_kernel,
+        in_specs=[pl.BlockSpec(memory_space=pltpu.SMEM)] + [vmem] * 3,
+        out_shape=[jax.ShapeDtypeStruct(grad.shape, f32)] * 2,
+        compiler_params=params(),
+        name="settle",
+    )(home, grad, state, back)
 
 
 def hidden_kernel(
@@ -943,19 +960,23 @@
     )
     fc_quarter = low(wide(fc_quarter_y) + wide(move(fc_quarter_y, x_near)))
     query_grad, fc_quarter = lax.optimization_barrier((query_grad, fc_quarter))
-    payload = weight_grads(
-        normed_full, query_grad, key_grad, value_grad, mixed_own, back_lo, back_hi
-    )
-    query_grad = after(query_grad, payload)
-    fc_quarter = low(wide(fc_quarter) + wide(move(fc_quarter, x_far)))
     lo, hi, small = project_back(
         query_grad, key_grad, value_grad, qkv_in, tokens_lo, tokens_hi, early
     )
-    got = exchange(join_rows(lo, f_lo, move(hi, cores), move(f_hi, cores)), ring_z)
+    small_here, small_above, small_below, small_across = [
+        wide(piece) for piece in ring_from(low(small), z_up, z_down, z_far)
+    ]
+    small = (small_here + small_across) + (small_above + small_below)
+    payload = weight_grads(
+        normed_full, after(query_grad, lo), key_grad, value_grad, mixed_own, back_lo, back_hi
+    )
+    fc_quarter = low(wide(fc_quarter) + wide(move(fc_quarter, x_far)))
+    rows_joined = join_rows(lo, f_lo, move(hi, cores), move(f_hi, cores))
 
     quarter = payload.shape[0] // 4
     got_q = exchange(payload, ring_y)
-    got_q, fc_quarter = lax.optimization_barrier((got_q, fc_quarter))
+    got_q, fc_quarter, rows_joined = lax.optimization_barrier((got_q, fc_quarter, rows_joined))
+    got = exchange(rows_joined, ring_z)
     rows_q = jnp.sum(wide(got_q).reshape(4, quarter, width), 0)
     wide_bias = jnp.concatenate(
         [qv_sums[:2].reshape(-1), grad_b1, jnp.zeros((model - 2 * width - hidden_here,), f32)]
@@ -971,8 +992,6 @@
     fine = quarter // 2
     kept = jnp.where(home_here, flow[:fine], move(flow[fine:quarter], cores))
     sent_y = jnp.concatenate([kept, flow[quarter:]], 0)
-    got_y = ring_from(sent_y, y_up, y_down, y_far)
-    (here, above, below, across), got = lax.optimization_barrier((tuple(got_y), got))
     gradient_one, state_one, rows_sent = last_rows(
         got,
         rows_in,
@@ -982,22 +1001,21 @@
         out_bias[layer, 1:2],
         layer_scale[layer, 1:2],
     )
-    rows_back = wide(move(rows_sent, regroup))
-    gradient_out = jnp.where(home_here, gradient_one, rows_back[:own])
-    state_out = jnp.where(home_here, state_one, rows_back[own:])
+    rows_back = move(rows_sent, regroup)
+    got_y = ring_from(sent_y, y_up, y_down, y_far)
+    (here, above, below, across), rows_back = lax.optimization_barrier((tuple(got_y), rows_back))
+    gradient_out, state_out = settle(home_arg, gradient_one, state_one, rows_back)
     extra = flow.shape[0] - quarter
     block = block_rows(extra, here, above, below, across)
     tail = block[4 * fine :]
     other = move(block, cores)
     small_rows = small.shape[0]
-    small = low(wide(tail[:small_rows]) + wide(other[4 * fine : 4 * fine + small_rows]))
-    small = jnp.sum(wide(exchange(jnp.concatenate([small] * 4, 0), ring_z)).reshape(4, -1, width), 0)
+    small = wide(tail[:small_rows]) + wide(other[4 * fine : 4 * fine + small_rows])
     small_total = unfold(small, 8)
     total_qkv, total_out = finish(
         jnp.concatenate([home_arg, y.astype(jnp.int32).reshape(1)]), block, other, model
     )
     total_qkv = jnp.moveaxis(total_qkv, 0, 1)
-    total_out = jnp.moveaxis(total_out, 0, 1).reshape(width, model)
     total_fc1, total_fc2 = finish_hidden(home_arg, fc_all, move(fc_all, cores), model)
     bias_rows_mine = jnp.where(home_here, tail[small_rows:], other[4 * fine + small_rows :])
     bias_total = wide(bias_rows_mine).reshape(2, model)[:1]

time: 290 us -> 286 us (0.986)
  waiting for transfers between devices: 50.8 us -> 61 us
  local copies, waits for them, and re-layouts: 27.3 us -> 21 us
  starting transfers between devices: 65.8 us -> 61.2 us
  other arithmetic: 19.6 us -> 16.2 us
    all_to_all x5 -> x4, waiting for transfers between devices: 19.5 us -> 27.4 us  [exchange(): lax.all_to_all(values, AXES, 0, 0, axis_index_groups=groups, tiled=True)]
    unnamed x126 -> x113, local copies, waits for them, and re-layouts: 19.2 us -> 13.4 us
    all_to_all x5 -> x4, starting transfers between devices: 20.5 us -> 16.5 us  [exchange(): lax.all_to_all(values, AXES, 0, 0, axis_index_groups=groups, tiled=True)]
    ppermute x21 -> x24, waiting for transfers between devices: 21.4 us -> 23.7 us  [move(): return lax.ppermute(values, AXES, pairs)]
    ppermute x21 -> x24, starting transfers between devices: 45.2 us -> 44.6 us  [move(): return lax.ppermute(values, AXES, pairs)]
  transfers between devices with their start and end apart: 29 -> 31, of which waited for: 15 -> 14; matrix products, arithmetic and copies ran while one was open for 11% -> 9% of each run, Pallas kernels for 13% -> 14%
where the time goes in v2:
time: 286 us; the launch traced here: 284 us
  starting transfers between devices  61.2 us (21%)
  waiting for transfers between devices  61 us (21%)
  Pallas kernels  55.6 us (19%)
  blocking collectives  50.1 us (18%)
  local copies, waits for them, and re-layouts  21 us (7%)
  other arithmetic  16.2 us (6%)
  between operations  14.5 us (5%)
  matrix products  4.77 us (2%)
    all_to_all x3, blocking collectives, exchange(): lax.all_to_all(values, AXES, 0, 0, axis_index_groups=groups, tiled=True)  50.1 us
    ppermute x24, starting transfers between devices, move(): return lax.ppermute(values, AXES, pairs)  44.6 us
    all_to_all x4, waiting for transfers between devices, exchange(): lax.all_to_all(values, AXES, 0, 0, axis_index_groups=groups, tiled=True)  27.4 us
    ppermute x24, waiting for transfers between devices, move(): return lax.ppermute(values, AXES, pairs)  23.7 us
    all_to_all x4, starting transfers between devices, exchange(): lax.all_to_all(values, AXES, 0, 0, axis_index_groups=groups, tiled=True)  16.5 us
    unnamed x113, local copies, waits for them, and re-layouts  13.4 us
    pallas_call x1, Pallas kernels, hidden_block(): pl.pallas_call(hidden_kernel, grid_spec=pltpu.PrefetchScalarGridSpec(num_...  11 us
    pallas_call x1, Pallas kernels, attend_back(): pl.pallas_call(attend_back_kernel, grid=(rows // BLOCK,), in_specs=[rows_...  8.37 us
  transfers between devices with their start and end apart: 31, of which 14 were waited for; matrix products, arithmetic and copies ran while one was open for 9% of the time, Pallas kernels for 14%

profile of v2, /device:TPU:1, one launch (start us, length us, event | category | flops | bytes accessed | tf_op | source)
XLA Modules:
  0.0 284.3 jit_solution(5629508434889836625)
XLA Ops:
  7.2 6.0 %collective-permute-start = (bf16[128,1024]{1,0:T(8,128)(2,1)}, bf16[128,1024]{1,0:T(8,128)(2,1)S(1)}, u32[]{:S(2)}, u32[]{:S(2)}) collective-permute-start(bf16[128,1024]{1,0:T(8,128)(2,1)} %param.12), channel_id=1, source_target_pairs={{8,4},{9,5},{10,6},{11,7},{24,20},{25,21},{26,22},{27,23},{40,36},... | collective-permute-start | bytes 786440 | tf_op jit(solution)/shard_map/ppermute | solution.py:791
  18.3 4.4 %collective-permute-start.1 = (bf16[5152,128]{1,0:T(8,128)(2,1)}, bf16[5152,128]{1,0:T(8,128)(2,1)}, u32[]{:S(2)}, u32[]{:S(2)}) collective-permute-start(bf16[5152,128]{1,0:T(8,128)(2,1)} %pack.1.mine_ref), channel_id=1, source_target_pairs={{8,4},{9,5},{10,6},{11,7},{24,20},{25,21},{26,22},{27,23},{40,36},... | collective-permute-start | bytes 3956744 | tf_op jit(solution)/shard_map/ppermute | solution.py:791
  23.8 5.2 %all-to-all-start = ((bf16[4,128,1024]{2,1,0:T(8,128)(2,1)}), bf16[4,128,1024]{2,1,0:T(8,128)(2,1)S(1)}, u32[]{:S(2)}, u32[]{:S(2)}) async-start(bf16[4,128,1024]{2,1,0:T(8,128)(2,1)} %bitcast.6), calls=%async_computation | async-start | bytes 2097152 | tf_op jit(solution)/shard_map/all_to_all | solution.py:795
  30.5 8.2 %all-to-all-done = bf16[4,128,1024]{2,1,0:T(8,128)(2,1)S(1)} async-done(((bf16[4,128,1024]{2,1,0:T(8,128)(2,1)}), bf16[4,128,1024]{2,1,0:T(8,128)(2,1)S(1)}, u32[]{:S(2)}, u32[]{:S(2)}) %all-to-all-start) | async-done | bytes 1048608 | tf_op jit(solution)/shard_map/all_to_all | solution.py:795
  39.2 2.8 %unpack.1 = (bf16[3,1024,128]{2,1,0:T(8,128)(2,1)S(1)}, bf16[2,128,1024]{2,1,0:T(8,128)(2,1)}, bf16[32,128]{1,0:T(8,128)(2,1)S(1)}) custom-call(s32[1]{0:T(128)} %bitcast.home_ref, bf16[5152,128]{1,0:T(8,128)(2,1)} %pack.1.mine_ref, bf16[5152,128]{1,0:T(8,128)(2,1)} %collective-permute-done.1.got_ref), custom_call_target="tpu_custom_call" | custom-call | tf_op jit(solution)/shard_map/unpack/pallas_call | solution.py:263
  42.3 2.5 collective-permute-done.2.hi_ref.x_hi_ref
  44.9 3.5 %norm_project.1 = (bf16[1024,1024]{1,0:T(8,128)(2,1)S(1)}, bf16[1024,128]{1,0:T(8,128)(2,1)S(1)}, bf16[1024,128]{1,0:T(8,128)(2,1)S(1)}, bf16[1024,128]{1,0:T(8,128)(2,1)S(1)}) custom-call(bf16[512,1024]{1,0:T(8,128)(2,1)S(1)} %bitcast.69, bf16[512,1024]{1,0:T(8,128)(2,1)S(1)} %collective-permute-done.2.hi_ref.x_hi_ref, ...), custom_call_target="tpu_custom_call" | custom-call | tf_op jit(solution)/shard_map/norm_project/pallas_call | solution.py:86
  49.7 5.4 %attend.1 = (bf16[1024,128]{1,0:T(8,128)(2,1)S(1)}, bf16[1024,128]{1,0:T(8,128)(2,1)S(1)}, f32[2,1024]{1,0:T(2,128)S(1)}) custom-call(s32[1]{0:T(128)} %bitcast.12.core_ref, bf16[1024,128]{1,0:T(8,128)(2,1)S(1)} %get-tuple-element.80.q_ref, bf16[1024,128]{1,0:T(8,128)(2,1)S(1)} %get-tuple-element.81.k_ref, bf16[1024,128]{1,0:T(8,128)(2,1)S(1)} %get-tuple-element.82.v_ref), custom_call_target="tpu_custom_call" | custom-call | tf_op jit(solution)/shard_map/attend/pallas_call | solution.py:127
  55.1 13.9 %all_to_all.53.pieces_ref = bf16[8,128,128]{2,1,0:T(8,128)(2,1)S(1)} all-to-all(bf16[8,128,128]{2,1,0:T(8,128)(2,1)S(1)} %bitcast.77), channel_id=1, replica_groups={{0,1,2,3,8,9,10,11},{64,65,66,67,72,73,74,75},{4,5,6,7,12,13,14,15},{68..., dimensions={0} | all-to-all | bytes 524288 | tf_op jit(solution)/shard_map/all_to_all | solution.py:795
  69.0 3.9 %collective-permute-start.4 = (bf16[2048,512]{1,0:T(8,128)(2,1)}, bf16[2048,512]{1,0:T(8,128)(2,1)}, u32[]{:S(2)}, u32[]{:S(2)}) collective-permute-start(bf16[2048,512]{1,0:T(8,128)(2,1)} %pad_maximum_fusion.mine_ref), channel_id=1, source_target_pairs={{8,4},{9,5},{10,6},{11,7},{24,20},{25,21},{26,22},{27,23},{40,36},... | collective-permute-start | bytes 6291464 | tf_op jit(solution)/shard_map/ppermute | solution.py:791
  73.0 6.2 %all-gather.3.cloned.1.call-done = bf16[2048,1024]{1,0:T(8,128)(2,1)} async-done(((bf16[256,1024]{1,0:T(8,128)(2,1)}), bf16[2048,1024]{1,0:T(8,128)(2,1)}) %all-gather.3.cloned.1.call-update) | async-done | bytes 4194320 | tf_op jit(solution)/shard_map/all_gather | solution.py:799
  81.6 17.1 %all_to_all.54 = bf16[4,128,1024]{2,1,0:T(8,128)(2,1)S(1)} all-to-all(bf16[4,128,1024]{2,1,0:T(8,128)(2,1)S(1)} %get-tuple-element.85), channel_id=1, replica_groups={{0,1,2,3},{64,65,66,67},{4,5,6,7},{68,69,70,71},{16,17,18,19},{80,81,82..., dimensions={0} | all-to-all | bytes 2097152 | tf_op jit(solution)/shard_map/all_to_all | solution.py:795
  102.4 11.0 %hidden_block.1 = (bf16[1024,1024]{1,0:T(8,128)(2,1)S(1)}, bf16[1024,1024]{1,0:T(8,128)(2,1)S(1)}, bf16[1024,512]{1,0:T(8,128)(2,1)S(1)}, bf16[1024,512]{1,0:T(8...) custom-call(s32[2]{0:T(128)S(1)} %pad_add_fusion.core_ref, ...), custom_call_target="tpu_custom_call" | custom-call | tf_op jit(solution)/shard_map/hidden_block/pallas_call | solution.py:644
  118.5 3.5 %all-to-all-start.3 = ((bf16[4,128,1024]{2,1,0:T(8,128)(2,1)}), bf16[4,128,1024]{2,1,0:T(8,128)(2,1)S(1)}, u32[]{:S(2)}, u32[]{:S(2)}) async-start(bf16[4,128,1024]{2,1,0:T(8,128)(2,1)} %bitcast.83), calls=%async_computation.3 | async-start | bytes 2097152 | tf_op jit(solution)/shard_map/all_to_all | solution.py:795
  128.0 8.9 %all-to-all-done.3.got_ref = bf16[4,128,1024]{2,1,0:T(8,128)(2,1)S(1)} async-done(((bf16[4,128,1024]{2,1,0:T(8,128)(2,1)}), bf16[4,128,1024]{2,1,0:T(8,128)(2,1)S(1)}, u32[]{:S(2)}, u32[]{:S(2)}) %all-to-all-start.3) | async-done | bytes 1048608 | tf_op jit(solution)/shard_map/all_to_all | solution.py:795
  136.9 3.1 %middle_back.1 = (f32[128,1024]{1,0:T(8,128)S(1)}, bf16[4,128,1280]{2,1,0:T(8,128)(2,1)S(1)}, f32[16,1024]{1,0:T(8,128)S(1)}) custom-call(s32[1]{0:T(128)} %bitcast.12.core_ref, bf16[4,128,1024]{2,1,0:T(8,128)(2,1)S(1)} %all-to-all-done.3.got_ref, f32[128,1024]{1,0:T(8,128)S(1)} %get-tuple-element.95.x1_ref, f32[128,1024]{1,0:T(8,128)S(1)} %copy-done.27, ...), custom_call_target="tpu_custom_call" | custom-call | tf_op jit(solution)/shard_map/middle_back/pallas_call | solution.py:370
  140.6 19.2 %all_to_all.55 = bf16[4,128,1280]{2,1,0:T(8,128)(2,1)S(1)} all-to-all(bf16[4,128,1280]{2,1,0:T(8,128)(2,1)S(1)} %get-tuple-element.98), channel_id=1, replica_groups={{0,1,2,3},{64,65,66,67},{4,5,6,7},{68,69,70,71},{16,17,18,19},{80,81,82..., dimensions={0} | all-to-all | bytes 2621440 | tf_op jit(solution)/shard_map/all_to_all | solution.py:795
  163.0 3.7 %reduce-scatter.2.cloned.1.call-done = bf16[512,512]{1,0:T(8,128)(2,1)} async-done(((bf16[2048,512]{1,0:T(8,128)(2,1)}), bf16[512,512]{1,0:T(8,128)(2,1)}) %reduce-scatter.2.cloned.1.call-update) | async-done | bytes 524304 | tf_op jit(solution)/shard_map/reduce_scatter | solution.py:933
  172.3 8.4 %attend_back.1 = (bf16[1024,128]{1,0:T(8,128)(2,1)S(1)}, bf16[1024,128]{1,0:T(8,128)(2,1)S(1)}, bf16[1024,128]{1,0:T(8,128)(2,1)S(1)}, f32[8,128]{1,0:T(8,128)S(1)}) custom-call(bf16[1024,128]{1,0:T(8,128)(2,1)S(1)} %copy-done.12, bf16[512,1280]{1,0:T(8,128)(2,1)S(1)} %bitcast.66, bf16[512,1152]{1,0:T(8,128)(2,1)S(1)} %collective-permute-done.6.do_hi_ref.da_hi_ref, ...), custom_call_target="tpu_custom_call" | custom-call | tf_op jit(solution)/shard_map/attend_back/pallas_call | solution.py:201
  181.7 4.6 %project_back.1 = (bf16[512,1024]{1,0:T(8,128)(2,1)S(1)}, bf16[512,1024]{1,0:T(8,128)(2,1)}, f32[64,128]{1,0:T(8,128)S(1)}) custom-call(bf16[1024,128]{1,0:T(8,128)(2,1)S(1)} %get-tuple-element.107.dq_ref, bf16[1024,128]{1,0:T(8,128)(2,1)S(1)} %get-tuple-element.103.dk_ref, bf16[1024,128]{1,0:T(8,128)(2,1)S(1)} %get-tuple-element.104.dv_ref, ...), custom_call_target="tpu_custom_call" | custom-call | tf_op jit(solution)/shard_map/project_back/pallas_call | solution.py:719
  188.1 3.7 %weight_grads.1 = bf16[4096,128]{1,0:T(8,128)(2,1)} custom-call(bf16[1024,1024]{1,0:T(8,128)(2,1)S(1)} %copy-done.7, bf16[1024,128]{1,0:T(8,128)(2,1)S(1)} %get-tuple-element.107.dq_ref, bf16[1024,128]{1,0:T(8,128)(2,1)S(1)} %get-tuple-element.103.dk_ref, bf16[1024,128]{1,0:T(8,128)(2,1)S(1)} %get-tuple-element.104.dv_ref, bf16[1024,128]{1,0:T(8,128)(2,1)S(1)} %copy-done.31, ...), custom_call_target="tpu_custom_call" | custom-call | tf_op jit(solution)/shard_map/weight_grads/pallas_call | solution.py:417
  191.8 3.7 %all-to-all-start.5 = ((bf16[4,1024,128]{2,1,0:T(8,128)(2,1)}), bf16[4,1024,128]{2,1,0:T(8,128)(2,1)S(1)}, u32[]{:S(2)}, u32[]{:S(2)}) async-start(bf16[4,1024,128]{2,1,0:T(8,128)(2,1)} %bitcast.27), calls=%async_computation.6 | async-start | bytes 2097152 | tf_op jit(solution)/shard_map/all_to_all | solution.py:795
  195.5 2.8 collective-permute-start.8
  204.8 2.7 collective-permute-done.11
  207.5 3.2 %collective-permute-done.8 = bf16[512,512]{1,0:T(8,128)(2,1)S(1)} collective-permute-done((bf16[512,512]{1,0:T(8,128)(2,1)}, bf16[512,512]{1,0:T(8,128)(2,1)S(1)}, u32[]{:S(2)}, u32[]{:S(2)}) %collective-permute-start.8) | collective-permute-done | bytes 524320 | tf_op jit(solution)/shard_map/ppermute | solution.py:791
  212.7 3.3 %join_rows.1 = bf16[4,256,1024]{2,1,0:T(8,128)(2,1)} custom-call(bf16[512,1024]{1,0:T(8,128)(2,1)S(1)} %copy-done.20, bf16[512,1024]{1,0:T(8,128)(2,1)S(1)} %copy-done.18, bf16[512,1024]{1,0:T(8,128)(2,1)} %collective-permute-done.9.got_ref, bf16[512,1024]{1,0:T(8,128)(2,1)} %collective-permute-done.10.f_got_ref), custom_call_target="tpu_custom_call" | custom-call | tf_op jit(solution)/shard_map/join_rows/pallas_call | solution.py:522
  216.4 2.8 collective-permute-start.14
  219.2 4.1 %all-to-all-start.6 = ((bf16[4,256,1024]{2,1,0:T(8,128)(2,1)}), bf16[4,256,1024]{2,1,0:T(8,128)(2,1)S(1)}, u32[]{:S(2)}, u32[]{:S(2)}) async-start(bf16[4,256,1024]{2,1,0:T(8,128)(2,1)} %join_rows.1), calls=%async_computation.7 | async-start | bytes 4194304 | tf_op jit(solution)/shard_map/all_to_all | solution.py:795
  229.6 4.4 %collective-permute-done.15 = bf16[1104,128]{1,0:T(8,128)(2,1)} collective-permute-done((bf16[1104,128]{1,0:T(8,128)(2,1)S(1)}, bf16[1104,128]{1,0:T(8,128)(2,1)}, u32[]{:S(2)}, u32[]{:S(2)}) %collective-permute-start.15) | collective-permute-done | bytes 282656 | tf_op jit(solution)/shard_map/ppermute | solution.py:791
  238.1 10.3 %all-to-all-done.6.got_ref = bf16[4,256,1024]{2,1,0:T(8,128)(2,1)S(1)} async-done(((bf16[4,256,1024]{2,1,0:T(8,128)(2,1)}), bf16[4,256,1024]{2,1,0:T(8,128)(2,1)S(1)}, u32[]{:S(2)}, u32[]{:S(2)}) %all-to-all-start.6) | async-done | bytes 2097184 | tf_op jit(solution)/shard_map/all_to_all | solution.py:795
  250.3 4.3 %collective-permute-start.21 = (bf16[256,1024]{1,0:T(8,128)(2,1)S(1)}, bf16[256,1024]{1,0:T(8,128)(2,1)S(1)}, u32[]{:S(2)}, u32[]{:S(2)}) collective-permute-start(bf16[256,1024]{1,0:T(8,128)(2,1)S(1)} %get-tuple-element.123), channel_id=1, source_target_pairs={{8,4},{9,5},{10,6},{11,7},{24,20},{25,21},{26,22},{27,23},{40,36},... | collective-permute-start | bytes 1572872 | tf_op jit(solution)/shard_map/ppermute | solution.py:791
  259.7 5.3 %collective-permute-done.18.above_ref = bf16[592,128]{1,0:T(8,128)(2,1)S(1)} collective-permute-done((bf16[592,128]{1,0:T(8,128)(2,1)S(1)}, bf16[592,128]{1,0:T(8,128)(2,1)S(1)}, u32[]{:S(2)}, u32[]{:S(2)}) %collective-permute-start.18) | collective-permute-done | bytes 151584 | tf_op jit(solution)/shard_map/ppermute | solution.py:791
  (219 shorter events, 77.7 us)
Async XLA Ops:
  7.2 11.1 %collective-permute-start = (bf16[128,1024]{1,0:T(8,128)(2,1)}, bf16[128,1024]{1,0:T(8,128)(2,1)S(1)}, u32[]{:S(2)}, u32[]{:S(2)}) collective-permute-start(bf16[128,1024]{1,0:T(8,128)(2,1)} %param.12), channel_id=1, source_target_pairs={{8,4},{9,5},{10,6},{11,7},{24,20},{25,21},{26,22},{27,23},{40,36},... | collective-permute-start | bytes 786440 | tf_op jit(solution)/shard_map/ppermute | solution.py:791
  18.3 61.0 %copy-start.2 = (bf16[128,1024]{1,0:T(8,128)(2,1)}, bf16[128,1024]{1,0:T(8,128)(2,1)S(1)}, u32[]{:S(2)}) copy-start(bf16[128,1024]{1,0:T(8,128)(2,1)S(1)} %broadcast_select_fusion.x_ref) | copy-start | bytes 786436
  18.3 21.0 %collective-permute-start.1 = (bf16[5152,128]{1,0:T(8,128)(2,1)}, bf16[5152,128]{1,0:T(8,128)(2,1)}, u32[]{:S(2)}, u32[]{:S(2)}) collective-permute-start(bf16[5152,128]{1,0:T(8,128)(2,1)} %pack.1.mine_ref), channel_id=1, source_target_pairs={{8,4},{9,5},{10,6},{11,7},{24,20},{25,21},{26,22},{27,23},{40,36},... | collective-permute-start | bytes 3956744 | tf_op jit(solution)/shard_map/ppermute | solution.py:791
  23.8 14.9 %all-to-all-start = ((bf16[4,128,1024]{2,1,0:T(8,128)(2,1)}), bf16[4,128,1024]{2,1,0:T(8,128)(2,1)S(1)}, u32[]{:S(2)}, u32[]{:S(2)}) async-start(bf16[4,128,1024]{2,1,0:T(8,128)(2,1)} %bitcast.6), calls=%async_computation | async-start | bytes 2097152 | tf_op jit(solution)/shard_map/all_to_all | solution.py:795
  28.9 50.3 %all-gather.3.cloned.1.call-start = ((), (), s32[]{:S(2)}) async-start(), calls=%async_computation.8 | async-start | bytes 4718592 | tf_op jit(solution)/shard_map/all_gather | solution.py:799
  42.1 2.7 collective-permute-start.2
  69.0 31.2 %collective-permute-start.4 = (bf16[2048,512]{1,0:T(8,128)(2,1)}, bf16[2048,512]{1,0:T(8,128)(2,1)}, u32[]{:S(2)}, u32[]{:S(2)}) collective-permute-start(bf16[2048,512]{1,0:T(8,128)(2,1)} %pad_maximum_fusion.mine_ref), channel_id=1, source_target_pairs={{8,4},{9,5},{10,6},{11,7},{24,20},{25,21},{26,22},{27,23},{40,36},... | collective-permute-start | bytes 6291464 | tf_op jit(solution)/shard_map/ppermute | solution.py:791
  98.7 3.7 %collective-permute-start.3 = (bf16[512,1024]{1,0:T(8,128)(2,1)S(1)}, bf16[512,1024]{1,0:T(8,128)(2,1)S(1)}, u32[]{:S(2)}, u32[]{:S(2)}) collective-permute-start(bf16[512,1024]{1,0:T(8,128)(2,1)S(1)} %bitcast.71), channel_id=1, source_target_pairs={{0,8},{8,0},{1,9},{9,1},{2,10},{10,2},{3,11},{11,3},{16,24},{24,16... | collective-permute-start | bytes 3145736 | tf_op jit(solution)/shard_map/ppermute | solution.py:791
  114.4 2.7 collective-permute-start.5
  118.5 18.3 %all-to-all-start.3 = ((bf16[4,128,1024]{2,1,0:T(8,128)(2,1)}), bf16[4,128,1024]{2,1,0:T(8,128)(2,1)S(1)}, u32[]{:S(2)}, u32[]{:S(2)}) async-start(bf16[4,128,1024]{2,1,0:T(8,128)(2,1)} %bitcast.83), calls=%async_computation.3 | async-start | bytes 2097152 | tf_op jit(solution)/shard_map/all_to_all | solution.py:795
  122.0 44.6 %reduce-scatter.2.cloned.1.call-start = ((), (), s32[]{:S(2)}) async-start(), calls=%async_computation.9 | async-start | bytes 2621440 | tf_op jit(solution)/shard_map/reduce_scatter | solution.py:933
  160.8 7.9 %collective-permute-start.6 = (bf16[512,1152]{1,0:T(8,128)(2,1)}, bf16[512,1152]{1,0:T(8,128)(2,1)S(1)}, u32[]{:S(2)}, u32[]{:S(2)}) collective-permute-start(bf16[512,1152]{1,0:T(8,128)(2,1)} %slice.200), channel_id=1, source_target_pairs={{0,8},{8,0},{1,9},{9,1},{2,10},{10,2},{3,11},{11,3},{16,24},{24,16... | collective-permute-start | bytes 3538952 | tf_op jit(solution)/shard_map/ppermute | solution.py:791
  166.6 14.1 %collective-permute-start.7 = (bf16[512,512]{1,0:T(8,128)(2,1)}, bf16[512,512]{1,0:T(8,128)(2,1)S(1)}, u32[]{:S(2)}, u32[]{:S(2)}) collective-permute-start(bf16[512,512]{1,0:T(8,128)(2,1)} %reduce-scatter.2.cloned.1.call-done), channel_id=1, source_target_pairs={{0,64},{8,72},{1,65},{9,73},{2,66},{10,74},{3,67},{11,75},{16,80},... | collective-permute-start | bytes 1572872 | tf_op jit(solution)/shard_map/ppermute | solution.py:791
  167.8 44.9 %collective-permute-start.10 = (bf16[512,1024]{1,0:T(8,128)(2,1)}, bf16[512,1024]{1,0:T(8,128)(2,1)}, u32[]{:S(2)}, u32[]{:S(2)}) collective-permute-start(bf16[512,1024]{1,0:T(8,128)(2,1)} %copy-done.42), channel_id=1, source_target_pairs={{0,8},{8,0},{1,9},{9,1},{2,10},{10,2},{3,11},{11,3},{16,24},{24,16... | collective-permute-start | bytes 3145736 | tf_op jit(solution)/shard_map/ppermute | solution.py:791
  186.3 26.4 %collective-permute-start.9 = (bf16[512,1024]{1,0:T(8,128)(2,1)}, bf16[512,1024]{1,0:T(8,128)(2,1)}, u32[]{:S(2)}, u32[]{:S(2)}) collective-permute-start(bf16[512,1024]{1,0:T(8,128)(2,1)} %get-tuple-element.111), channel_id=1, source_target_pairs={{0,8},{8,0},{1,9},{9,1},{2,10},{10,2},{3,11},{11,3},{16,24},{24,16... | collective-permute-start | bytes 3145736 | tf_op jit(solution)/shard_map/ppermute | solution.py:791
  191.8 24.3 %all-to-all-start.5 = ((bf16[4,1024,128]{2,1,0:T(8,128)(2,1)}), bf16[4,1024,128]{2,1,0:T(8,128)(2,1)S(1)}, u32[]{:S(2)}, u32[]{:S(2)}) async-start(bf16[4,1024,128]{2,1,0:T(8,128)(2,1)} %bitcast.27), calls=%async_computation.6 | async-start | bytes 2097152 | tf_op jit(solution)/shard_map/all_to_all | solution.py:795
  195.5 15.3 %collective-permute-start.8 = (bf16[512,512]{1,0:T(8,128)(2,1)}, bf16[512,512]{1,0:T(8,128)(2,1)S(1)}, u32[]{:S(2)}, u32[]{:S(2)}) collective-permute-start(bf16[512,512]{1,0:T(8,128)(2,1)} %add_convert_fusion.2), channel_id=1, source_target_pairs={{0,4},{8,12},{1,5},{9,13},{2,6},{10,14},{3,7},{11,15},{16,20},{24,... | collective-permute-start | bytes 1572872 | tf_op jit(solution)/shard_map/ppermute | solution.py:791
  199.0 4.1 %collective-permute-start.13 = (bf16[64,128]{1,0:T(8,128)(2,1)S(1)}, bf16[64,128]{1,0:T(8,128)(2,1)S(1)}, u32[]{:S(2)}, u32[]{:S(2)}) collective-permute-start(bf16[64,128]{1,0:T(8,128)(2,1)S(1)} %convert_element_type.99), channel_id=1, source_target_pairs={{0,1},{8,9},{1,2},{9,10},{2,3},{10,11},{3,0},{11,8},{16,17},{24,25... | collective-permute-start | bytes 49160 | tf_op jit(solution)/shard_map/ppermute | solution.py:791
  201.0 3.8 %collective-permute-start.12 = (bf16[64,128]{1,0:T(8,128)(2,1)S(1)}, bf16[64,128]{1,0:T(8,128)(2,1)S(1)}, u32[]{:S(2)}, u32[]{:S(2)}) collective-permute-start(bf16[64,128]{1,0:T(8,128)(2,1)S(1)} %convert_element_type.99), channel_id=1, source_target_pairs={{0,3},{8,11},{1,0},{9,8},{2,1},{10,9},{3,2},{11,10},{16,19},{24,27... | collective-permute-start | bytes 49160 | tf_op jit(solution)/shard_map/ppermute | solution.py:791
  203.1 4.4 %collective-permute-start.11 = (bf16[64,128]{1,0:T(8,128)(2,1)S(1)}, bf16[64,128]{1,0:T(8,128)(2,1)S(1)}, u32[]{:S(2)}, u32[]{:S(2)}) collective-permute-start(bf16[64,128]{1,0:T(8,128)(2,1)S(1)} %convert_element_type.99), channel_id=1, source_target_pairs={{0,2},{8,10},{1,3},{9,11},{2,0},{10,8},{3,1},{11,9},{16,18},{24,26... | collective-permute-start | bytes 49160 | tf_op jit(solution)/shard_map/ppermute | solution.py:791
  216.4 9.5 %collective-permute-start.14 = (bf16[1104,128]{1,0:T(8,128)(2,1)S(1)}, bf16[1104,128]{1,0:T(8,128)(2,1)}, u32[]{:S(2)}, u32[]{:S(2)}) collective-permute-start(bf16[1104,128]{1,0:T(8,128)(2,1)S(1)} %pad_maximum_fusion.3), channel_id=1, source_target_pairs={{0,4},{8,12},{1,5},{9,13},{2,6},{10,14},{3,7},{11,15},{16,20},{24,... | collective-permute-start | bytes 847880 | tf_op jit(solution)/shard_map/ppermute | solution.py:791
  219.2 29.1 %all-to-all-start.6 = ((bf16[4,256,1024]{2,1,0:T(8,128)(2,1)}), bf16[4,256,1024]{2,1,0:T(8,128)(2,1)S(1)}, u32[]{:S(2)}, u32[]{:S(2)}) async-start(bf16[4,256,1024]{2,1,0:T(8,128)(2,1)} %join_rows.1), calls=%async_computation.7 | async-start | bytes 4194304 | tf_op jit(solution)/shard_map/all_to_all | solution.py:795
  223.4 45.9 %all-gather.5.cloned.1.call-start = ((), (), s32[]{:S(2)}) async-start(), calls=%async_computation.10 | async-start | bytes 1310720 | tf_op jit(solution)/shard_map/all_gather | solution.py:799
  224.4 3.4 %collective-permute-start.16 = (bf16[256,512]{1,0:T(8,128)(2,1)S(1)}, bf16[256,512]{1,0:T(8,128)(2,1)S(1)}, u32[]{:S(2)}, u32[]{:S(2)}) collective-permute-start(bf16[256,512]{1,0:T(8,128)(2,1)S(1)} %slice.168), channel_id=1, source_target_pairs={{0,8},{8,0},{1,9},{9,1},{2,10},{10,2},{3,11},{11,3},{16,24},{24,16... | collective-permute-start | bytes 786440 | tf_op jit(solution)/shard_map/ppermute | solution.py:791
  226.9 7.1 %collective-permute-start.15 = (bf16[1104,128]{1,0:T(8,128)(2,1)S(1)}, bf16[1104,128]{1,0:T(8,128)(2,1)}, u32[]{:S(2)}, u32[]{:S(2)}) collective-permute-start(bf16[1104,128]{1,0:T(8,128)(2,1)S(1)} %add_convert_fusion.4), channel_id=1, source_target_pairs={{0,64},{8,72},{1,65},{9,73},{2,66},{10,74},{3,67},{11,75},{16,80},... | collective-permute-start | bytes 847880 | tf_op jit(solution)/shard_map/ppermute | solution.py:791
  235.8 18.8 %collective-permute-start.17 = (bf16[512,128]{1,0:T(8,128)(2,1)}, bf16[512,128]{1,0:T(8,128)(2,1)}, u32[]{:S(2)}, u32[]{:S(2)}) collective-permute-start(bf16[512,128]{1,0:T(8,128)(2,1)} %slice.170), channel_id=1, source_target_pairs={{0,8},{8,0},{1,9},{9,1},{2,10},{10,2},{3,11},{11,3},{16,24},{24,16... | collective-permute-start | bytes 393224 | tf_op jit(solution)/shard_map/ppermute | solution.py:791
  250.3 16.6 %collective-permute-start.21 = (bf16[256,1024]{1,0:T(8,128)(2,1)S(1)}, bf16[256,1024]{1,0:T(8,128)(2,1)S(1)}, u32[]{:S(2)}, u32[]{:S(2)}) collective-permute-start(bf16[256,1024]{1,0:T(8,128)(2,1)S(1)} %get-tuple-element.123), channel_id=1, source_target_pairs={{8,4},{9,5},{10,6},{11,7},{24,20},{25,21},{26,22},{27,23},{40,36},... | collective-permute-start | bytes 1572872 | tf_op jit(solution)/shard_map/ppermute | solution.py:791
  255.6 9.4 %collective-permute-start.18 = (bf16[592,128]{1,0:T(8,128)(2,1)S(1)}, bf16[592,128]{1,0:T(8,128)(2,1)S(1)}, u32[]{:S(2)}, u32[]{:S(2)}) collective-permute-start(bf16[592,128]{1,0:T(8,128)(2,1)S(1)} %pad_maximum_fusion.4.here_ref), channel_id=1, source_target_pairs={{0,48},{8,56},{1,49},{9,57},{2,50},{10,58},{3,51},{11,59},{16,0},{... | collective-permute-start | bytes 454664 | tf_op jit(solution)/shard_map/ppermute | solution.py:791
  257.9 9.0 %collective-permute-start.19 = (bf16[592,128]{1,0:T(8,128)(2,1)S(1)}, bf16[592,128]{1,0:T(8,128)(2,1)S(1)}, u32[]{:S(2)}, u32[]{:S(2)}) collective-permute-start(bf16[592,128]{1,0:T(8,128)(2,1)S(1)} %pad_maximum_fusion.4.here_ref), channel_id=1, source_target_pairs={{0,16},{8,24},{1,17},{9,25},{2,18},{10,26},{3,19},{11,27},{16,32},... | collective-permute-start | bytes 454664 | tf_op jit(solution)/shard_map/ppermute | solution.py:791
  257.9 9.0 %collective-permute-start.20 = (bf16[592,128]{1,0:T(8,128)(2,1)S(1)}, bf16[592,128]{1,0:T(8,128)(2,1)S(1)}, u32[]{:S(2)}, u32[]{:S(2)}) collective-permute-start(bf16[592,128]{1,0:T(8,128)(2,1)S(1)} %pad_maximum_fusion.4.here_ref), channel_id=1, source_target_pairs={{0,32},{8,40},{1,33},{9,41},{2,34},{10,42},{3,35},{11,43},{16,48},... | collective-permute-start | bytes 454664 | tf_op jit(solution)/shard_map/ppermute | solution.py:791
  266.9 2.8 collective-permute-start.22
  269.3 5.1 %collective-permute-start.23 = (bf16[4,256,512]{2,1,0:T(8,128)(2,1)}, bf16[4,256,512]{2,1,0:T(8,128)(2,1)S(1)}, u32[]{:S(2)}, u32[]{:S(2)}) collective-permute-start(bf16[4,256,512]{2,1,0:T(8,128)(2,1)} %bitcast.73), channel_id=1, source_target_pairs={{0,8},{8,0},{1,9},{9,1},{2,10},{10,2},{3,11},{11,3},{16,24},{24,16... | collective-permute-start | bytes 3145736 | tf_op jit(solution)/shard_map/ppermute | solution.py:791
  (53 other events, 577.1 us)
Sparse Core Ops, SparseCore 0:
  42.2 36.9 all-gather.2
  137.0 29.6 reduce-scatter.1
  235.2 26.1 all-gather.4

commit v3 on v2

--- a/solution.py
+++ b/solution.py
@@ -975,7 +975,7 @@
 
     quarter = payload.shape[0] // 4
     got_q = exchange(payload, ring_y)
-    got_q, fc_quarter, rows_joined = lax.optimization_barrier((got_q, fc_quarter, rows_joined))
+    got_q, rows_joined = lax.optimization_barrier((got_q, rows_joined))
     got = exchange(rows_joined, ring_z)
     rows_q = jnp.sum(wide(got_q).reshape(4, quarter, width), 0)
     wide_bias = jnp.concatenate(
@@ -984,6 +984,7 @@
     wide_bias = jnp.concatenate([wide_bias, jnp.zeros_like(wide_bias)]).reshape(-1, width)
     flow = jnp.concatenate([low(rows_q), low(small), low(wide_bias)], 0)
     flow = low(wide(flow) + wide(move(flow, x_far)))
+    flow, fc_quarter = lax.optimization_barrier((flow, fc_quarter))
     fc_half = fc_quarter.shape[0] // 2
     fc_part = jnp.where(home_here, fc_quarter[:fc_half], move(fc_quarter[fc_half:], cores))
     flow = low(wide(flow) + wide(move(flow, x_near)))

time: 286 us -> 285 us (level)
  starting transfers between devices: 61.2 us -> 65 us
  waiting for transfers between devices: 61 us -> 57.5 us
    ppermute x24, starting transfers between devices: 44.6 us -> 49 us  [move(): return lax.ppermute(values, AXES, pairs)]
    ppermute x24, waiting for transfers between devices: 23.7 us -> 20.4 us  [move(): return lax.ppermute(values, AXES, pairs)]
    unnamed x113 -> x115, local copies, waits for them, and re-layouts: 13.4 us -> 13.4 us
where the time goes in v3:
time: 285 us; the launch traced here: 283 us
  starting transfers between devices  65 us (23%)
  waiting for transfers between devices  57.5 us (20%)
  Pallas kernels  55.6 us (20%)
  blocking collectives  50.1 us (18%)
  local copies, waits for them, and re-layouts  20.3 us (7%)
  other arithmetic  15.6 us (5%)
  between operations  14.5 us (5%)
  matrix products  4.77 us (2%)
    all_to_all x3, blocking collectives, exchange(): lax.all_to_all(values, AXES, 0, 0, axis_index_groups=groups, tiled=True)  50.1 us
    ppermute x24, starting transfers between devices, move(): return lax.ppermute(values, AXES, pairs)  49 us
    all_to_all x4, waiting for transfers between devices, exchange(): lax.all_to_all(values, AXES, 0, 0, axis_index_groups=groups, tiled=True)  27.1 us
    ppermute x24, waiting for transfers between devices, move(): return lax.ppermute(values, AXES, pairs)  20.4 us
    all_to_all x4, starting transfers between devices, exchange(): lax.all_to_all(values, AXES, 0, 0, axis_index_groups=groups, tiled=True)  15.9 us
    unnamed x115, local copies, waits for them, and re-layouts  13.4 us
    pallas_call x1, Pallas kernels, hidden_block(): pl.pallas_call(hidden_kernel, grid_spec=pltpu.PrefetchScalarGridSpec(num_...  11 us
    pallas_call x1, Pallas kernels, attend_back(): pl.pallas_call(attend_back_kernel, grid=(rows // BLOCK,), in_specs=[rows_...  8.37 us
  transfers between devices with their start and end apart: 31, of which 14 were waited for; matrix products, arithmetic and copies ran while one was open for 9% of the time, Pallas kernels for 14%

profile of v3, /device:TPU:1, one launch (start us, length us, event | category | flops | bytes accessed | tf_op | source)
XLA Modules:
  0.0 283.5 jit_solution(10666570945167292135)
XLA Ops:
  7.2 6.0 %collective-permute-start = (bf16[128,1024]{1,0:T(8,128)(2,1)}, bf16[128,1024]{1,0:T(8,128)(2,1)S(1)}, u32[]{:S(2)}, u32[]{:S(2)}) collective-permute-start(bf16[128,1024]{1,0:T(8,128)(2,1)} %param.12), channel_id=1, source_target_pairs={{8,4},{9,5},{10,6},{11,7},{24,20},{25,21},{26,22},{27,23},{40,36},... | collective-permute-start | bytes 786440 | tf_op jit(solution)/shard_map/ppermute | solution.py:791
  18.3 4.4 %collective-permute-start.1 = (bf16[5152,128]{1,0:T(8,128)(2,1)}, bf16[5152,128]{1,0:T(8,128)(2,1)}, u32[]{:S(2)}, u32[]{:S(2)}) collective-permute-start(bf16[5152,128]{1,0:T(8,128)(2,1)} %pack.1.mine_ref), channel_id=1, source_target_pairs={{8,4},{9,5},{10,6},{11,7},{24,20},{25,21},{26,22},{27,23},{40,36},... | collective-permute-start | bytes 3956744 | tf_op jit(solution)/shard_map/ppermute | solution.py:791
  23.8 5.2 %all-to-all-start = ((bf16[4,128,1024]{2,1,0:T(8,128)(2,1)}), bf16[4,128,1024]{2,1,0:T(8,128)(2,1)S(1)}, u32[]{:S(2)}, u32[]{:S(2)}) async-start(bf16[4,128,1024]{2,1,0:T(8,128)(2,1)} %bitcast.6), calls=%async_computation | async-start | bytes 2097152 | tf_op jit(solution)/shard_map/all_to_all | solution.py:795
  30.5 8.2 %all-to-all-done = bf16[4,128,1024]{2,1,0:T(8,128)(2,1)S(1)} async-done(((bf16[4,128,1024]{2,1,0:T(8,128)(2,1)}), bf16[4,128,1024]{2,1,0:T(8,128)(2,1)S(1)}, u32[]{:S(2)}, u32[]{:S(2)}) %all-to-all-start) | async-done | bytes 1048608 | tf_op jit(solution)/shard_map/all_to_all | solution.py:795
  39.2 2.8 %unpack.1 = (bf16[3,1024,128]{2,1,0:T(8,128)(2,1)S(1)}, bf16[2,128,1024]{2,1,0:T(8,128)(2,1)}, bf16[32,128]{1,0:T(8,128)(2,1)S(1)}) custom-call(s32[1]{0:T(128)} %bitcast.home_ref, bf16[5152,128]{1,0:T(8,128)(2,1)} %pack.1.mine_ref, bf16[5152,128]{1,0:T(8,128)(2,1)} %collective-permute-done.1.got_ref), custom_call_target="tpu_custom_call" | custom-call | tf_op jit(solution)/shard_map/unpack/pallas_call | solution.py:263
  42.3 2.5 collective-permute-done.2.hi_ref.x_hi_ref
  44.9 3.5 %norm_project.1 = (bf16[1024,1024]{1,0:T(8,128)(2,1)S(1)}, bf16[1024,128]{1,0:T(8,128)(2,1)S(1)}, bf16[1024,128]{1,0:T(8,128)(2,1)S(1)}, bf16[1024,128]{1,0:T(8,128)(2,1)S(1)}) custom-call(bf16[512,1024]{1,0:T(8,128)(2,1)S(1)} %bitcast.69, bf16[512,1024]{1,0:T(8,128)(2,1)S(1)} %collective-permute-done.2.hi_ref.x_hi_ref, ...), custom_call_target="tpu_custom_call" | custom-call | tf_op jit(solution)/shard_map/norm_project/pallas_call | solution.py:86
  49.7 5.4 %attend.1 = (bf16[1024,128]{1,0:T(8,128)(2,1)S(1)}, bf16[1024,128]{1,0:T(8,128)(2,1)S(1)}, f32[2,1024]{1,0:T(2,128)S(1)}) custom-call(s32[1]{0:T(128)} %bitcast.12.core_ref, bf16[1024,128]{1,0:T(8,128)(2,1)S(1)} %get-tuple-element.81.q_ref, bf16[1024,128]{1,0:T(8,128)(2,1)S(1)} %get-tuple-element.82.k_ref, bf16[1024,128]{1,0:T(8,128)(2,1)S(1)} %get-tuple-element.83.v_ref), custom_call_target="tpu_custom_call" | custom-call | tf_op jit(solution)/shard_map/attend/pallas_call | solution.py:127
  55.1 13.9 %all_to_all.53.pieces_ref = bf16[8,128,128]{2,1,0:T(8,128)(2,1)S(1)} all-to-all(bf16[8,128,128]{2,1,0:T(8,128)(2,1)S(1)} %bitcast.77), channel_id=1, replica_groups={{0,1,2,3,8,9,10,11},{64,65,66,67,72,73,74,75},{4,5,6,7,12,13,14,15},{68..., dimensions={0} | all-to-all | bytes 524288 | tf_op jit(solution)/shard_map/all_to_all | solution.py:795
  69.0 3.9 %collective-permute-start.4 = (bf16[2048,512]{1,0:T(8,128)(2,1)}, bf16[2048,512]{1,0:T(8,128)(2,1)}, u32[]{:S(2)}, u32[]{:S(2)}) collective-permute-start(bf16[2048,512]{1,0:T(8,128)(2,1)} %pad_maximum_fusion.mine_ref), channel_id=1, source_target_pairs={{8,4},{9,5},{10,6},{11,7},{24,20},{25,21},{26,22},{27,23},{40,36},... | collective-permute-start | bytes 6291464 | tf_op jit(solution)/shard_map/ppermute | solution.py:791
  73.0 6.2 %all-gather.3.cloned.1.call-done = bf16[2048,1024]{1,0:T(8,128)(2,1)} async-done(((bf16[256,1024]{1,0:T(8,128)(2,1)}), bf16[2048,1024]{1,0:T(8,128)(2,1)}) %all-gather.3.cloned.1.call-update) | async-done | bytes 4194320 | tf_op jit(solution)/shard_map/all_gather | solution.py:799
  81.6 17.1 %all_to_all.54 = bf16[4,128,1024]{2,1,0:T(8,128)(2,1)S(1)} all-to-all(bf16[4,128,1024]{2,1,0:T(8,128)(2,1)S(1)} %get-tuple-element.86), channel_id=1, replica_groups={{0,1,2,3},{64,65,66,67},{4,5,6,7},{68,69,70,71},{16,17,18,19},{80,81,82..., dimensions={0} | all-to-all | bytes 2097152 | tf_op jit(solution)/shard_map/all_to_all | solution.py:795
  102.4 11.0 %hidden_block.1 = (bf16[1024,1024]{1,0:T(8,128)(2,1)S(1)}, bf16[1024,1024]{1,0:T(8,128)(2,1)S(1)}, bf16[1024,512]{1,0:T(8,128)(2,1)S(1)}, bf16[1024,512]{1,0:T(8...) custom-call(s32[2]{0:T(128)S(1)} %pad_add_fusion.core_ref, ...), custom_call_target="tpu_custom_call" | custom-call | tf_op jit(solution)/shard_map/hidden_block/pallas_call | solution.py:644
  118.5 3.5 %all-to-all-start.3 = ((bf16[4,128,1024]{2,1,0:T(8,128)(2,1)}), bf16[4,128,1024]{2,1,0:T(8,128)(2,1)S(1)}, u32[]{:S(2)}, u32[]{:S(2)}) async-start(bf16[4,128,1024]{2,1,0:T(8,128)(2,1)} %bitcast.83), calls=%async_computation.3 | async-start | bytes 2097152 | tf_op jit(solution)/shard_map/all_to_all | solution.py:795
  127.9 8.9 %all-to-all-done.3.got_ref = bf16[4,128,1024]{2,1,0:T(8,128)(2,1)S(1)} async-done(((bf16[4,128,1024]{2,1,0:T(8,128)(2,1)}), bf16[4,128,1024]{2,1,0:T(8,128)(2,1)S(1)}, u32[]{:S(2)}, u32[]{:S(2)}) %all-to-all-start.3) | async-done | bytes 1048608 | tf_op jit(solution)/shard_map/all_to_all | solution.py:795
  136.9 3.1 %middle_back.1 = (f32[128,1024]{1,0:T(8,128)S(1)}, bf16[4,128,1280]{2,1,0:T(8,128)(2,1)S(1)}, f32[16,1024]{1,0:T(8,128)S(1)}) custom-call(s32[1]{0:T(128)} %bitcast.12.core_ref, bf16[4,128,1024]{2,1,0:T(8,128)(2,1)S(1)} %all-to-all-done.3.got_ref, f32[128,1024]{1,0:T(8,128)S(1)} %get-tuple-element.96.x1_ref, f32[128,1024]{1,0:T(8,128)S(1)} %copy-done.27, ...), custom_call_target="tpu_custom_call" | custom-call | tf_op jit(solution)/shard_map/middle_back/pallas_call | solution.py:370
  140.5 19.2 %all_to_all.55 = bf16[4,128,1280]{2,1,0:T(8,128)(2,1)S(1)} all-to-all(bf16[4,128,1280]{2,1,0:T(8,128)(2,1)S(1)} %get-tuple-element.99), channel_id=1, replica_groups={{0,1,2,3},{64,65,66,67},{4,5,6,7},{68,69,70,71},{16,17,18,19},{80,81,82..., dimensions={0} | all-to-all | bytes 2621440 | tf_op jit(solution)/shard_map/all_to_all | solution.py:795
  162.9 3.7 %reduce-scatter.2.cloned.1.call-done = bf16[512,512]{1,0:T(8,128)(2,1)} async-done(((bf16[2048,512]{1,0:T(8,128)(2,1)}), bf16[512,512]{1,0:T(8,128)(2,1)}) %reduce-scatter.2.cloned.1.call-update) | async-done | bytes 524304 | tf_op jit(solution)/shard_map/reduce_scatter | solution.py:933
  172.3 8.4 %attend_back.1 = (bf16[1024,128]{1,0:T(8,128)(2,1)S(1)}, bf16[1024,128]{1,0:T(8,128)(2,1)S(1)}, bf16[1024,128]{1,0:T(8,128)(2,1)S(1)}, f32[8,128]{1,0:T(8,128)S(1)}) custom-call(bf16[1024,128]{1,0:T(8,128)(2,1)S(1)} %copy-done.12, bf16[512,1280]{1,0:T(8,128)(2,1)S(1)} %bitcast.66, bf16[512,1152]{1,0:T(8,128)(2,1)S(1)} %collective-permute-done.6.do_hi_ref.da_hi_ref, ...), custom_call_target="tpu_custom_call" | custom-call | tf_op jit(solution)/shard_map/attend_back/pallas_call | solution.py:201
  181.6 4.6 %project_back.1 = (bf16[512,1024]{1,0:T(8,128)(2,1)S(1)}, bf16[512,1024]{1,0:T(8,128)(2,1)}, f32[64,128]{1,0:T(8,128)S(1)}) custom-call(bf16[1024,128]{1,0:T(8,128)(2,1)S(1)} %get-tuple-element.108.dq_ref, bf16[1024,128]{1,0:T(8,128)(2,1)S(1)} %get-tuple-element.104.dk_ref, bf16[1024,128]{1,0:T(8,128)(2,1)S(1)} %get-tuple-element.105.dv_ref, ...), custom_call_target="tpu_custom_call" | custom-call | tf_op jit(solution)/shard_map/project_back/pallas_call | solution.py:719
  186.8 3.7 %weight_grads.1 = bf16[4096,128]{1,0:T(8,128)(2,1)} custom-call(bf16[1024,1024]{1,0:T(8,128)(2,1)S(1)} %copy-done.7, bf16[1024,128]{1,0:T(8,128)(2,1)S(1)} %get-tuple-element.108.dq_ref, bf16[1024,128]{1,0:T(8,128)(2,1)S(1)} %get-tuple-element.104.dk_ref, bf16[1024,128]{1,0:T(8,128)(2,1)S(1)} %get-tuple-element.105.dv_ref, bf16[1024,128]{1,0:T(8,128)(2,1)S(1)} %copy-done.31, ...), custom_call_target="tpu_custom_call" | custom-call | tf_op jit(solution)/shard_map/weight_grads/pallas_call | solution.py:417
  190.5 3.7 %all-to-all-start.5 = ((bf16[4,1024,128]{2,1,0:T(8,128)(2,1)}), bf16[4,1024,128]{2,1,0:T(8,128)(2,1)S(1)}, u32[]{:S(2)}, u32[]{:S(2)}) async-start(bf16[4,1024,128]{2,1,0:T(8,128)(2,1)} %bitcast.27), calls=%async_computation.6 | async-start | bytes 2097152 | tf_op jit(solution)/shard_map/all_to_all | solution.py:795
  200.0 2.7 collective-permute-start.14
  202.8 3.3 %join_rows.1 = bf16[4,256,1024]{2,1,0:T(8,128)(2,1)} custom-call(bf16[512,1024]{1,0:T(8,128)(2,1)S(1)} %copy-done.20, bf16[512,1024]{1,0:T(8,128)(2,1)S(1)} %copy-done.18, bf16[512,1024]{1,0:T(8,128)(2,1)} %collective-permute-done.8.got_ref, bf16[512,1024]{1,0:T(8,128)(2,1)} %collective-permute-done.9.f_got_ref), custom_call_target="tpu_custom_call" | custom-call | tf_op jit(solution)/shard_map/join_rows/pallas_call | solution.py:522
  206.2 3.3 %all-to-all-done.5 = bf16[4,1024,128]{2,1,0:T(8,128)(2,1)S(1)} async-done(((bf16[4,1024,128]{2,1,0:T(8,128)(2,1)}), bf16[4,1024,128]{2,1,0:T(8,128)(2,1)S(1)}, u32[]{:S(2)}, u32[]{:S(2)}) %all-to-all-start.5) | async-done | bytes 1048608 | tf_op jit(solution)/shard_map/all_to_all | solution.py:795
  209.7 2.7 collective-permute-start.13
  216.4 3.6 %all-to-all-start.6 = ((bf16[4,256,1024]{2,1,0:T(8,128)(2,1)}), bf16[4,256,1024]{2,1,0:T(8,128)(2,1)S(1)}, u32[]{:S(2)}, u32[]{:S(2)}) async-start(bf16[4,256,1024]{2,1,0:T(8,128)(2,1)} %join_rows.1), calls=%async_computation.7 | async-start | bytes 4194304 | tf_op jit(solution)/shard_map/all_to_all | solution.py:795
  222.5 2.9 %collective-permute-start.16 = (bf16[256,512]{1,0:T(8,128)(2,1)S(1)}, bf16[256,512]{1,0:T(8,128)(2,1)S(1)}, u32[]{:S(2)}, u32[]{:S(2)}) collective-permute-start(bf16[256,512]{1,0:T(8,128)(2,1)S(1)} %slice.168), channel_id=1, source_target_pairs={{0,8},{8,0},{1,9},{9,1},{2,10},{10,2},{3,11},{11,3},{16,24},{24,16... | collective-permute-start | bytes 786440 | tf_op jit(solution)/shard_map/ppermute | solution.py:791
  228.2 5.5 %collective-permute-done.15 = bf16[1104,128]{1,0:T(8,128)(2,1)} collective-permute-done((bf16[1104,128]{1,0:T(8,128)(2,1)S(1)}, bf16[1104,128]{1,0:T(8,128)(2,1)}, u32[]{:S(2)}, u32[]{:S(2)}) %collective-permute-start.15) | collective-permute-done | bytes 282656 | tf_op jit(solution)/shard_map/ppermute | solution.py:791
  236.4 6.7 %all-to-all-done.6.got_ref = bf16[4,256,1024]{2,1,0:T(8,128)(2,1)S(1)} async-done(((bf16[4,256,1024]{2,1,0:T(8,128)(2,1)}), bf16[4,256,1024]{2,1,0:T(8,128)(2,1)S(1)}, u32[]{:S(2)}, u32[]{:S(2)}) %all-to-all-start.6) | async-done | bytes 2097184 | tf_op jit(solution)/shard_map/all_to_all | solution.py:795
  245.1 8.6 %collective-permute-start.21 = (bf16[256,1024]{1,0:T(8,128)(2,1)S(1)}, bf16[256,1024]{1,0:T(8,128)(2,1)S(1)}, u32[]{:S(2)}, u32[]{:S(2)}) collective-permute-start(bf16[256,1024]{1,0:T(8,128)(2,1)S(1)} %get-tuple-element.125), channel_id=1, source_target_pairs={{8,4},{9,5},{10,6},{11,7},{24,20},{25,21},{26,22},{27,23},{40,36},... | collective-permute-start | bytes 1572872 | tf_op jit(solution)/shard_map/ppermute | solution.py:791
  258.8 5.9 %collective-permute-done.18.above_ref = bf16[592,128]{1,0:T(8,128)(2,1)S(1)} collective-permute-done((bf16[592,128]{1,0:T(8,128)(2,1)S(1)}, bf16[592,128]{1,0:T(8,128)(2,1)S(1)}, u32[]{:S(2)}, u32[]{:S(2)}) %collective-permute-start.18) | collective-permute-done | bytes 151584 | tf_op jit(solution)/shard_map/ppermute | solution.py:791
  (221 shorter events, 74.8 us)
Async XLA Ops:
  7.2 11.1 %collective-permute-start = (bf16[128,1024]{1,0:T(8,128)(2,1)}, bf16[128,1024]{1,0:T(8,128)(2,1)S(1)}, u32[]{:S(2)}, u32[]{:S(2)}) collective-permute-start(bf16[128,1024]{1,0:T(8,128)(2,1)} %param.12), channel_id=1, source_target_pairs={{8,4},{9,5},{10,6},{11,7},{24,20},{25,21},{26,22},{27,23},{40,36},... | collective-permute-start | bytes 786440 | tf_op jit(solution)/shard_map/ppermute | solution.py:791
  18.3 61.0 %copy-start.2 = (bf16[128,1024]{1,0:T(8,128)(2,1)}, bf16[128,1024]{1,0:T(8,128)(2,1)S(1)}, u32[]{:S(2)}) copy-start(bf16[128,1024]{1,0:T(8,128)(2,1)S(1)} %broadcast_select_fusion.x_ref) | copy-start | bytes 786436
  18.3 21.0 %collective-permute-start.1 = (bf16[5152,128]{1,0:T(8,128)(2,1)}, bf16[5152,128]{1,0:T(8,128)(2,1)}, u32[]{:S(2)}, u32[]{:S(2)}) collective-permute-start(bf16[5152,128]{1,0:T(8,128)(2,1)} %pack.1.mine_ref), channel_id=1, source_target_pairs={{8,4},{9,5},{10,6},{11,7},{24,20},{25,21},{26,22},{27,23},{40,36},... | collective-permute-start | bytes 3956744 | tf_op jit(solution)/shard_map/ppermute | solution.py:791
  23.8 14.9 %all-to-all-start = ((bf16[4,128,1024]{2,1,0:T(8,128)(2,1)}), bf16[4,128,1024]{2,1,0:T(8,128)(2,1)S(1)}, u32[]{:S(2)}, u32[]{:S(2)}) async-start(bf16[4,128,1024]{2,1,0:T(8,128)(2,1)} %bitcast.6), calls=%async_computation | async-start | bytes 2097152 | tf_op jit(solution)/shard_map/all_to_all | solution.py:795
  28.9 50.3 %all-gather.3.cloned.1.call-start = ((), (), s32[]{:S(2)}) async-start(), calls=%async_computation.8 | async-start | bytes 4718592 | tf_op jit(solution)/shard_map/all_gather | solution.py:799
  42.1 2.7 collective-permute-start.2
  69.0 31.2 %collective-permute-start.4 = (bf16[2048,512]{1,0:T(8,128)(2,1)}, bf16[2048,512]{1,0:T(8,128)(2,1)}, u32[]{:S(2)}, u32[]{:S(2)}) collective-permute-start(bf16[2048,512]{1,0:T(8,128)(2,1)} %pad_maximum_fusion.mine_ref), channel_id=1, source_target_pairs={{8,4},{9,5},{10,6},{11,7},{24,20},{25,21},{26,22},{27,23},{40,36},... | collective-permute-start | bytes 6291464 | tf_op jit(solution)/shard_map/ppermute | solution.py:791
  98.7 3.7 %collective-permute-start.3 = (bf16[512,1024]{1,0:T(8,128)(2,1)S(1)}, bf16[512,1024]{1,0:T(8,128)(2,1)S(1)}, u32[]{:S(2)}, u32[]{:S(2)}) collective-permute-start(bf16[512,1024]{1,0:T(8,128)(2,1)S(1)} %bitcast.71), channel_id=1, source_target_pairs={{0,8},{8,0},{1,9},{9,1},{2,10},{10,2},{3,11},{11,3},{16,24},{24,16... | collective-permute-start | bytes 3145736 | tf_op jit(solution)/shard_map/ppermute | solution.py:791
  114.3 2.7 collective-permute-start.5
  118.5 18.3 %all-to-all-start.3 = ((bf16[4,128,1024]{2,1,0:T(8,128)(2,1)}), bf16[4,128,1024]{2,1,0:T(8,128)(2,1)S(1)}, u32[]{:S(2)}, u32[]{:S(2)}) async-start(bf16[4,128,1024]{2,1,0:T(8,128)(2,1)} %bitcast.83), calls=%async_computation.3 | async-start | bytes 2097152 | tf_op jit(solution)/shard_map/all_to_all | solution.py:795
  122.0 44.6 %reduce-scatter.2.cloned.1.call-start = ((), (), s32[]{:S(2)}) async-start(), calls=%async_computation.9 | async-start | bytes 2621440 | tf_op jit(solution)/shard_map/reduce_scatter | solution.py:933
  160.8 7.9 %collective-permute-start.6 = (bf16[512,1152]{1,0:T(8,128)(2,1)}, bf16[512,1152]{1,0:T(8,128)(2,1)S(1)}, u32[]{:S(2)}, u32[]{:S(2)}) collective-permute-start(bf16[512,1152]{1,0:T(8,128)(2,1)} %slice.200), channel_id=1, source_target_pairs={{0,8},{8,0},{1,9},{9,1},{2,10},{10,2},{3,11},{11,3},{16,24},{24,16... | collective-permute-start | bytes 3538952 | tf_op jit(solution)/shard_map/ppermute | solution.py:791
  166.6 14.0 %collective-permute-start.7 = (bf16[512,512]{1,0:T(8,128)(2,1)}, bf16[512,512]{1,0:T(8,128)(2,1)S(1)}, u32[]{:S(2)}, u32[]{:S(2)}) collective-permute-start(bf16[512,512]{1,0:T(8,128)(2,1)} %reduce-scatter.2.cloned.1.call-done), channel_id=1, source_target_pairs={{0,64},{8,72},{1,65},{9,73},{2,66},{10,74},{3,67},{11,75},{16,80},... | collective-permute-start | bytes 1572872 | tf_op jit(solution)/shard_map/ppermute | solution.py:791
  167.8 35.0 %collective-permute-start.9 = (bf16[512,1024]{1,0:T(8,128)(2,1)}, bf16[512,1024]{1,0:T(8,128)(2,1)}, u32[]{:S(2)}, u32[]{:S(2)}) collective-permute-start(bf16[512,1024]{1,0:T(8,128)(2,1)} %copy-done.42), channel_id=1, source_target_pairs={{0,8},{8,0},{1,9},{9,1},{2,10},{10,2},{3,11},{11,3},{16,24},{24,16... | collective-permute-start | bytes 3145736 | tf_op jit(solution)/shard_map/ppermute | solution.py:791
  186.3 16.5 %collective-permute-start.8 = (bf16[512,1024]{1,0:T(8,128)(2,1)}, bf16[512,1024]{1,0:T(8,128)(2,1)}, u32[]{:S(2)}, u32[]{:S(2)}) collective-permute-start(bf16[512,1024]{1,0:T(8,128)(2,1)} %get-tuple-element.111), channel_id=1, source_target_pairs={{0,8},{8,0},{1,9},{9,1},{2,10},{10,2},{3,11},{11,3},{16,24},{24,16... | collective-permute-start | bytes 3145736 | tf_op jit(solution)/shard_map/ppermute | solution.py:791
  190.5 19.0 %all-to-all-start.5 = ((bf16[4,1024,128]{2,1,0:T(8,128)(2,1)}), bf16[4,1024,128]{2,1,0:T(8,128)(2,1)S(1)}, u32[]{:S(2)}, u32[]{:S(2)}) async-start(bf16[4,1024,128]{2,1,0:T(8,128)(2,1)} %bitcast.27), calls=%async_computation.6 | async-start | bytes 2097152 | tf_op jit(solution)/shard_map/all_to_all | solution.py:795
  195.7 4.3 %collective-permute-start.12 = (bf16[64,128]{1,0:T(8,128)(2,1)S(1)}, bf16[64,128]{1,0:T(8,128)(2,1)S(1)}, u32[]{:S(2)}, u32[]{:S(2)}) collective-permute-start(bf16[64,128]{1,0:T(8,128)(2,1)S(1)} %convert_element_type.96), channel_id=1, source_target_pairs={{0,1},{8,9},{1,2},{9,10},{2,3},{10,11},{3,0},{11,8},{16,17},{24,25... | collective-permute-start | bytes 49160 | tf_op jit(solution)/shard_map/ppermute | solution.py:791
  196.9 5.8 %collective-permute-start.11 = (bf16[64,128]{1,0:T(8,128)(2,1)S(1)}, bf16[64,128]{1,0:T(8,128)(2,1)S(1)}, u32[]{:S(2)}, u32[]{:S(2)}) collective-permute-start(bf16[64,128]{1,0:T(8,128)(2,1)S(1)} %convert_element_type.96), channel_id=1, source_target_pairs={{0,3},{8,11},{1,0},{9,8},{2,1},{10,9},{3,2},{11,10},{16,19},{24,27... | collective-permute-start | bytes 49160 | tf_op jit(solution)/shard_map/ppermute | solution.py:791
  198.4 4.3 %collective-permute-start.10 = (bf16[64,128]{1,0:T(8,128)(2,1)S(1)}, bf16[64,128]{1,0:T(8,128)(2,1)S(1)}, u32[]{:S(2)}, u32[]{:S(2)}) collective-permute-start(bf16[64,128]{1,0:T(8,128)(2,1)S(1)} %convert_element_type.96), channel_id=1, source_target_pairs={{0,2},{8,10},{1,3},{9,11},{2,0},{10,8},{3,1},{11,9},{16,18},{24,26... | collective-permute-start | bytes 49160 | tf_op jit(solution)/shard_map/ppermute | solution.py:791
  200.0 14.4 %collective-permute-start.14 = (bf16[512,512]{1,0:T(8,128)(2,1)}, bf16[512,512]{1,0:T(8,128)(2,1)}, u32[]{:S(2)}, u32[]{:S(2)}) collective-permute-start(bf16[512,512]{1,0:T(8,128)(2,1)} %add_convert_fusion.2), channel_id=1, source_target_pairs={{0,4},{8,12},{1,5},{9,13},{2,6},{10,14},{3,7},{11,15},{16,20},{24,... | collective-permute-start | bytes 1572872 | tf_op jit(solution)/shard_map/ppermute | solution.py:791
  209.7 10.7 %collective-permute-start.13 = (bf16[1104,128]{1,0:T(8,128)(2,1)S(1)}, bf16[1104,128]{1,0:T(8,128)(2,1)}, u32[]{:S(2)}, u32[]{:S(2)}) collective-permute-start(bf16[1104,128]{1,0:T(8,128)(2,1)S(1)} %pad_maximum_fusion.3), channel_id=1, source_target_pairs={{0,4},{8,12},{1,5},{9,13},{2,6},{10,14},{3,7},{11,15},{16,20},{24,... | collective-permute-start | bytes 847880 | tf_op jit(solution)/shard_map/ppermute | solution.py:791
  216.4 26.8 %all-to-all-start.6 = ((bf16[4,256,1024]{2,1,0:T(8,128)(2,1)}), bf16[4,256,1024]{2,1,0:T(8,128)(2,1)S(1)}, u32[]{:S(2)}, u32[]{:S(2)}) async-start(bf16[4,256,1024]{2,1,0:T(8,128)(2,1)} %join_rows.1), calls=%async_computation.7 | async-start | bytes 4194304 | tf_op jit(solution)/shard_map/all_to_all | solution.py:795
  220.0 48.4 %all-gather.5.cloned.1.call-start = ((), (), s32[]{:S(2)}) async-start(), calls=%async_computation.10 | async-start | bytes 1310720 | tf_op jit(solution)/shard_map/all_gather | solution.py:799
  222.5 4.1 %collective-permute-start.16 = (bf16[256,512]{1,0:T(8,128)(2,1)S(1)}, bf16[256,512]{1,0:T(8,128)(2,1)S(1)}, u32[]{:S(2)}, u32[]{:S(2)}) collective-permute-start(bf16[256,512]{1,0:T(8,128)(2,1)S(1)} %slice.168), channel_id=1, source_target_pairs={{0,8},{8,0},{1,9},{9,1},{2,10},{10,2},{3,11},{11,3},{16,24},{24,16... | collective-permute-start | bytes 786440 | tf_op jit(solution)/shard_map/ppermute | solution.py:791
  225.4 8.4 %collective-permute-start.15 = (bf16[1104,128]{1,0:T(8,128)(2,1)S(1)}, bf16[1104,128]{1,0:T(8,128)(2,1)}, u32[]{:S(2)}, u32[]{:S(2)}) collective-permute-start(bf16[1104,128]{1,0:T(8,128)(2,1)S(1)} %add_convert_fusion.4), channel_id=1, source_target_pairs={{0,64},{8,72},{1,65},{9,73},{2,66},{10,74},{3,67},{11,75},{16,80},... | collective-permute-start | bytes 847880 | tf_op jit(solution)/shard_map/ppermute | solution.py:791
  235.5 18.1 %collective-permute-start.17 = (bf16[512,128]{1,0:T(8,128)(2,1)}, bf16[512,128]{1,0:T(8,128)(2,1)}, u32[]{:S(2)}, u32[]{:S(2)}) collective-permute-start(bf16[512,128]{1,0:T(8,128)(2,1)} %slice.170), channel_id=1, source_target_pairs={{0,8},{8,0},{1,9},{9,1},{2,10},{10,2},{3,11},{11,3},{16,24},{24,16... | collective-permute-start | bytes 393224 | tf_op jit(solution)/shard_map/ppermute | solution.py:791
  245.1 20.9 %collective-permute-start.21 = (bf16[256,1024]{1,0:T(8,128)(2,1)S(1)}, bf16[256,1024]{1,0:T(8,128)(2,1)S(1)}, u32[]{:S(2)}, u32[]{:S(2)}) collective-permute-start(bf16[256,1024]{1,0:T(8,128)(2,1)S(1)} %get-tuple-element.125), channel_id=1, source_target_pairs={{8,4},{9,5},{10,6},{11,7},{24,20},{25,21},{26,22},{27,23},{40,36},... | collective-permute-start | bytes 1572872 | tf_op jit(solution)/shard_map/ppermute | solution.py:791
  254.6 10.1 %collective-permute-start.18 = (bf16[592,128]{1,0:T(8,128)(2,1)S(1)}, bf16[592,128]{1,0:T(8,128)(2,1)S(1)}, u32[]{:S(2)}, u32[]{:S(2)}) collective-permute-start(bf16[592,128]{1,0:T(8,128)(2,1)S(1)} %pad_maximum_fusion.4.here_ref), channel_id=1, source_target_pairs={{0,48},{8,56},{1,49},{9,57},{2,50},{10,58},{3,51},{11,59},{16,0},{... | collective-permute-start | bytes 454664 | tf_op jit(solution)/shard_map/ppermute | solution.py:791
  257.1 8.9 %collective-permute-start.19 = (bf16[592,128]{1,0:T(8,128)(2,1)S(1)}, bf16[592,128]{1,0:T(8,128)(2,1)S(1)}, u32[]{:S(2)}, u32[]{:S(2)}) collective-permute-start(bf16[592,128]{1,0:T(8,128)(2,1)S(1)} %pad_maximum_fusion.4.here_ref), channel_id=1, source_target_pairs={{0,16},{8,24},{1,17},{9,25},{2,18},{10,26},{3,19},{11,27},{16,32},... | collective-permute-start | bytes 454664 | tf_op jit(solution)/shard_map/ppermute | solution.py:791
  257.1 8.9 %collective-permute-start.20 = (bf16[592,128]{1,0:T(8,128)(2,1)S(1)}, bf16[592,128]{1,0:T(8,128)(2,1)S(1)}, u32[]{:S(2)}, u32[]{:S(2)}) collective-permute-start(bf16[592,128]{1,0:T(8,128)(2,1)S(1)} %pad_maximum_fusion.4.here_ref), channel_id=1, source_target_pairs={{0,32},{8,40},{1,33},{9,41},{2,34},{10,42},{3,35},{11,43},{16,48},... | collective-permute-start | bytes 454664 | tf_op jit(solution)/shard_map/ppermute | solution.py:791
  266.1 2.8 collective-permute-start.22
  268.4 5.1 %collective-permute-start.23 = (bf16[4,256,512]{2,1,0:T(8,128)(2,1)}, bf16[4,256,512]{2,1,0:T(8,128)(2,1)S(1)}, u32[]{:S(2)}, u32[]{:S(2)}) collective-permute-start(bf16[4,256,512]{2,1,0:T(8,128)(2,1)} %bitcast.73), channel_id=1, source_target_pairs={{0,8},{8,0},{1,9},{9,1},{2,10},{10,2},{3,11},{11,3},{16,24},{24,16... | collective-permute-start | bytes 3145736 | tf_op jit(solution)/shard_map/ppermute | solution.py:791
  (54 other events, 563.8 us)
Sparse Core Ops, SparseCore 0:
  42.2 36.9 all-gather.2
  137.0 29.6 reduce-scatter.1
  235.0 27.3 all-gather.4
